TPU v7x, 32 devices: a whole 2x2x4 slice. The times are simulated.
32 devices in a mesh: tm: 4 (over x, core), rep: 8 (over z, y).
Axes of the slice: x: 2, y: 2, z: 4, core: 2. Of those that a mesh axis runs over, the one named last changes fastest.
Arguments:
- snapshots: float32 [32, 256, 1024], P('tm', 'rep'), may hold values from -6 to 6
- freq_bins: int32 [32], replicated, may hold values from 1 to 511
- replicas: float32 [2, 32, 8192, 256], P(None, 'tm', 'rep'), may hold values from -6 to 6
Outputs:
- power: float32 [8192], P(('rep', 'tm'))
All inputs are finite; a program needn't handle non-finite values.
Results may differ from a plain program's by a relative error of at most 0.00005.
Values sent between devices are 32-bit elements; how exact they have to be, the bound alone decides.
No kernel may reach another device: no remote copies, remote signals or barrier semaphores. Data moves between devices by JAX's collectives and lax.ppermute only.
A program may use at most 64 MiB of HBM per device.

v0:
```python
import math

import jax
import jax.numpy as jnp
from jax import lax
from jax.sharding import PartitionSpec as P

epsilon = 1e-06


def dft_table(freq_bins, length):
    offsets = jnp.arange(length, dtype=jnp.int32)
    phases = offsets[:, None] * freq_bins[None, :] % length
    angles = phases.astype(jnp.float32) * (2.0 * math.pi / length)
    window = 0.5 - 0.5 * jnp.cos(offsets.astype(jnp.float32) * (2.0 * math.pi / length))
    return jnp.concatenate(
        [window[:, None] * jnp.cos(angles), -window[:, None] * jnp.sin(angles)], axis=1
    )


def matmul(left, right):
    return jnp.dot(left, right, precision=lax.Precision.HIGHEST, preferred_element_type=jnp.float32)


def shards(snapshots, freq_bins, replicas):
    snap_rows, elem_rows, samples = snapshots.shape
    bin_count = freq_bins.shape[0]
    dft_rows = dft_table(freq_bins, samples)
    spectra = matmul(snapshots.reshape(snap_rows * elem_rows, samples), dft_rows).reshape(
        snap_rows, elem_rows, 2, bin_count
    )
    gathered = lax.all_gather(spectra, "rep", axis=1, tiled=True)
    by_owner = lax.all_to_all(gathered, "tm", split_axis=3, concat_axis=0, tiled=True)
    total_snaps = by_owner.shape[0]
    elem_count = by_owner.shape[1]
    local_bins = by_owner.shape[3]
    running = jnp.zeros((replicas.shape[2],), jnp.float32)
    for column in range(local_bins):
        spec_re = by_owner[:, :, 0, column]
        spec_im = by_owner[:, :, 1, column]
        rep_re = replicas[0, column]
        rep_im = replicas[1, column]
        power_trace = jnp.sum(spec_re * spec_re + spec_im * spec_im) / total_snaps + epsilon
        norm_sq = jnp.sum(rep_re * rep_re + rep_im * rep_im, axis=1) + epsilon
        proj_re = matmul(rep_re, spec_re.T) + matmul(rep_im, spec_im.T)
        proj_im = matmul(rep_re, spec_im.T) - matmul(rep_im, spec_re.T)
        quadratic = jnp.sum(proj_re * proj_re + proj_im * proj_im, axis=1) / total_snaps
        running = running + quadratic / (norm_sq * power_trace / elem_count)
    partial_value = running / bin_count
    return lax.psum_scatter(partial_value, "tm", scatter_dimension=0, tiled=True)


def solution(mesh):
    in_specs = (P("tm", "rep", None), P(), P(None, "tm", "rep", None))
    out_specs = P(("rep", "tm"))
    return jax.shard_map(shards, mesh=mesh, in_specs=in_specs, out_specs=out_specs, check_vma=False)
```

profile of v0, /device:TPU:0, one launch (start us, length us, event | category | flops | bytes accessed | tf_op | source)
XLA Modules:
  0.0 154.9 jit_solution(10852273086647012249)
XLA Ops:
  2.8 46.3 %all_gather.3 = f32[8,256,2,32]{3,0,2,1:T(8,128)S(1)} all-gather(f32[8,32,2,32]{3,0,2,1:T(8,128)S(1)} %copy.18), channel_id=1, replica_groups=mesh['tm'=4,'rep'=8] {'rep'}, dimensions={1}, use_global_device_ids=true | all-gather | bytes 589824 | tf_op jit(solution)/shard_map/all_gather | solution.py:32
  50.9 3.5 %all-to-all-start = ((f32[8,256,2,32]{1,2,0,3:T(2,128)}), f32[8,256,2,32]{1,2,0,3:T(2,128)S(1)}, u32[]{:S(2)}, u32[]{:S(2)}) async-start(f32[8,256,2,32]{1,2,0,3:T(2,128)} %copy.19), calls=%async_computation | async-start | bytes 1048576 | tf_op jit(solution)/shard_map/all_to_all | solution.py:33
  56.3 6.6 %fusion.91 = (f32[1024]{0:T(1024)S(1)}, f32[1024]{0:T(1024)S(1)}, f32[1024]{0:T(1024)S(1)}, f32[1024]{0:T(1024)S(1)}, f32[1024]{0:T(1024)S(1)}, /*index=5*/f32[1024]{0:T(1024)S(1)}, f32[1024]{0:T(1024)S(1)}, f32[1024]{0:T(1024)S(1)}) fusion(f32[2,8,1024,256]{3,2,1,0:T(8,128)} %param.5), kind=kLoop, calls=%fused_computation.123 | loop fusion | flops 8380416 | bytes 16809984 | tf_op jit(solution)/shard_map/reduce_sum | solution.py:44
  64.0 2.3 %fusion.92 = f32[32,1024]{1,0:T(8,128)S(1)} fusion(f32[2,8,1024,256]{3,2,1,0:T(8,128)} %param.5, f32[32,256,1,1]{1,3,2,0:T(1,128)S(1)} %get-tuple-element.28), kind=kOutput, calls=%fused_computation.125 | convolution fusion | flops 100663296 | bytes 1212416 | tf_op jit(solution)/shard_map/dot_general | solution.py:22
  66.3 2.3 %fusion.94 = f32[32,1024]{1,0:T(8,128)S(1)} fusion(f32[2,8,1024,256]{3,2,1,0:T(8,128)} %param.5, f32[32,256,1,1]{1,3,2,0:T(1,128)S(1)} %get-tuple-element.13), kind=kOutput, calls=%fused_computation.127 | convolution fusion | flops 100663296 | bytes 1212416 | tf_op jit(solution)/shard_map/dot_general | solution.py:22
  69.1 2.3 %fusion.84 = f32[32,1024]{1,0:T(8,128)S(1)} fusion(f32[2,8,1024,256]{3,2,1,0:T(8,128)} %param.5, f32[32,256,1,1]{1,3,2,0:T(1,128)S(1)} %get-tuple-element.26), kind=kOutput, calls=%fused_computation.115 | convolution fusion | flops 100663296 | bytes 1212416 | tf_op jit(solution)/shard_map/dot_general | solution.py:22
  71.4 2.3 %fusion.86 = f32[32,1024]{1,0:T(8,128)S(1)} fusion(f32[2,8,1024,256]{3,2,1,0:T(8,128)} %param.5, f32[32,256,1,1]{1,3,2,0:T(1,128)S(1)} %get-tuple-element.27), kind=kOutput, calls=%fused_computation.117 | convolution fusion | flops 100663296 | bytes 1212416 | tf_op jit(solution)/shard_map/dot_general | solution.py:22
  76.6 2.3 %fusion.78 = f32[32,1024]{1,0:T(8,128)S(1)} fusion(f32[2,8,1024,256]{3,2,1,0:T(8,128)} %param.5, f32[32,256,1,1]{1,3,2,0:T(1,128)S(1)} %get-tuple-element.25), kind=kOutput, calls=%fused_computation.107 | convolution fusion | flops 100663296 | bytes 1212416 | tf_op jit(solution)/shard_map/dot_general | solution.py:22
  81.8 2.3 %fusion.70 = f32[32,1024]{1,0:T(8,128)S(1)} fusion(f32[2,8,1024,256]{3,2,1,0:T(8,128)} %param.5, f32[32,256,1,1]{1,3,2,0:T(1,128)S(1)} %get-tuple-element.23), kind=kOutput, calls=%fused_computation.97 | convolution fusion | flops 100663296 | bytes 1212416 | tf_op jit(solution)/shard_map/dot_general | solution.py:22
  87.0 2.3 %fusion.62 = f32[32,1024]{1,0:T(8,128)S(1)} fusion(f32[2,8,1024,256]{3,2,1,0:T(8,128)} %param.5, f32[32,256,1,1]{1,3,2,0:T(1,128)S(1)} %get-tuple-element.21), kind=kOutput, calls=%fused_computation.87 | convolution fusion | flops 100663296 | bytes 1212416 | tf_op jit(solution)/shard_map/dot_general | solution.py:22
  89.9 2.3 %fusion.52 = f32[32,1024]{1,0:T(8,128)S(1)} fusion(f32[2,8,1024,256]{3,2,1,0:T(8,128)} %param.5, f32[32,256,1,1]{1,3,2,0:T(1,128)S(1)} %get-tuple-element.18), kind=kOutput, calls=%fused_computation.75 | convolution fusion | flops 100663296 | bytes 1212416 | tf_op jit(solution)/shard_map/dot_general | solution.py:22
  92.2 2.3 %fusion.54 = f32[32,1024]{1,0:T(8,128)S(1)} fusion(f32[2,8,1024,256]{3,2,1,0:T(8,128)} %param.5, f32[32,256,1,1]{1,3,2,0:T(1,128)S(1)} %get-tuple-element.19), kind=kOutput, calls=%fused_computation.77 | convolution fusion | flops 100663296 | bytes 1212416 | tf_op jit(solution)/shard_map/dot_general | solution.py:22
  97.3 2.3 %fusion.46 = f32[32,1024]{1,0:T(8,128)S(1)} fusion(f32[2,8,1024,256]{3,2,1,0:T(8,128)} %param.5, f32[32,256,1,1]{1,3,2,0:T(1,128)S(1)} %get-tuple-element.17), kind=kOutput, calls=%fused_computation.67 | convolution fusion | flops 100663296 | bytes 1212416 | tf_op jit(solution)/shard_map/dot_general | solution.py:22
  100.3 2.5 %fusion.36 = f32[32,1024]{1,0:T(8,128)S(1)} fusion(f32[2,8,1024,256]{3,2,1,0:T(8,128)} %param.5, f32[32,256,1,1]{1,3,2,0:T(1,128)S(1)} %get-tuple-element.14), kind=kOutput, calls=%fused_computation.55 | convolution fusion | flops 100663296 | bytes 1212416 | tf_op jit(solution)/shard_map/dot_general | solution.py:22
  102.8 2.3 %fusion.38 = f32[32,1024]{1,0:T(8,128)S(1)} fusion(f32[2,8,1024,256]{3,2,1,0:T(8,128)} %param.5, f32[32,256,1,1]{1,3,2,0:T(1,128)S(1)} %get-tuple-element.15), kind=kOutput, calls=%fused_computation.57 | convolution fusion | flops 100663296 | bytes 1212416 | tf_op jit(solution)/shard_map/dot_general | solution.py:22
  105.7 2.3 %fusion.14 = f32[32,1024]{1,0:T(8,128)S(1)} fusion(f32[32,1024]{1,0:T(8,128)S(1)} %fusion.92, f32[2,8,1024,256]{3,2,1,0:T(8,128)} %param.5, f32[32,256,1,1]{1,3,2,0:T(1,128)S(1)} %get-tuple-element.13), kind=kOutput, calls=%fused_computation.29 | convolution fusion | flops 100728832 | bytes 1343488 | tf_op jit(solution)/shard_map/dot_general | solution.py:22
  107.9 2.3 %fusion.12 = f32[32,1024]{1,0:T(8,128)S(1)} fusion(f32[32,1024]{1,0:T(8,128)S(1)} %fusion.84, f32[2,8,1024,256]{3,2,1,0:T(8,128)} %param.5, f32[32,256,1,1]{1,3,2,0:T(1,128)S(1)} %get-tuple-element.27), kind=kOutput, calls=%fused_computation.25 | convolution fusion | flops 100728832 | bytes 1343488 | tf_op jit(solution)/shard_map/dot_general | solution.py:22
  110.2 2.3 %fusion.10 = f32[32,1024]{1,0:T(8,128)S(1)} fusion(f32[32,1024]{1,0:T(8,128)S(1)} %fusion.76, f32[2,8,1024,256]{3,2,1,0:T(8,128)} %param.5, f32[32,256,1,1]{1,3,2,0:T(1,128)S(1)} %get-tuple-element.25), kind=kOutput, calls=%fused_computation.21 | convolution fusion | flops 100728832 | bytes 1343488 | tf_op jit(solution)/shard_map/dot_general | solution.py:22
  112.5 2.3 %fusion.8 = f32[32,1024]{1,0:T(8,128)S(1)} fusion(f32[32,1024]{1,0:T(8,128)S(1)} %fusion.68, f32[2,8,1024,256]{3,2,1,0:T(8,128)} %param.5, f32[32,256,1,1]{1,3,2,0:T(1,128)S(1)} %get-tuple-element.23), kind=kOutput, calls=%fused_computation.17 | convolution fusion | flops 100728832 | bytes 1343488 | tf_op jit(solution)/shard_map/dot_general | solution.py:22
  114.8 2.3 %fusion.6 = f32[32,1024]{1,0:T(8,128)S(1)} fusion(f32[32,1024]{1,0:T(8,128)S(1)} %fusion.60, f32[2,8,1024,256]{3,2,1,0:T(8,128)} %param.5, f32[32,256,1,1]{1,3,2,0:T(1,128)S(1)} %get-tuple-element.21), kind=kOutput, calls=%fused_computation.13 | convolution fusion | flops 100728832 | bytes 1343488 | tf_op jit(solution)/shard_map/dot_general | solution.py:22
  117.0 2.3 %fusion.4 = f32[32,1024]{1,0:T(8,128)S(1)} fusion(f32[32,1024]{1,0:T(8,128)S(1)} %fusion.52, f32[2,8,1024,256]{3,2,1,0:T(8,128)} %param.5, f32[32,256,1,1]{1,3,2,0:T(1,128)S(1)} %get-tuple-element.19), kind=kOutput, calls=%fused_computation.9 | convolution fusion | flops 100728832 | bytes 1343488 | tf_op jit(solution)/shard_map/dot_general | solution.py:22
  119.3 2.3 %fusion.2 = f32[32,1024]{1,0:T(8,128)S(1)} fusion(f32[32,1024]{1,0:T(8,128)S(1)} %fusion.44, f32[2,8,1024,256]{3,2,1,0:T(8,128)} %param.5, f32[32,256,1,1]{1,3,2,0:T(1,128)S(1)} %get-tuple-element.17), kind=kOutput, calls=%fused_computation.5 | convolution fusion | flops 100728832 | bytes 1343488 | tf_op jit(solution)/shard_map/dot_general | solution.py:22
  121.6 2.3 %fusion = f32[32,1024]{1,0:T(8,128)S(1)} fusion(f32[32,1024]{1,0:T(8,128)S(1)} %fusion.36, f32[2,8,1024,256]{3,2,1,0:T(8,128)} %param.5, f32[32,256,1,1]{1,3,2,0:T(1,128)S(1)} %get-tuple-element.15), kind=kOutput, calls=%fused_computation.1 | convolution fusion | flops 100728832 | bytes 1343488 | tf_op jit(solution)/shard_map/dot_general | solution.py:22
  128.8 2.3 %fusion.31 = f32[1024]{0:T(1024)S(1)} fusion(f32[32,1024]{1,0:T(8,128)S(1)} %fusion.14, f32[32,1024]{1,0:T(8,128)S(1)} %fusion.94, f32[2,8,1024,256]{3,2,1,0:T(8,128)} %param.5, f32[32,256,1,1]{1,3,2,0:T(1,128)S(1)} %get-tuple-element.28), kind=kOutput, calls=%fused_computation.47 | convolution fusion | flops 100793344 | bytes 1347584 | tf_op jit(solution)/shard_map/dot_general | solution.py:22
  131.1 2.3 %fusion.30 = f32[1024]{0:T(1024)S(1)} fusion(f32[32,1024]{1,0:T(8,128)S(1)} %fusion.12, f32[32,1024]{1,0:T(8,128)S(1)} %fusion.86, f32[2,8,1024,256]{3,2,1,0:T(8,128)} %param.5, f32[32,256,1,1]{1,3,2,0:T(1,128)S(1)} %get-tuple-element.26), kind=kOutput, calls=%fused_computation.46 | convolution fusion | flops 100793344 | bytes 1347584 | tf_op jit(solution)/shard_map/dot_general | solution.py:22
  133.4 2.3 %fusion.29 = f32[1024]{0:T(1024)S(1)} fusion(f32[32,1024]{1,0:T(8,128)S(1)} %fusion.10, f32[32,1024]{1,0:T(8,128)S(1)} %fusion.78, f32[2,8,1024,256]{3,2,1,0:T(8,128)} %param.5, f32[32,256,1,1]{1,3,2,0:T(1,128)S(1)} %get-tuple-element.24), kind=kOutput, calls=%fused_computation.45 | convolution fusion | flops 100793344 | bytes 1347584 | tf_op jit(solution)/shard_map/dot_general | solution.py:22
  135.7 2.3 %fusion.28 = f32[1024]{0:T(1024)S(1)} fusion(f32[32,1024]{1,0:T(8,128)S(1)} %fusion.8, f32[32,1024]{1,0:T(8,128)S(1)} %fusion.70, f32[2,8,1024,256]{3,2,1,0:T(8,128)} %param.5, f32[32,256,1,1]{1,3,2,0:T(1,128)S(1)} %get-tuple-element.22), kind=kOutput, calls=%fused_computation.44 | convolution fusion | flops 100793344 | bytes 1347584 | tf_op jit(solution)/shard_map/dot_general | solution.py:22
  138.0 2.3 %fusion.27 = f32[1024]{0:T(1024)S(1)} fusion(f32[32,1024]{1,0:T(8,128)S(1)} %fusion.6, f32[32,1024]{1,0:T(8,128)S(1)} %fusion.62, f32[2,8,1024,256]{3,2,1,0:T(8,128)} %param.5, f32[32,256,1,1]{1,3,2,0:T(1,128)S(1)} %get-tuple-element.20), kind=kOutput, calls=%fused_computation.43 | convolution fusion | flops 100793344 | bytes 1347584 | tf_op jit(solution)/shard_map/dot_general | solution.py:22
  140.3 2.3 %fusion.26 = f32[1024]{0:T(1024)S(1)} fusion(f32[32,1024]{1,0:T(8,128)S(1)} %fusion.4, f32[32,1024]{1,0:T(8,128)S(1)} %fusion.54, f32[2,8,1024,256]{3,2,1,0:T(8,128)} %param.5, f32[32,256,1,1]{1,3,2,0:T(1,128)S(1)} %get-tuple-element.18), kind=kOutput, calls=%fused_computation.42 | convolution fusion | flops 100793344 | bytes 1347584 | tf_op jit(solution)/shard_map/dot_general | solution.py:22
  142.6 2.3 %fusion.25 = f32[1024]{0:T(1024)S(1)} fusion(f32[32,1024]{1,0:T(8,128)S(1)} %fusion.2, f32[32,1024]{1,0:T(8,128)S(1)} %fusion.46, f32[2,8,1024,256]{3,2,1,0:T(8,128)} %param.5, f32[32,256,1,1]{1,3,2,0:T(1,128)S(1)} %get-tuple-element.16), kind=kOutput, calls=%fused_computation.41 | convolution fusion | flops 100793344 | bytes 1347584 | tf_op jit(solution)/shard_map/dot_general | solution.py:22
  144.9 2.3 %fusion.24 = f32[1024]{0:T(1024)S(1)} fusion(f32[32,1024]{1,0:T(8,128)S(1)} %fusion, f32[32,1024]{1,0:T(8,128)S(1)} %fusion.38, f32[2,8,1024,256]{3,2,1,0:T(8,128)} %param.5, f32[32,256,1,1]{1,3,2,0:T(1,128)S(1)} %get-tuple-element.14), kind=kOutput, calls=%fused_computation.40 | convolution fusion | flops 100793344 | bytes 1347584 | tf_op jit(solution)/shard_map/dot_general | solution.py:22
  147.2 7.1 %all-reduce = f32[1024]{0:T(1024)S(1)} all-reduce(f32[1024]{0:T(1024)S(1)} %add_multiply_fusion), channel_id=2, replica_groups=mesh['tm'=4,'rep'=8] {'tm'}, use_global_device_ids=true, to_apply=%region_24.25.clone | all-reduce | flops 1024 | bytes 8192
  (27 shorter events, 21.7 us)
Async XLA Ops:
  0.0 1.4 copy-start
  50.9 12.3 %all-to-all-start = ((f32[8,256,2,32]{1,2,0,3:T(2,128)}), f32[8,256,2,32]{1,2,0,3:T(2,128)S(1)}, u32[]{:S(2)}, u32[]{:S(2)}) async-start(f32[8,256,2,32]{1,2,0,3:T(2,128)} %copy.19), calls=%async_computation | async-start | bytes 1048576 | tf_op jit(solution)/shard_map/all_to_all | solution.py:33
where the time goes:
time: 156 us; the launch traced here: 155 us
  matrix products  74 us (47%)
  blocking collectives  53.4 us (34%)
  other arithmetic  13.1 us (8%)
  between operations  5.94 us (4%)
  local copies, waits for them, and re-layouts  4.76 us (3%)
  starting transfers between devices  3.47 us (2%)
    dot_general x33, matrix products, matmul(): jnp.dot(left, right, precision=lax.Precision.HIGHEST, preferred_element_t...  74 us
    all_gather x1, blocking collectives, shards(): gathered = lax.all_gather(spectra, 'rep', axis=1, tiled=True)  46.3 us
    unnamed x1, blocking collectives  7.1 us
    reduce_sum x1, other arithmetic, shards(): norm_sq = jnp.sum(rep_re * rep_re + rep_im * rep_im, axis=1) + epsilon  6.6 us
    reduce_sum x8, other arithmetic, shards(): jnp.sum(spec_re * spec_re + spec_im * spec_im) / total_snaps + epsilon  5.07 us
    all_to_all x1, starting transfers between devices, shards(): lax.all_to_all(gathered, 'tm', split_axis=3, concat_axis=0, tiled=True)  3.47 us
  transfers between devices with their start and end apart: 1, of which 1 were waited for; matrix products, arithmetic and copies ran while one was open for 5% of the time, Pallas kernels for 0%

commit v1 on v0

v1 whole, which is shorter than its diff:
```python
import functools
import math

import jax
import jax.numpy as jnp
from jax import lax
from jax.experimental import pallas as pl
from jax.experimental.pallas import tpu as pltpu
from jax.sharding import PartitionSpec as P

EPS = 1e-06
HIGHEST = lax.Precision.HIGHEST
F32 = jnp.float32
BF16 = jnp.bfloat16


def split(x):
    high = x.astype(BF16)
    return high, (x - high.astype(F32)).astype(BF16)


def dft_kernel(owners, repeats, bins_ref, snap_ref, out_ref, table_ref):
    snaps, elems, samples = snap_ref.shape
    bins = bins_ref.shape[0]
    cols = 2 * bins
    group = cols // owners
    fine = 2 ** (samples.bit_length() // 2)
    while samples % fine:
        fine //= 2
    coarse = samples // fine
    turn = 2.0 * math.pi / samples

    lane = lax.broadcasted_iota(jnp.int32, (1, cols), 1)
    bin_row = jnp.zeros((1, cols), jnp.int32)
    for k in range(bins):
        bin_row = jnp.where(lane // 2 == k, bins_ref[k], bin_row)
    odd = lane % 2 == 1

    def angle(count, step, freq):
        steps = lax.broadcasted_iota(jnp.int32, (count, cols), 0) * step
        return (steps * freq % samples).astype(F32) * turn

    angle_c, angle_f = angle(coarse, fine, bin_row), angle(fine, 1, bin_row)
    cos_c, sin_c = jnp.cos(angle_c), jnp.sin(angle_c)
    cos_f, sin_f = jnp.cos(angle_f), jnp.sin(angle_f)
    left = jnp.where(odd, -sin_c, cos_c)
    right = jnp.where(odd, cos_c, sin_c)
    win_c, win_f = angle(coarse, fine, 1), angle(fine, 1, 1)
    wcos_c, wsin_c = jnp.cos(win_c), jnp.sin(win_c)
    wcos_f, wsin_f = jnp.cos(win_f), jnp.sin(win_f)
    for a in range(coarse):
        row = slice(a, a + 1)
        window = 0.5 - 0.5 * (wcos_c[row] * wcos_f - wsin_c[row] * wsin_f)
        table_ref[a * fine : (a + 1) * fine, :] = window * (left[row] * cos_f - right[row] * sin_f)

    spectra = jnp.dot(
        snap_ref[...].reshape(snaps * elems, samples), table_ref[...], precision=HIGHEST, preferred_element_type=F32
    )
    width = snaps * group
    source = lax.broadcasted_iota(jnp.int32, (width, width), 0)
    target = lax.broadcasted_iota(jnp.int32, (width, width), 1)
    order = jnp.where(source == target % snaps * group + target // snaps, 1.0, 0.0)
    for t in range(owners):
        pieces = [spectra[s * elems : (s + 1) * elems, t * group : (t + 1) * group] for s in range(snaps)]
        message = jnp.dot(
            jnp.concatenate(pieces, axis=1), order, precision=HIGHEST, preferred_element_type=F32
        )
        for r in range(repeats):
            out_ref[r, t] = message


def main_kernel(total_snaps, bins, spec_ref, rep_ref, out_ref, sum_ref):
    reps, owners, elems, width = spec_ref.shape
    local_bins = pl.num_programs(0)
    col = pl.program_id(0)
    grid_rows, elem_count = rep_ref.shape[2], rep_ref.shape[3]
    chunk = out_ref.shape[1]

    @pl.when(col == 0)
    def _():
        sum_ref[...] = jnp.zeros_like(sum_ref)

    group = 2 * (total_snaps // owners)
    lanes = owners * group
    pieces = []
    for t in range(owners):
        block = spec_ref[:, t].reshape(reps * elems, width)
        rolled = pltpu.roll(block, width - col * group, 1) if width > group else block
        pieces.append(rolled[:, :group])
    spec = jnp.concatenate(pieces, axis=1)
    trace = jnp.sum(spec * spec) / total_snaps + EPS
    half = group // 2
    place = lax.broadcasted_iota(jnp.int32, spec.shape, 1) % group
    turned = jnp.where(place < half, pltpu.roll(spec, lanes - half, 1), -pltpu.roll(spec, half, 1))
    spec_hi, spec_lo = split(spec)
    turned_hi, turned_lo = split(turned)
    zero = jnp.zeros_like(spec_hi)
    right_re = jnp.concatenate([spec_hi, spec_lo], axis=1)
    right_im = jnp.concatenate([turned_hi, turned_lo], axis=1)
    low_re = jnp.concatenate([spec_hi, zero], axis=1)
    low_im = jnp.concatenate([turned_hi, zero], axis=1)
    dot = functools.partial(jnp.dot, preferred_element_type=F32)
    factor = 0.5 * elem_count / (trace * total_snaps * bins)
    tile = chunk
    for k in range(grid_rows // tile):
        rows = slice(k * tile, (k + 1) * tile)
        re, im = rep_ref[0, 0, rows], rep_ref[1, 0, rows]
        norm = jnp.sum(re * re + im * im, axis=1, keepdims=True) + EPS
        re_hi, re_lo = split(re)
        im_hi, im_lo = split(im)
        proj = dot(re_hi, right_re) + dot(im_hi, right_im) + dot(re_lo, low_re) + dot(im_lo, low_im)
        proj = proj + pltpu.roll(proj, lanes, 1)
        sum_ref[rows] += proj * proj * (factor / norm)

    @pl.when(col == local_bins - 1)
    def _():
        ones = jnp.ones((8, sum_ref.shape[1]), F32)
        for k in range(out_ref.shape[0]):
            block = sum_ref[k * chunk : (k + 1) * chunk]
            row = lax.dot_general(
                ones, block, (((1,), (1,)), ((), ())), precision=HIGHEST, preferred_element_type=F32
            )
            out_ref[k : k + 1] = row[0:1]


def partners(count, step):
    if count & (count - 1) == 0:
        return [(i, i ^ step) for i in range(count)]
    return [(i, (i + step) % count) for i in range(count)]


def shards(tm, rep, snapshots, freq_bins, replicas):
    snaps, elems, samples = snapshots.shape
    bins = freq_bins.shape[0]
    _, local_bins, grid_rows, elem_count = replicas.shape
    width = 2 * local_bins * snaps
    total_snaps = snaps * tm
    messages = pl.pallas_call(
        functools.partial(dft_kernel, tm, rep),
        out_shape=jax.ShapeDtypeStruct((rep, tm, elems, width), F32),
        in_specs=[pl.BlockSpec(memory_space=pltpu.SMEM), pl.BlockSpec(memory_space=pltpu.VMEM)],
        out_specs=pl.BlockSpec(memory_space=pltpu.VMEM),
        scratch_shapes=[pltpu.VMEM((samples, 2 * bins), F32)],
        compiler_params=pltpu.CompilerParams(vmem_limit_bytes=24 * 2**20),
        name="dft",
    )(freq_bins, snapshots)
    spectra = lax.all_to_all(
        messages.reshape(rep * tm, elems, width), ("rep", "tm"), split_axis=0, concat_axis=0, tiled=True
    ).reshape(rep, tm, elems, width)
    partial = pl.pallas_call(
        functools.partial(main_kernel, total_snaps, bins),
        grid=(local_bins,),
        out_shape=jax.ShapeDtypeStruct((tm, grid_rows // tm), F32),
        in_specs=[
            pl.BlockSpec((rep, tm, elems, width), lambda f: (0, 0, 0, 0)),
            pl.BlockSpec((2, 1, grid_rows, elem_count), lambda f: (0, f, 0, 0)),
        ],
        out_specs=pl.BlockSpec((tm, grid_rows // tm), lambda f: (0, 0)),
        scratch_shapes=[pltpu.VMEM((grid_rows, 4 * total_snaps), F32)],
        compiler_params=pltpu.CompilerParams(vmem_limit_bytes=32 * 2**20),
        name="power",
    )(spectra, replicas)
    me = lax.axis_index("tm")
    result = lax.dynamic_index_in_dim(partial, me, 0, keepdims=False)
    for step in range(1, tm):
        to = me ^ step if tm & (tm - 1) == 0 else (me + step) % tm
        mine = lax.dynamic_index_in_dim(partial, to, 0, keepdims=False)
        result = result + lax.ppermute(mine, "tm", partners(tm, step))
    return result


def solution(mesh):
    in_specs = (P("tm", "rep", None), P(), P(None, "tm", "rep", None))
    body = functools.partial(shards, mesh.shape["tm"], mesh.shape["rep"])
    return jax.shard_map(body, mesh=mesh, in_specs=in_specs, out_specs=P(("rep", "tm")), check_vma=False)
```

time: 156 us -> 52.3 us (0.34)
  matrix products: 74 us -> 0 us
  blocking collectives: 53.4 us -> 0 us
  waiting for transfers between devices: 0.3 us -> 18.2 us
  Pallas kernels: 0 us -> 16.4 us
  other arithmetic: 13.1 us -> 0.57 us
  between operations: 5.94 us -> 0.05 us
  starting transfers between devices: 3.47 us -> 9.22 us
  local copies, waits for them, and re-layouts: 4.76 us -> 7.67 us
    dot_general x33 -> x0, matrix products: 74 us -> none  [matmul(): jnp.dot(left, right, precision=lax.Precision.HIGHEST, preferred_element_t...]
    all_gather x1 -> x0, blocking collectives: 46.3 us -> none  [shards(): gathered = lax.all_gather(spectra, 'rep', axis=1, tiled=True)]
    pallas_call x0 -> x2, Pallas kernels: none -> 16.4 us  [the longest x1 12.9 us: shards(): pl.pallas_call(functools.partial(main_kernel, total_snaps, bins), grid=(l...]
    all_to_all x1, waiting for transfers between devices: 0.3 us -> 15.5 us  [shards(): lax.all_to_all(messages.reshape(rep * tm, elems, width), ('rep', 'tm'), s...]
    reduce_sum x9 -> x0, other arithmetic: 11.7 us -> none  [the longest x1 6.6 us: shards(): norm_sq = jnp.sum(rep_re * rep_re + rep_im * rep_im, axis=1) + epsilon]
    unnamed x1 -> x0, blocking collectives: 7.1 us -> none
    unnamed x4 -> x6, local copies, waits for them, and re-layouts: 1.88 us -> 7.65 us
    all_to_all x1, starting transfers between devices: 3.47 us -> 7.3 us  [shards(): lax.all_to_all(messages.reshape(rep * tm, elems, width), ('rep', 'tm'), s...]
  transfers between devices with their start and end apart: 1 -> 4, of which waited for: 1 -> 3; matrix products, arithmetic and copies ran while one was open for 5% -> 0% of each run, Pallas kernels for 0% -> 0%
where the time goes in v1:
time: 52.3 us; the launch traced here: 52.1 us
  waiting for transfers between devices  18.2 us (35%)
  Pallas kernels  16.4 us (31%)
  starting transfers between devices  9.22 us (18%)
  local copies, waits for them, and re-layouts  7.67 us (15%)
  other arithmetic  0.57 us (1%)
    all_to_all x1, waiting for transfers between devices, shards(): lax.all_to_all(messages.reshape(rep * tm, elems, width), ('rep', 'tm'), s...  15.5 us
    pallas_call x1, Pallas kernels, shards(): pl.pallas_call(functools.partial(main_kernel, total_snaps, bins), grid=(l...  12.9 us
    unnamed x6, local copies, waits for them, and re-layouts  7.65 us
    all_to_all x1, starting transfers between devices, shards(): lax.all_to_all(messages.reshape(rep * tm, elems, width), ('rep', 'tm'), s...  7.3 us
    pallas_call x1, Pallas kernels, shards(): pl.pallas_call(functools.partial(dft_kernel, tm, rep), out_shape=jax.Shap...  3.51 us
    ppermute x3, waiting for transfers between devices, shards(): result = result + lax.ppermute(mine, 'tm', partners(tm, step))  2.65 us
    ppermute x3, starting transfers between devices, shards(): result = result + lax.ppermute(mine, 'tm', partners(tm, step))  1.93 us
  transfers between devices with their start and end apart: 4, of which 3 were waited for; matrix products, arithmetic and copies ran while one was open for 0% of the time, Pallas kernels for 0%

profile of v1, /device:TPU:0, one launch (start us, length us, event | category | flops | bytes accessed | tf_op | source)
XLA Modules:
  0.0 52.1 jit_solution(1929684774228460234)
XLA Ops:
  0.0 0.0 copy-start.1
  0.0 1.2 %copy-done.1 = f32[8,32,1024]{2,1,0:T(8,128)S(1)} copy-done((f32[8,32,1024]{2,1,0:T(8,128)S(1)}, f32[8,32,1024]{2,1,0:T(8,128)}, u32[]{:S(2)}) %copy-start.1) | copy-done | bytes 1048600
  1.2 0.0 copy-start.2
  1.2 0.7 %copy-done.2 = s32[32]{0:T(128)S(1)} copy-done((s32[32]{0:T(128)S(1)}, s32[32]{0:T(128)}, u32[]{:S(2)}) %copy-start.2) | copy-done | bytes 152
  1.9 3.5 %dft.1 = f32[8,4,32,128]{3,2,1,0:T(8,128)} custom-call(s32[32]{0:T(128)S(1)} %copy-done.2, f32[8,32,1024]{2,1,0:T(8,128)S(1)} %copy-done.1), custom_call_target="tpu_custom_call" | custom-call | tf_op jit(solution)/shard_map/dft/pallas_call | solution.py:138
  5.4 7.3 %all-to-all-start = ((f32[32,32,128]{2,1,0:T(8,128)}), f32[32,32,128]{2,1,0:T(8,128)S(1)}, u32[]{:S(2)}, u32[]{:S(2)}) async-start(f32[32,32,128]{2,1,0:T(8,128)} %bitcast), calls=%async_computation | async-start | bytes 1048576 | tf_op jit(solution)/shard_map/all_to_all | solution.py:147
  12.7 15.5 %all-to-all-done = f32[32,32,128]{2,1,0:T(8,128)S(1)} async-done(((f32[32,32,128]{2,1,0:T(8,128)}), f32[32,32,128]{2,1,0:T(8,128)S(1)}, u32[]{:S(2)}, u32[]{:S(2)}) %all-to-all-start) | async-done | bytes 524320 | tf_op jit(solution)/shard_map/all_to_all | solution.py:147
  28.2 0.0 copy-start
  28.2 5.8 %copy-done = f32[2,8,1024,256]{3,2,1,0:T(8,128)S(1)} copy-done((f32[2,8,1024,256]{3,2,1,0:T(8,128)S(1)}, f32[2,8,1024,256]{3,2,1,0:T(8,128)}, u32[]{:S(2)}) %copy-start) | copy-done | bytes 16777240
  34.0 12.9 %power.1 = f32[4,256]{1,0:T(4,128)S(1)} custom-call(f32[8,4,32,128]{3,2,1,0:T(8,128)S(1)} %bitcast.6, f32[2,8,1024,256]{3,2,1,0:T(8,128)S(1)} %copy-done), custom_call_target="tpu_custom_call" | custom-call | tf_op jit(solution)/shard_map/power/pallas_call | solution.py:150
  46.9 1.0 %collective-permute-start.2 = (f32[256]{0:T(256)S(1)}, f32[256]{0:T(256)S(1)}, u32[]{:S(2)}, u32[]{:S(2)}) collective-permute-start(f32[256]{0:T(256)S(1)} %bitcast.10), channel_id=1, source_target_pairs={{0,24},{8,16},{16,8},{24,0},{1,25},{9,17},{17,9},{25,1},{2,26},{10... | collective-permute-start | bytes 3080 | tf_op jit(solution)/shard_map/ppermute | solution.py:168
  47.9 0.6 %collective-permute-start.1 = (f32[256]{0:T(256)S(1)}, f32[256]{0:T(256)S(1)}, u32[]{:S(2)}, u32[]{:S(2)}) collective-permute-start(f32[256]{0:T(256)S(1)} %bitcast.9), channel_id=1, source_target_pairs={{0,16},{8,24},{16,0},{24,8},{1,17},{9,25},{17,1},{25,9},{2,18},{10... | collective-permute-start | bytes 3080 | tf_op jit(solution)/shard_map/ppermute | solution.py:168
  48.5 0.3 collective-permute-start
  48.9 1.1 %collective-permute-done.2 = f32[256]{0:T(256)S(1)} collective-permute-done((f32[256]{0:T(256)S(1)}, f32[256]{0:T(256)S(1)}, u32[]{:S(2)}, u32[]{:S(2)}) %collective-permute-start.2) | collective-permute-done | bytes 1056 | tf_op jit(solution)/shard_map/ppermute | solution.py:168
  50.0 1.5 %collective-permute-done.1 = f32[256]{0:T(256)S(1)} collective-permute-done((f32[256]{0:T(256)S(1)}, f32[256]{0:T(256)S(1)}, u32[]{:S(2)}, u32[]{:S(2)}) %collective-permute-start.1) | collective-permute-done | bytes 1056 | tf_op jit(solution)/shard_map/ppermute | solution.py:168
  51.5 0.0 collective-permute-done
  51.5 0.6 %add_add_fusion = f32[256]{0:T(256)} fusion(f32[256]{0:T(256)S(1)} %collective-permute-done.2, f32[256]{0:T(256)S(1)} %collective-permute-done.1, f32[256]{0:T(256)S(1)} %bitcast.7, f32[256]{0:T(256)S(1)} %collective-permute-done), kind=kLoop, calls=%fused_computation | loop fusion | flops 768 | bytes 5120 | tf_op jit(solution)/shard_map/add | solution.py:168
  (1 shorter events, 0.0 us)
Async XLA Ops:
  0.0 1.2 %copy-start.1 = (f32[8,32,1024]{2,1,0:T(8,128)S(1)}, f32[8,32,1024]{2,1,0:T(8,128)}, u32[]{:S(2)}) copy-start(f32[8,32,1024]{2,1,0:T(8,128)} %snap_ref.1) | copy-start | bytes 3145732
  1.2 0.7 %copy-start.2 = (s32[32]{0:T(128)S(1)}, s32[32]{0:T(128)}, u32[]{:S(2)}) copy-start(s32[32]{0:T(128)} %bins_ref.1) | copy-start | bytes 388
  5.4 22.9 %all-to-all-start = ((f32[32,32,128]{2,1,0:T(8,128)}), f32[32,32,128]{2,1,0:T(8,128)S(1)}, u32[]{:S(2)}, u32[]{:S(2)}) async-start(f32[32,32,128]{2,1,0:T(8,128)} %bitcast), calls=%async_computation | async-start | bytes 1048576 | tf_op jit(solution)/shard_map/all_to_all | solution.py:147
  28.2 5.8 %copy-start = (f32[2,8,1024,256]{3,2,1,0:T(8,128)S(1)}, f32[2,8,1024,256]{3,2,1,0:T(8,128)}, u32[]{:S(2)}) copy-start(f32[2,8,1024,256]{3,2,1,0:T(8,128)} %rep_ref.1) | copy-start | bytes 50331652
  46.9 3.1 %collective-permute-start.2 = (f32[256]{0:T(256)S(1)}, f32[256]{0:T(256)S(1)}, u32[]{:S(2)}, u32[]{:S(2)}) collective-permute-start(f32[256]{0:T(256)S(1)} %bitcast.10), channel_id=1, source_target_pairs={{0,24},{8,16},{16,8},{24,0},{1,25},{9,17},{17,9},{25,1},{2,26},{10... | collective-permute-start | bytes 3080 | tf_op jit(solution)/shard_map/ppermute | solution.py:168
  47.9 3.6 %collective-permute-start.1 = (f32[256]{0:T(256)S(1)}, f32[256]{0:T(256)S(1)}, u32[]{:S(2)}, u32[]{:S(2)}) collective-permute-start(f32[256]{0:T(256)S(1)} %bitcast.9), channel_id=1, source_target_pairs={{0,16},{8,24},{16,0},{24,8},{1,17},{9,25},{17,1},{25,9},{2,18},{10... | collective-permute-start | bytes 3080 | tf_op jit(solution)/shard_map/ppermute | solution.py:168
  48.5 3.0 %collective-permute-start = (f32[256]{0:T(256)S(1)}, f32[256]{0:T(256)S(1)}, u32[]{:S(2)}, u32[]{:S(2)}) collective-permute-start(f32[256]{0:T(256)S(1)} %bitcast.8), channel_id=1, source_target_pairs={{0,8},{8,0},{16,24},{24,16},{1,9},{9,1},{17,25},{25,17},{2,10},{10... | collective-permute-start | bytes 3080 | tf_op jit(solution)/shard_map/ppermute | solution.py:168

commit v2 on v0

v2 whole, which is shorter than its diff:
```python
import functools
import math

import jax
import jax.numpy as jnp
from jax import lax
from jax.experimental import pallas as pl
from jax.experimental.pallas import tpu as pltpu
from jax.sharding import PartitionSpec as P

EPS = 1e-06
HIGHEST = lax.Precision.HIGHEST
F32 = jnp.float32
BF16 = jnp.bfloat16
MIB = 2**20


def dot(left, right):
    return jnp.dot(left, right, preferred_element_type=F32)


def halves(x):
    high = x.astype(BF16).astype(F32)
    return high, x - high


def dft_kernel(owners, bins_hbm, snap_hbm, out_ref, snap_ref, bins_ref, table_ref, sems):
    snaps, elems, samples = snap_ref.shape
    bins = bins_ref.shape[0]
    load_bins = pltpu.make_async_copy(bins_hbm, bins_ref, sems.at[0])
    load_snaps = pltpu.make_async_copy(snap_hbm, snap_ref, sems.at[1])
    load_bins.start()
    load_snaps.start()
    me = lax.axis_index("tm")
    cols = 2 * bins
    group = cols // owners
    fine = 1
    while fine * fine < samples and samples % (2 * fine) == 0:
        fine *= 2
    coarse = samples // fine
    turn = 2.0 * math.pi / samples

    def angle(count, step, freq):
        steps = lax.broadcasted_iota(jnp.int32, (count, cols), 0) * step
        return (steps * freq % samples).astype(F32) * turn

    win_c, win_f = angle(coarse, fine, 1), angle(fine, 1, 1)
    wcos_c, wsin_c = jnp.cos(win_c), jnp.sin(win_c)
    wcos_f, wsin_f = jnp.cos(win_f), jnp.sin(win_f)
    lane = lax.broadcasted_iota(jnp.int32, (1, cols), 1)
    odd = lane % 2 == 1
    bin_row = jnp.zeros((1, cols), jnp.int32)
    load_bins.wait()
    for d in range(owners):
        for f in range(group // 2):
            value = bins_ref[(me ^ d) * (group // 2) + f]
            bin_row = jnp.where(lane // 2 == d * (group // 2) + f, value, bin_row)
    angle_c, angle_f = angle(coarse, fine, bin_row), angle(fine, 1, bin_row)
    cos_c, sin_c = jnp.cos(angle_c), jnp.sin(angle_c)
    cos_f, sin_f = jnp.cos(angle_f), jnp.sin(angle_f)
    left = jnp.where(odd, -sin_c, cos_c)
    right = jnp.where(odd, cos_c, sin_c)
    for a in range(coarse):
        row = slice(a, a + 1)
        window = 0.5 - 0.5 * (wcos_c[row] * wcos_f - wsin_c[row] * wsin_f)
        high, low = halves(window * (left[row] * cos_f - right[row] * sin_f))
        table_ref[a * fine : (a + 1) * fine, :] = jnp.concatenate([high, low], axis=1).astype(BF16)
    load_snaps.wait()
    high, low = halves(snap_ref[...].reshape(snaps * elems, samples))
    product = dot(high.astype(BF16), table_ref[...]) + dot(low.astype(BF16), table_ref[...])
    spectra = product[:, :cols] + product[:, cols:]

    width = snaps * group
    source = lax.broadcasted_iota(jnp.int32, (width, width), 0)
    target = lax.broadcasted_iota(jnp.int32, (width, width), 1)
    order = jnp.where(source == target % snaps * group + target // snaps, 1.0, 0.0).astype(BF16)
    messages = jnp.concatenate(
        [
            jnp.concatenate(
                [spectra[s * elems : (s + 1) * elems, d * group : (d + 1) * group] for s in range(snaps)], axis=1
            )
            for d in range(owners)
        ],
        axis=0,
    )
    high, rest = halves(messages)
    middle, low = halves(rest)
    moved = dot(high.astype(BF16), order) + dot(middle.astype(BF16), order) + dot(low.astype(BF16), order)
    out_ref[...] = moved.reshape(out_ref.shape)


def pack_kernel(local_bins, *refs):
    *blocks, out_ref = refs
    parts = [ref[k] for ref in blocks for k in range(ref.shape[0])]
    group = parts[0].shape[1] // local_bins
    out_ref[0] = jnp.concatenate(
        [part[:, f * group : (f + 1) * group] for f in range(local_bins) for part in parts], axis=1
    )


def prepare_kernel(elems, rep_ref, high_ref, low_ref):
    f = pl.program_id(0)
    rows, elem_count = rep_ref.shape[2:]
    tile = math.gcd(rows, 128)
    step = 128 if 128 % (2 * elems) == 0 and elem_count % 128 == 0 else elem_count
    lane = lax.broadcasted_iota(jnp.int32, (tile, step), 1)
    even = lane // elems % 2 == 0

    def body(k, _):
        at = pl.ds(pl.multiple_of(k * tile, tile), tile)
        re, im = rep_ref[0, 0, at], rep_ref[1, 0, at]
        scale = lax.rsqrt(jnp.sum(re * re + im * im, axis=1, keepdims=True) + EPS)
        for j in range(elem_count // step):
            cut = slice(j * step, (j + 1) * step)
            real, imag = re[:, cut] * scale, im[:, cut] * scale
            pair = (
                jnp.where(even, real, pltpu.roll(imag, elems, 1)),
                jnp.where(even, pltpu.roll(real, step - elems, 1), imag),
            )
            for a in range(2):
                high = pair[a].astype(BF16)
                high_ref[a, f, at, cut] = high
                low_ref[a, f, at, cut] = (pair[a] - high.astype(F32)).astype(BF16)
        return 0

    lax.fori_loop(0, rows // tile, body, 0)


def operand(spec_ref, f, lanes, half, side, me, bits):
    count = spec_ref.shape[0]
    blocks = []
    for p in range(count):
        apart = (2 * p + side) ^ me
        slot = 0
        for k in range(1, bits):
            slot = slot + ((apart >> k) & 1) * (1 << (bits - 1 - k))
        block = spec_ref[slot, :, f * lanes : (f + 1) * lanes]
        place = lax.broadcasted_iota(jnp.int32, block.shape, 1) % (2 * half)
        turned = jnp.where(place < half, pltpu.roll(block, lanes - half, 1), -pltpu.roll(block, half, 1))
        blocks += [block, turned]
    high, low = halves(jnp.concatenate(blocks, axis=0))
    return jnp.concatenate([high, low], axis=1).astype(BF16)


def first_kernel(half, bits, spec_ref, high_ref, low_ref, proj_ref):
    _, local_bins, rows, _ = high_ref.shape
    lanes = spec_ref.shape[2] // local_bins
    me = lax.axis_index("rep")
    side = me & 1
    for f in range(local_bins):
        right = operand(spec_ref, f, lanes, half, side, me, bits)
        proj_ref[f] = dot(high_ref[side, f], right) + dot(low_ref[side, f], right)


def second_kernel(bins, half, bits, spec_ref, own_ref, proj_ref, high_ref, low_ref, out_ref, sum_ref):
    _, local_bins, rows, elem_count = high_ref.shape
    lanes = spec_ref.shape[2] // local_bins
    total_snaps = lanes // 2
    chunk = out_ref.shape[1]
    me = lax.axis_index("rep")
    side = 1 - (me & 1)
    for f in range(local_bins):
        right = operand(spec_ref, f, lanes, half, side, me ^ 1, bits)
        cut = slice(f * lanes, (f + 1) * lanes)
        mine, other = own_ref[:, :, cut], spec_ref[:, :, cut]
        trace = jnp.sum(mine * mine + other * other) / total_snaps + EPS
        factor = 0.5 * elem_count / (trace * total_snaps * bins)
        for k in range(out_ref.shape[0]):
            at = slice(k * chunk, (k + 1) * chunk)
            proj = proj_ref[f, at] + dot(high_ref[side, f, at], right) + dot(low_ref[side, f, at], right)
            proj += pltpu.roll(proj, lanes, 1)
            value = proj * proj * factor
            sum_ref[at] = value if f == 0 else sum_ref[at] + value
    ones = jnp.ones((8, 2 * lanes), F32)
    for k in range(out_ref.shape[0]):
        block = sum_ref[k * chunk : (k + 1) * chunk]
        row = lax.dot_general(ones, block, (((1,), (1,)), ((), ())), precision=HIGHEST, preferred_element_type=F32)
        out_ref[k : k + 1] = row[0:1]


def swap(x, axis, count, bit):
    return lax.ppermute(x, axis, [(i, i ^ bit) for i in range(count)])


def bits_of(count):
    assert count & (count - 1) == 0
    return [1 << k for k in reversed(range(count.bit_length() - 1))]


def shards(tm, rep, snapshots, freq_bins, replicas):
    snaps, elems, samples = snapshots.shape
    bins = freq_bins.shape[0]
    _, local_bins, rows, elem_count = replicas.shape
    width = 2 * local_bins * snaps
    lanes = 2 * snaps * tm
    vmem = pl.BlockSpec(memory_space=pltpu.VMEM)
    hbm = pl.BlockSpec(memory_space=pltpu.HBM)
    parts = (2, local_bins, rows, elem_count)
    high, low = pl.pallas_call(
        functools.partial(prepare_kernel, elems),
        grid=(local_bins,),
        out_shape=(pltpu.VMEM(parts, BF16), pltpu.VMEM(parts, BF16)),
        in_specs=[pl.BlockSpec((2, 1, rows, elem_count), lambda f: (0, f, 0, 0))],
        out_specs=[vmem] * 2,
        compiler_params=pltpu.CompilerParams(vmem_limit_bytes=32 * MIB),
        cost_estimate=pl.CostEstimate(flops=8 * replicas.size, bytes_accessed=4 * replicas.size, transcendentals=0),
        name="prepare",
    )(replicas)
    messages = pl.pallas_call(
        functools.partial(dft_kernel, tm),
        out_shape=jax.ShapeDtypeStruct((tm, elems, width), F32),
        in_specs=[hbm, hbm],
        out_specs=vmem,
        scratch_shapes=[
            pltpu.VMEM(snapshots.shape, F32),
            pltpu.SMEM((bins,), jnp.int32),
            pltpu.VMEM((samples, 4 * bins), BF16),
            pltpu.SemaphoreType.DMA((2,)),
        ],
        compiler_params=pltpu.CompilerParams(vmem_limit_bytes=48 * MIB),
        name="dft",
    )(freq_bins, snapshots)
    held = [messages]
    for bit in bits_of(tm):
        away = jnp.concatenate([h[bit:] for h in held]) if len(held) > 1 else held[0][bit:]
        came = swap(away, "tm", tm, bit)
        held = [h[:bit] for h in held] + [came[k * bit : (k + 1) * bit] for k in range(len(held))]
    spectra = pl.pallas_call(
        functools.partial(pack_kernel, local_bins),
        out_shape=jax.ShapeDtypeStruct((1, elems, local_bins * lanes), F32),
        in_specs=[vmem] * len(held),
        out_specs=vmem,
        compiler_params=pltpu.CompilerParams(vmem_limit_bytes=4 * MIB),
        name="pack",
    )(*held)
    *early, last = bits_of(rep)
    for bit in early:
        spectra = jnp.concatenate([spectra, swap(spectra, "rep", rep, bit)])
    other = swap(spectra, "rep", rep, last)
    bits = rep.bit_length() - 1
    work = 2 * rows * elem_count * lanes * local_bins * 2
    proj = pl.pallas_call(
        functools.partial(first_kernel, snaps, bits),
        out_shape=pltpu.VMEM((local_bins, rows, 2 * lanes), F32),
        in_specs=[vmem] * 3,
        out_specs=vmem,
        compiler_params=pltpu.CompilerParams(vmem_limit_bytes=12 * MIB),
        cost_estimate=pl.CostEstimate(flops=work, bytes_accessed=2 * replicas.size, transcendentals=0),
        name="first",
    )(spectra, high, low)
    partial = pl.pallas_call(
        functools.partial(second_kernel, bins, snaps, bits),
        out_shape=jax.ShapeDtypeStruct((tm, rows // tm), F32),
        in_specs=[vmem] * 5,
        out_specs=vmem,
        scratch_shapes=[pltpu.VMEM((rows, 2 * lanes), F32)],
        compiler_params=pltpu.CompilerParams(vmem_limit_bytes=12 * MIB),
        name="second",
    )(other, spectra, proj, high, low)
    me = lax.axis_index("tm")
    result = lax.dynamic_index_in_dim(partial, me, 0, keepdims=False)
    for step in range(1, tm):
        mine = lax.dynamic_index_in_dim(partial, me ^ step, 0, keepdims=False)
        result = result + swap(mine, "tm", tm, step)
    return result


def solution(mesh):
    in_specs = (P("tm", "rep", None), P(), P(None, "tm", "rep", None))
    body = functools.partial(shards, mesh.shape["tm"], mesh.shape["rep"])
    return jax.shard_map(body, mesh=mesh, in_specs=in_specs, out_specs=P(("rep", "tm")), check_vma=False)
```

time: 156 us -> 52.2 us (0.33)
  matrix products: 74 us -> 0 us
  blocking collectives: 53.4 us -> 0 us
  Pallas kernels: 0 us -> 25.8 us
  waiting for transfers between devices: 0.3 us -> 12.9 us
  other arithmetic: 13.1 us -> 0.6 us
  starting transfers between devices: 3.47 us -> 10.7 us
  between operations: 5.94 us -> 0.09 us
  local copies, waits for them, and re-layouts: 4.76 us -> 1.93 us
    dot_general x33 -> x0, matrix products: 74 us -> none  [matmul(): jnp.dot(left, right, precision=lax.Precision.HIGHEST, preferred_element_t...]
    all_gather x1 -> x0, blocking collectives: 46.3 us -> none  [shards(): gathered = lax.all_gather(spectra, 'rep', axis=1, tiled=True)]
    pallas_call x0 -> x5, Pallas kernels: none -> 25.8 us  [the longest x1 16.5 us: shards(): pl.pallas_call(functools.partial(prepare_kernel, elems), grid=(local_bins...]
    ppermute x0 -> x8, waiting for transfers between devices: none -> 12.9 us  [swap(): return lax.ppermute(x, axis, [(i, i ^ bit) for i in range(count)])]
    reduce_sum x9 -> x0, other arithmetic: 11.7 us -> none  [the longest x1 6.6 us: shards(): norm_sq = jnp.sum(rep_re * rep_re + rep_im * rep_im, axis=1) + epsilon]
    ppermute x0 -> x8, starting transfers between devices: none -> 10.7 us  [swap(): return lax.ppermute(x, axis, [(i, i ^ bit) for i in range(count)])]
    unnamed x1 -> x0, blocking collectives: 7.1 us -> none
    all_to_all x1 -> x0, starting transfers between devices: 3.47 us -> none  [shards(): lax.all_to_all(gathered, 'tm', split_axis=3, concat_axis=0, tiled=True)]
  transfers between devices with their start and end apart: 1 -> 8, of which waited for: 1 -> 6; matrix products, arithmetic and copies ran while one was open for 5% -> 0% of each run, Pallas kernels for 0% -> 37%
where the time goes in v2:
time: 52.2 us; the launch traced here: 52.1 us
  Pallas kernels  25.8 us (49%)
  waiting for transfers between devices  12.9 us (25%)
  starting transfers between devices  10.7 us (20%)
  local copies, waits for them, and re-layouts  1.93 us (4%)
  other arithmetic  0.6 us (1%)
    pallas_call x1, Pallas kernels, shards(): pl.pallas_call(functools.partial(prepare_kernel, elems), grid=(local_bins...  16.5 us
    ppermute x8, waiting for transfers between devices, swap(): return lax.ppermute(x, axis, [(i, i ^ bit) for i in range(count)])  12.9 us
    ppermute x8, starting transfers between devices, swap(): return lax.ppermute(x, axis, [(i, i ^ bit) for i in range(count)])  10.7 us
    pallas_call x1, Pallas kernels, shards(): pl.pallas_call(functools.partial(second_kernel, bins, snaps, bits), out_s...  4.52 us
    pallas_call x1, Pallas kernels, shards(): pl.pallas_call(functools.partial(first_kernel, snaps, bits), out_shape=pl...  2.77 us
    unnamed x4, local copies, waits for them, and re-layouts  1.88 us
    pallas_call x1, Pallas kernels, shards(): pl.pallas_call(functools.partial(dft_kernel, tm), out_shape=jax.ShapeDtyp...  1.84 us
  transfers between devices with their start and end apart: 8, of which 6 were waited for; matrix products, arithmetic and copies ran while one was open for 0% of the time, Pallas kernels for 37%

profile of v2, /device:TPU:0, one launch (start us, length us, event | category | flops | bytes accessed | tf_op | source)
XLA Modules:
  0.0 52.1 jit_solution(16269370533714553989)
XLA Ops:
  0.0 0.0 copy-start
  0.0 1.2 %copy-done = f32[8,32,1024]{2,1,0:T(8,128)S(1)} copy-done((f32[8,32,1024]{2,1,0:T(8,128)S(1)}, f32[8,32,1024]{2,1,0:T(8,128)}, u32[]{:S(2)}) %copy-start) | copy-done | bytes 1048600
  1.2 0.0 copy-start.1
  1.2 0.7 %copy-done.1 = s32[32]{0:T(128)S(1)} copy-done((s32[32]{0:T(128)S(1)}, s32[32]{0:T(128)}, u32[]{:S(2)}) %copy-start.1) | copy-done | bytes 152
  1.9 1.8 %dft.1 = f32[4,32,128]{2,1,0:T(8,128)S(1)} custom-call(s32[32]{0:T(128)S(1)} %copy-done.1, f32[8,32,1024]{2,1,0:T(8,128)S(1)} %copy-done), custom_call_target="tpu_custom_call" | custom-call | tf_op jit(solution)/shard_map/dft/pallas_call | solution.py:209
  3.7 3.0 %collective-permute-start = (f32[2,32,128]{2,1,0:T(8,128)S(1)}, f32[2,32,128]{2,1,0:T(8,128)S(1)}, u32[]{:S(2)}, u32[]{:S(2)}) collective-permute-start(f32[2,32,128]{2,1,0:T(8,128)S(1)} %slice.32), channel_id=1, source_target_pairs={{0,16},{8,24},{16,0},{24,8},{1,17},{9,25},{17,1},{25,9},{2,18},{10... | collective-permute-start | bytes 98312 | tf_op jit(solution)/shard_map/ppermute | solution.py:182
  6.7 1.9 %collective-permute-done = f32[2,32,128]{2,1,0:T(8,128)S(1)} collective-permute-done((f32[2,32,128]{2,1,0:T(8,128)S(1)}, f32[2,32,128]{2,1,0:T(8,128)S(1)}, u32[]{:S(2)}, u32[]{:S(2)}) %collective-permute-start) | collective-permute-done | bytes 32800 | tf_op jit(solution)/shard_map/ppermute | solution.py:182
  8.6 0.1 collective-permute-start.1
  8.7 1.2 %collective-permute-done.1 = f32[2,32,128]{2,1,0:T(8,128)S(1)} collective-permute-done((f32[2,32,128]{2,1,0:T(8,128)S(1)}, f32[2,32,128]{2,1,0:T(8,128)S(1)}, u32[]{:S(2)}, u32[]{:S(2)}) %collective-permute-start.1) | collective-permute-done | bytes 32800 | tf_op jit(solution)/shard_map/ppermute | solution.py:182
  9.9 0.2 pack.1
  10.1 3.2 %collective-permute-start.2 = (f32[1,32,512]{2,1,0:T(8,128)S(1)}, f32[1,32,512]{2,1,0:T(8,128)S(1)}, u32[]{:S(2)}, u32[]{:S(2)}) collective-permute-start(f32[1,32,512]{2,1,0:T(8,128)S(1)} %pack.1), channel_id=1, source_target_pairs={{0,4},{1,5},{2,6},{3,7},{4,0},{5,1},{6,2},{7,3},{8,12},{9,13},{10,... | collective-permute-start | bytes 196616 | tf_op jit(solution)/shard_map/ppermute | solution.py:182
  13.3 3.8 %collective-permute-done.2 = f32[1,32,512]{2,1,0:T(8,128)S(1)} collective-permute-done((f32[1,32,512]{2,1,0:T(8,128)S(1)}, f32[1,32,512]{2,1,0:T(8,128)S(1)}, u32[]{:S(2)}, u32[]{:S(2)}) %collective-permute-start.2) | collective-permute-done | bytes 65568 | tf_op jit(solution)/shard_map/ppermute | solution.py:182
  17.1 0.8 %collective-permute-start.3 = (f32[2,32,512]{2,1,0:T(8,128)S(1)}, f32[2,32,512]{2,1,0:T(8,128)S(1)}, u32[]{:S(2)}, u32[]{:S(2)}) collective-permute-start(f32[2,32,512]{2,1,0:T(8,128)S(1)} %pad_maximum_fusion.1), channel_id=1, source_target_pairs={{0,2},{1,3},{2,0},{3,1},{4,6},{5,7},{6,4},{7,5},{8,10},{9,11},{10,... | collective-permute-start | bytes 393224 | tf_op jit(solution)/shard_map/ppermute | solution.py:182
  17.9 4.2 %collective-permute-done.3 = f32[2,32,512]{2,1,0:T(8,128)S(1)} collective-permute-done((f32[2,32,512]{2,1,0:T(8,128)S(1)}, f32[2,32,512]{2,1,0:T(8,128)S(1)}, u32[]{:S(2)}, u32[]{:S(2)}) %collective-permute-start.3) | collective-permute-done | bytes 131104 | tf_op jit(solution)/shard_map/ppermute | solution.py:182
  22.2 1.7 %collective-permute-start.4 = (f32[4,32,512]{2,1,0:T(8,128)S(1)}, f32[4,32,512]{2,1,0:T(8,128)S(1)}, u32[]{:S(2)}, u32[]{:S(2)}) collective-permute-start(f32[4,32,512]{2,1,0:T(8,128)S(1)} %pad_maximum_fusion.spec_ref.own_ref), channel_id=1, source_target_pairs={{0,1},{1,0},{2,3},{3,2},{4,5},{5,4},{6,7},{7,6},{8,9},{9,8},{10,11... | collective-permute-start | bytes 786440 | tf_op jit(solution)/shard_map/ppermute | solution.py:182
  23.9 16.5 %prepare.1 = (bf16[2,8,1024,256]{3,2,1,0:T(8,128)(2,1)S(1)}, bf16[2,8,1024,256]{3,2,1,0:T(8,128)(2,1)S(1)}) custom-call(f32[2,8,1024,256]{3,2,1,0:T(8,128)} %rep_ref.1), custom_call_target="tpu_custom_call" | custom-call | flops 33554432 | bytes 16777216 | tf_op jit(solution)/shard_map/prepare/pallas_call | solution.py:199
  40.5 2.8 %first.1.proj_ref = f32[8,1024,128]{2,1,0:T(8,128)S(1)} custom-call(f32[4,32,512]{2,1,0:T(8,128)S(1)} %pad_maximum_fusion.spec_ref.own_ref, bf16[2,8,1024,256]{3,2,1,0:T(8,128)(2,1)S(1)} %get-tuple-element.7.high_ref, bf16[2,8,1024,256]{3,2,1,0:T(8,128)(2,1)S(1)} %get-tuple-element.8.low_ref), custom_call_target="tpu_custom_call" | custom-call | flops 536870912 | bytes 8388608 | tf_op jit(solution)/shard_map/first/pallas_call | solution.py:242
  43.2 0.0 collective-permute-done.4.spec_ref
  43.2 4.5 %second.1 = f32[4,256]{1,0:T(4,128)S(1)} custom-call(f32[4,32,512]{2,1,0:T(8,128)S(1)} %collective-permute-done.4.spec_ref, f32[4,32,512]{2,1,0:T(8,128)S(1)} %pad_maximum_fusion.spec_ref.own_ref, f32[8,1024,128]{2,1,0:T(8,128)S(1)} %first.1.proj_ref, bf16[2,8,1024,256]{3,2,1,0:T(8,128)(2,1)S(1)} %get-tuple-element.7.high_ref, ...), custom_call_target="tpu_custom_call" | custom-call | tf_op jit(solution)/shard_map/second/pallas_call | solution.py:251
  47.8 0.1 collective-permute-start.7
  47.9 1.6 %collective-permute-start.6 = (f32[256]{0:T(256)S(1)}, f32[256]{0:T(256)S(1)}, u32[]{:S(2)}, u32[]{:S(2)}) collective-permute-start(f32[256]{0:T(256)S(1)} %bitcast.6), channel_id=1, source_target_pairs={{0,16},{8,24},{16,0},{24,8},{1,17},{9,25},{17,1},{25,9},{2,18},{10... | collective-permute-start | bytes 3080 | tf_op jit(solution)/shard_map/ppermute | solution.py:182
  49.4 0.3 collective-permute-start.5
  49.7 1.1 %collective-permute-done.7 = f32[256]{0:T(256)S(1)} collective-permute-done((f32[256]{0:T(256)S(1)}, f32[256]{0:T(256)S(1)}, u32[]{:S(2)}, u32[]{:S(2)}) %collective-permute-start.7) | collective-permute-done | bytes 1056 | tf_op jit(solution)/shard_map/ppermute | solution.py:182
  50.9 0.7 %collective-permute-done.6 = f32[256]{0:T(256)S(1)} collective-permute-done((f32[256]{0:T(256)S(1)}, f32[256]{0:T(256)S(1)}, u32[]{:S(2)}, u32[]{:S(2)}) %collective-permute-start.6) | collective-permute-done | bytes 1056 | tf_op jit(solution)/shard_map/ppermute | solution.py:182
  51.5 0.0 collective-permute-done.5
  51.5 0.6 %add_add_fusion = f32[256]{0:T(256)} fusion(f32[256]{0:T(256)S(1)} %collective-permute-done.7, f32[256]{0:T(256)S(1)} %collective-permute-done.6, f32[256]{0:T(256)S(1)} %bitcast.4, f32[256]{0:T(256)S(1)} %collective-permute-done.5), kind=kLoop, calls=%fused_computation.3 | loop fusion | flops 768 | bytes 5120 | tf_op jit(solution)/shard_map/add | solution.py:264
  (8 shorter events, 0.1 us)
Async XLA Ops:
  0.0 1.2 %copy-start = (f32[8,32,1024]{2,1,0:T(8,128)S(1)}, f32[8,32,1024]{2,1,0:T(8,128)}, u32[]{:S(2)}) copy-start(f32[8,32,1024]{2,1,0:T(8,128)} %snap_hbm.1) | copy-start | bytes 3145732
  1.2 0.7 %copy-start.1 = (s32[32]{0:T(128)S(1)}, s32[32]{0:T(128)}, u32[]{:S(2)}) copy-start(s32[32]{0:T(128)} %bins_hbm.1) | copy-start | bytes 388
  3.7 4.9 %collective-permute-start = (f32[2,32,128]{2,1,0:T(8,128)S(1)}, f32[2,32,128]{2,1,0:T(8,128)S(1)}, u32[]{:S(2)}, u32[]{:S(2)}) collective-permute-start(f32[2,32,128]{2,1,0:T(8,128)S(1)} %slice.32), channel_id=1, source_target_pairs={{0,16},{8,24},{16,0},{24,8},{1,17},{9,25},{17,1},{25,9},{2,18},{10... | collective-permute-start | bytes 98312 | tf_op jit(solution)/shard_map/ppermute | solution.py:182
  8.6 1.3 %collective-permute-start.1 = (f32[2,32,128]{2,1,0:T(8,128)S(1)}, f32[2,32,128]{2,1,0:T(8,128)S(1)}, u32[]{:S(2)}, u32[]{:S(2)}) collective-permute-start(f32[2,32,128]{2,1,0:T(8,128)S(1)} %pad_maximum_fusion.2), channel_id=1, source_target_pairs={{0,8},{8,0},{16,24},{24,16},{1,9},{9,1},{17,25},{25,17},{2,10},{10... | collective-permute-start | bytes 98312 | tf_op jit(solution)/shard_map/ppermute | solution.py:182
  10.1 7.0 %collective-permute-start.2 = (f32[1,32,512]{2,1,0:T(8,128)S(1)}, f32[1,32,512]{2,1,0:T(8,128)S(1)}, u32[]{:S(2)}, u32[]{:S(2)}) collective-permute-start(f32[1,32,512]{2,1,0:T(8,128)S(1)} %pack.1), channel_id=1, source_target_pairs={{0,4},{1,5},{2,6},{3,7},{4,0},{5,1},{6,2},{7,3},{8,12},{9,13},{10,... | collective-permute-start | bytes 196616 | tf_op jit(solution)/shard_map/ppermute | solution.py:182
  17.1 5.0 %collective-permute-start.3 = (f32[2,32,512]{2,1,0:T(8,128)S(1)}, f32[2,32,512]{2,1,0:T(8,128)S(1)}, u32[]{:S(2)}, u32[]{:S(2)}) collective-permute-start(f32[2,32,512]{2,1,0:T(8,128)S(1)} %pad_maximum_fusion.1), channel_id=1, source_target_pairs={{0,2},{1,3},{2,0},{3,1},{4,6},{5,7},{6,4},{7,5},{8,10},{9,11},{10,... | collective-permute-start | bytes 393224 | tf_op jit(solution)/shard_map/ppermute | solution.py:182
  22.2 21.1 %collective-permute-start.4 = (f32[4,32,512]{2,1,0:T(8,128)S(1)}, f32[4,32,512]{2,1,0:T(8,128)S(1)}, u32[]{:S(2)}, u32[]{:S(2)}) collective-permute-start(f32[4,32,512]{2,1,0:T(8,128)S(1)} %pad_maximum_fusion.spec_ref.own_ref), channel_id=1, source_target_pairs={{0,1},{1,0},{2,3},{3,2},{4,5},{5,4},{6,7},{7,6},{8,9},{9,8},{10,11... | collective-permute-start | bytes 786440 | tf_op jit(solution)/shard_map/ppermute | solution.py:182
  47.8 3.1 %collective-permute-start.7 = (f32[256]{0:T(256)S(1)}, f32[256]{0:T(256)S(1)}, u32[]{:S(2)}, u32[]{:S(2)}) collective-permute-start(f32[256]{0:T(256)S(1)} %bitcast.7), channel_id=1, source_target_pairs={{0,24},{8,16},{16,8},{24,0},{1,25},{9,17},{17,9},{25,1},{2,26},{10... | collective-permute-start | bytes 3080 | tf_op jit(solution)/shard_map/ppermute | solution.py:182
  47.9 3.6 %collective-permute-start.6 = (f32[256]{0:T(256)S(1)}, f32[256]{0:T(256)S(1)}, u32[]{:S(2)}, u32[]{:S(2)}) collective-permute-start(f32[256]{0:T(256)S(1)} %bitcast.6), channel_id=1, source_target_pairs={{0,16},{8,24},{16,0},{24,8},{1,17},{9,25},{17,1},{25,9},{2,18},{10... | collective-permute-start | bytes 3080 | tf_op jit(solution)/shard_map/ppermute | solution.py:182
  49.4 2.1 %collective-permute-start.5 = (f32[256]{0:T(256)S(1)}, f32[256]{0:T(256)S(1)}, u32[]{:S(2)}, u32[]{:S(2)}) collective-permute-start(f32[256]{0:T(256)S(1)} %bitcast.5), channel_id=1, source_target_pairs={{0,8},{8,0},{16,24},{24,16},{1,9},{9,1},{17,25},{25,17},{2,10},{10... | collective-permute-start | bytes 3080 | tf_op jit(solution)/shard_map/ppermute | solution.py:182

commit v3 on v2

v3 whole, which is shorter than its diff:
```python
import functools
import math

import jax
import jax.numpy as jnp
from jax import lax
from jax.experimental import pallas as pl
from jax.experimental.pallas import tpu as pltpu
from jax.sharding import PartitionSpec as P

EPS = 1e-06
HIGHEST = lax.Precision.HIGHEST
F32 = jnp.float32
BF16 = jnp.bfloat16
MIB = 2**20
COST = 2 * 10**10


def dot(left, right):
    return jnp.dot(left, right, preferred_element_type=F32)


def halves(x):
    high = x.astype(BF16).astype(F32)
    return high, x - high


def dft_kernel(owners, bins_hbm, snap_hbm, keep_ref, away_ref, snap_ref, bins_ref, table_ref, sems):
    snaps, elems, samples = snap_ref.shape
    bins = bins_ref.shape[0]
    load_bins = pltpu.make_async_copy(bins_hbm, bins_ref, sems.at[0])
    load_snaps = pltpu.make_async_copy(snap_hbm, snap_ref, sems.at[1])
    load_bins.start()
    load_snaps.start()
    me = lax.axis_index("tm")
    cols = 2 * bins
    group = cols // owners
    fine = 1
    while fine * fine < samples and samples % (2 * fine) == 0:
        fine *= 2
    coarse = samples // fine
    turn = 2.0 * math.pi / samples

    def angle(count, step, freq):
        steps = lax.broadcasted_iota(jnp.int32, (count, cols), 0) * step
        return (steps * freq % samples).astype(F32) * turn

    win_c, win_f = angle(coarse, fine, 1), angle(fine, 1, 1)
    wcos_c, wsin_c = jnp.cos(win_c), jnp.sin(win_c)
    wcos_f, wsin_f = jnp.cos(win_f), jnp.sin(win_f)
    lane = lax.broadcasted_iota(jnp.int32, (1, cols), 1)
    odd = lane % 2 == 1
    bin_row = jnp.zeros((1, cols), jnp.int32)
    load_bins.wait()
    for d in range(owners):
        for f in range(group // 2):
            value = bins_ref[(me ^ d) * (group // 2) + f]
            bin_row = jnp.where(lane // 2 == d * (group // 2) + f, value, bin_row)
    angle_c, angle_f = angle(coarse, fine, bin_row), angle(fine, 1, bin_row)
    cos_c, sin_c = jnp.cos(angle_c), jnp.sin(angle_c)
    cos_f, sin_f = jnp.cos(angle_f), jnp.sin(angle_f)
    left = jnp.where(odd, -sin_c, cos_c)
    right = jnp.where(odd, cos_c, sin_c)
    for a in range(coarse):
        row = slice(a, a + 1)
        window = 0.5 - 0.5 * (wcos_c[row] * wcos_f - wsin_c[row] * wsin_f)
        high, low = halves(window * (left[row] * cos_f - right[row] * sin_f))
        table_ref[a * fine : (a + 1) * fine, :] = jnp.concatenate([high, low], axis=1).astype(BF16)
    load_snaps.wait()
    high, low = halves(snap_ref[...].reshape(snaps * elems, samples))
    product = dot(high.astype(BF16), table_ref[...]) + dot(low.astype(BF16), table_ref[...])
    spectra = product[:, :cols] + product[:, cols:]

    width = snaps * group
    source = lax.broadcasted_iota(jnp.int32, (width, width), 0)
    target = lax.broadcasted_iota(jnp.int32, (width, width), 1)
    order = jnp.where(source == target % snaps * group + target // snaps, 1.0, 0.0).astype(BF16)
    messages = jnp.concatenate(
        [
            jnp.concatenate(
                [spectra[s * elems : (s + 1) * elems, d * group : (d + 1) * group] for s in range(snaps)], axis=1
            )
            for d in range(owners)
        ],
        axis=0,
    )
    high, rest = halves(messages)
    middle, low = halves(rest)
    moved = dot(high.astype(BF16), order) + dot(middle.astype(BF16), order) + dot(low.astype(BF16), order)
    moved = moved.reshape((owners,) + keep_ref.shape[1:])
    keep_ref[...] = moved[: keep_ref.shape[0]]
    away_ref[...] = moved[keep_ref.shape[0] :]


def pack_kernel(local_bins, slots, *refs):
    *blocks, out_ref = refs
    for n in range(out_ref.shape[0]):
        parts = [blocks[k][b] for k, b in slots[n]]
        group = parts[0].shape[1] // local_bins
        out_ref[n] = jnp.concatenate(
            [part[:, f * group : (f + 1) * group] for f in range(local_bins) for part in parts], axis=1
        )


def collect_kernel(after_ref, *refs):
    del after_ref
    *blocks, out_ref = refs
    for k, block in enumerate(blocks):
        out_ref[k] = block[1]


def prepare_kernel(first, elems, after_ref, rep_hbm, high_ref, low_ref, rep_ref, scale_ref, sems):
    del after_ref
    rows, elem_count = rep_ref.shape[2:]
    tile = math.gcd(rows, 256)
    step = 128 if 128 % (2 * elems) == 0 and elem_count % 128 == 0 else elem_count
    lane = lax.broadcasted_iota(jnp.int32, (tile, step), 1)
    even = lane // elems % 2 == 0
    ones = jnp.ones((elem_count, 128), BF16)
    count = high_ref.shape[1]
    loads = [
        [pltpu.make_async_copy(rep_hbm.at[part, first + i], rep_ref.at[part, i], sems.at[part, i]) for part in range(2)]
        for i in range(count)
    ]
    for pair in loads:
        for load in pair:
            load.start()
    for i in range(count):
        for load in loads[i]:
            load.wait()
        re, im = rep_ref[0, i], rep_ref[1, i]
        high, low = halves(re * re + im * im)
        norm = dot(high.astype(BF16), ones) + dot(low.astype(BF16), ones) + EPS
        scale_ref[i] = lax.rsqrt(norm)
        for k in range(rows // tile):
            at = slice(k * tile, (k + 1) * tile)
            scale = scale_ref[i, at]
            for j in range(elem_count // step):
                cut = slice(j * step, (j + 1) * step)
                wide = jnp.concatenate([scale] * (step // 128), axis=1)
                real, imag = rep_ref[0, i, at, cut] * wide, rep_ref[1, i, at, cut] * wide
                pair = (
                    jnp.where(even, real, pltpu.roll(imag, elems, 1)),
                    jnp.where(even, pltpu.roll(real, step - elems, 1), imag),
                )
                for a in range(2):
                    high = pair[a].astype(BF16)
                    high_ref[a, i, at, cut] = high
                    low_ref[a, i, at, cut] = (pair[a] - high.astype(F32)).astype(BF16)


def operand(spec_ref, f, lanes, half, side, me, bits):
    count = spec_ref.shape[0]
    blocks = []
    for p in range(count):
        apart = (2 * p + side) ^ me
        slot = 0
        for k in range(1, bits):
            slot = slot + ((apart >> k) & 1) * (1 << (bits - 1 - k))
        block = spec_ref[slot, :, f * lanes : (f + 1) * lanes]
        place = lax.broadcasted_iota(jnp.int32, block.shape, 1) % (2 * half)
        turned = jnp.where(place < half, pltpu.roll(block, lanes - half, 1), -pltpu.roll(block, half, 1))
        blocks += [block, turned]
    high, low = halves(jnp.concatenate(blocks, axis=0))
    return jnp.concatenate([high, low], axis=1).astype(BF16)


def first_kernel(half, bits, spec_ref, *refs):
    *parts, proj_ref = refs
    local_bins = proj_ref.shape[0]
    each = parts[0].shape[1]
    lanes = spec_ref.shape[2] // local_bins
    me = lax.axis_index("rep")
    side = me & 1
    for f in range(local_bins):
        right = operand(spec_ref, f, lanes, half, side, me, bits)
        high_ref, low_ref = parts[f // each * 2 : f // each * 2 + 2]
        proj_ref[f] = dot(high_ref[side, f % each], right) + dot(low_ref[side, f % each], right)


def second_kernel(elem_count, bins, half, bits, count, spec_ref, own_ref, proj_ref, *refs):
    *refs, row_ref, sum_ref = refs
    parts, outs = refs[:count], refs[count:]
    local_bins = proj_ref.shape[0]
    each = parts[0].shape[1]
    lanes = spec_ref.shape[2] // local_bins
    total_snaps = lanes // 2
    chunk = row_ref.shape[2]
    me = lax.axis_index("rep")
    side = 1 - (me & 1)
    for f in range(local_bins):
        high_ref, low_ref = parts[f // each * 2 : f // each * 2 + 2]
        right = operand(spec_ref, f, lanes, half, side, me ^ 1, bits)
        cut = slice(f * lanes, (f + 1) * lanes)
        mine, other = own_ref[:, :, cut], spec_ref[:, :, cut]
        trace = jnp.sum(mine * mine + other * other) / total_snaps + EPS
        factor = 0.5 * elem_count / (trace * total_snaps * bins)
        for k in range(row_ref.shape[0]):
            at = slice(k * chunk, (k + 1) * chunk)
            proj = proj_ref[f, at] + dot(high_ref[side, f % each, at], right)
            proj += dot(low_ref[side, f % each, at], right)
            proj += pltpu.roll(proj, lanes, 1)
            value = proj * proj * factor
            sum_ref[at] = value if f == 0 else sum_ref[at] + value
    ones = jnp.ones((8, 2 * lanes), F32)
    for k in range(row_ref.shape[0]):
        block = sum_ref[k * chunk : (k + 1) * chunk]
        row = lax.dot_general(ones, block, (((1,), (1,)), ((), ())), precision=HIGHEST, preferred_element_type=F32)
        row_ref[k] = row[0:1]
    owner = lax.axis_index("tm")
    for d, out_ref in enumerate(outs):
        out_ref[...] = row_ref[owner ^ d]


def swap(x, mesh_shape, tm_bit, rep_bit):
    tm, rep = mesh_shape
    pairs = [(t * rep + r, (t ^ tm_bit) * rep + (r ^ rep_bit)) for t in range(tm) for r in range(rep)]
    return lax.ppermute(x, ("tm", "rep"), pairs)


def bits_of(count):
    assert count & (count - 1) == 0
    return [1 << k for k in reversed(range(count.bit_length() - 1))]


def shards(tm, rep, snapshots, freq_bins, replicas):
    snaps, elems, samples = snapshots.shape
    bins = freq_bins.shape[0]
    _, local_bins, rows, elem_count = replicas.shape
    width = 2 * local_bins * snaps
    lanes = 2 * snaps * tm
    vmem = pl.BlockSpec(memory_space=pltpu.VMEM)
    hbm = pl.BlockSpec(memory_space=pltpu.HBM)
    shape = (tm // 2, elems, width)
    keep, away = pl.pallas_call(
        functools.partial(dft_kernel, tm),
        out_shape=(pltpu.VMEM(shape, F32), pltpu.VMEM(shape, F32)),
        in_specs=[hbm, hbm],
        out_specs=[vmem] * 2,
        scratch_shapes=[
            pltpu.VMEM(snapshots.shape, F32),
            pltpu.SMEM((bins,), jnp.int32),
            pltpu.VMEM((samples, 4 * bins), BF16),
            pltpu.SemaphoreType.DMA((2,)),
        ],
        compiler_params=pltpu.CompilerParams(vmem_limit_bytes=60 * MIB),
        name="dft",
    )(freq_bins, snapshots)
    each = -(-local_bins // 2)

    def prepare(k, after):
        shape = (2, each, rows, elem_count)
        return pl.pallas_call(
            functools.partial(prepare_kernel, k * each, elems),
            out_shape=(pltpu.VMEM(shape, BF16), pltpu.VMEM(shape, BF16)),
            in_specs=[hbm, hbm],
            out_specs=[vmem] * 2,
            scratch_shapes=[
                pltpu.VMEM(shape, F32),
                pltpu.VMEM((each, rows, 128), F32),
                pltpu.SemaphoreType.DMA((2, each)),
            ],
            compiler_params=pltpu.CompilerParams(vmem_limit_bytes=36 * MIB),
            cost_estimate=pl.CostEstimate(flops=COST, bytes_accessed=0, transcendentals=0),
            name="prepare",
        )(after, replicas)

    send = functools.partial(swap, mesh_shape=(tm, rep))
    held = [(keep, away)]
    parts = prepare(0, keep)
    for bit in bits_of(tm)[:-2]:
        came = [send(b, tm_bit=bit, rep_bit=0) for _, b in held]
        kept = [a for a, _ in held] + came
        held = [(k[: bit // 2], k[bit // 2 :]) for k in kept]
    top, *middle = bits_of(rep)[:-2]
    near = [a for a, _ in held] + [send(b, tm_bit=2, rep_bit=0) for _, b in held]
    far = [send(a, tm_bit=0, rep_bit=top) for a, _ in held] + [send(b, tm_bit=2, rep_bit=top) for _, b in held]
    count = len(near)
    crossing = pl.pallas_call(
        collect_kernel,
        out_shape=pltpu.VMEM((2 * count, elems, width), F32),
        in_specs=[pl.BlockSpec(memory_space=pl.ANY)] + [vmem] * (2 * count),
        out_specs=vmem,
        compiler_params=pltpu.CompilerParams(vmem_limit_bytes=4 * MIB),
        name="collect",
    )(parts[1], *near, *far)
    came = send(crossing, tm_bit=1, rep_bit=0)
    slots = [[(n * count + k, 0) for k in range(count)] + [(2 * count, n * count + k) for k in range(count)] for n in range(2)]
    spectra = pl.pallas_call(
        functools.partial(pack_kernel, local_bins, slots),
        out_shape=pltpu.VMEM((2, elems, local_bins * lanes), F32),
        in_specs=[vmem] * (2 * count + 1),
        out_specs=vmem,
        compiler_params=pltpu.CompilerParams(vmem_limit_bytes=4 * MIB),
        name="pack",
    )(*near, *far, came)
    if each < local_bins:
        parts += prepare(1, spectra)
    for bit in middle:
        spectra = jnp.concatenate([spectra, send(spectra, tm_bit=0, rep_bit=bit)])
    own = jnp.concatenate([spectra, send(spectra, tm_bit=0, rep_bit=2)])
    other = jnp.concatenate([send(spectra, tm_bit=0, rep_bit=1), send(spectra, tm_bit=0, rep_bit=3)])
    bits = rep.bit_length() - 1
    proj = pl.pallas_call(
        functools.partial(first_kernel, snaps, bits),
        out_shape=pltpu.VMEM((local_bins, rows, 2 * lanes), F32),
        in_specs=[vmem] * (1 + len(parts)),
        out_specs=vmem,
        compiler_params=pltpu.CompilerParams(vmem_limit_bytes=6 * MIB),
        cost_estimate=pl.CostEstimate(flops=COST, bytes_accessed=0, transcendentals=0),
        name="first",
    )(own, *parts)
    chunk = rows // tm
    shares = pl.pallas_call(
        functools.partial(second_kernel, elem_count, bins, snaps, bits, len(parts)),
        out_shape=[pltpu.VMEM((1, chunk), F32)] * tm,
        in_specs=[vmem] * (3 + len(parts)),
        out_specs=[vmem] * tm,
        scratch_shapes=[pltpu.VMEM((tm, 1, chunk), F32), pltpu.VMEM((rows, 2 * lanes), F32)],
        compiler_params=pltpu.CompilerParams(vmem_limit_bytes=6 * MIB),
        name="second",
    )(other, own, proj, *parts)
    result = shares[0]
    for step in range(1, tm):
        result = result + send(shares[step], tm_bit=step, rep_bit=0)
    return result.reshape(chunk)


def solution(mesh):
    in_specs = (P("tm", "rep", None), P(), P(None, "tm", "rep", None))
    body = functools.partial(shards, mesh.shape["tm"], mesh.shape["rep"])
    return jax.shard_map(body, mesh=mesh, in_specs=in_specs, out_specs=P(("rep", "tm")), check_vma=False)
```

time: 52.2 us -> 36.6 us (0.70)
  waiting for transfers between devices: 12.9 us -> 4.17 us
  Pallas kernels: 25.8 us -> 20.3 us
  local copies, waits for them, and re-layouts: 1.93 us -> 0 us
    ppermute x8 -> x10, waiting for transfers between devices: 12.9 us -> 4.17 us  [swap(): return lax.ppermute(x, ('tm', 'rep'), pairs)]
    pallas_call x4 -> x6, Pallas kernels: 23.1 us -> 17.5 us  [the longest x2 10.5 us: prepare(): pl.pallas_call(functools.partial(prepare_kernel, k * each, elems), out_sh...]
    unnamed x4 -> x0, local copies, waits for them, and re-layouts: 1.88 us -> none
    ppermute x8 -> x10, starting transfers between devices: 10.7 us -> 11.2 us  [swap(): return lax.ppermute(x, ('tm', 'rep'), pairs)]
  transfers between devices with their start and end apart: 8 -> 10, of which waited for: 6 -> 3; matrix products, arithmetic and copies ran while one was open for 0% -> 0% of each run, Pallas kernels for 37% -> 36%
where the time goes in v3:
time: 36.6 us; the launch traced here: 36.4 us
  Pallas kernels  20.3 us (55%)
  starting transfers between devices  11.2 us (31%)
  waiting for transfers between devices  4.17 us (11%)
  other arithmetic  0.61 us (2%)
    ppermute x10, starting transfers between devices, swap(): return lax.ppermute(x, ('tm', 'rep'), pairs)  11.2 us
    pallas_call x2, Pallas kernels, prepare(): pl.pallas_call(functools.partial(prepare_kernel, k * each, elems), out_sh...  10.5 us
    pallas_call x1, Pallas kernels, shards(): pl.pallas_call(functools.partial(second_kernel, elem_count, bins, snaps,...  4.69 us
    ppermute x10, waiting for transfers between devices, swap(): return lax.ppermute(x, ('tm', 'rep'), pairs)  4.17 us
    pallas_call x1, Pallas kernels, shards(): pl.pallas_call(functools.partial(first_kernel, snaps, bits), out_shape=pl...  2.78 us
    pallas_call x1, Pallas kernels, shards(): pl.pallas_call(functools.partial(dft_kernel, tm), out_shape=(pltpu.VMEM(s...  2.05 us
  transfers between devices with their start and end apart: 10, of which 3 were waited for; matrix products, arithmetic and copies ran while one was open for 0% of the time, Pallas kernels for 36%

profile of v3, /device:TPU:0, one launch (start us, length us, event | category | flops | bytes accessed | tf_op | source)
XLA Modules:
  0.0 36.4 jit_solution(12882377570495980381)
XLA Ops:
  0.0 2.1 %dft.1 = (f32[2,32,128]{2,1,0:T(8,128)S(1)}, f32[2,32,128]{2,1,0:T(8,128)S(1)}) custom-call(s32[32]{0:T(128)} %bins_hbm.1, f32[8,32,1024]{2,1,0:T(8,128)} %snap_hbm.1), custom_call_target="tpu_custom_call" | custom-call | tf_op jit(solution)/shard_map/dft/pallas_call | solution.py:235
  2.1 5.0 %collective-permute-start.2 = (f32[2,32,128]{2,1,0:T(8,128)S(1)}, f32[2,32,128]{2,1,0:T(8,128)S(1)}, u32[]{:S(2)}, u32[]{:S(2)}) collective-permute-start(f32[2,32,128]{2,1,0:T(8,128)S(1)} %get-tuple-element.16), channel_id=1, source_target_pairs={{0,20},{1,21},{2,22},{3,23},{4,16},{5,17},{6,18},{7,19},{8,28},{9,... | collective-permute-start | bytes 98312 | tf_op jit(solution)/shard_map/ppermute | solution.py:218
  7.1 0.5 %collective-permute-start = (f32[2,32,128]{2,1,0:T(8,128)S(1)}, f32[2,32,128]{2,1,0:T(8,128)S(1)}, u32[]{:S(2)}, u32[]{:S(2)}) collective-permute-start(f32[2,32,128]{2,1,0:T(8,128)S(1)} %get-tuple-element.16), channel_id=1, source_target_pairs={{0,16},{1,17},{2,18},{3,19},{4,20},{5,21},{6,22},{7,23},{8,24},{9,... | collective-permute-start | bytes 98312 | tf_op jit(solution)/shard_map/ppermute | solution.py:218
  7.6 0.1 collective-permute-start.1
  7.7 5.2 %prepare.2 = (bf16[2,4,1024,256]{3,2,1,0:T(8,128)(2,1)S(1)}, bf16[2,4,1024,256]{3,2,1,0:T(8,128)(2,1)S(1)}) custom-call(f32[2,32,128]{2,1,0:T(8,128)S(1)} %get-tuple-element.15.after_ref.refs_0_, f32[2,8,1024,256]{3,2,1,0:T(8,128)} %rep_hbm.3), custom_call_target="tpu_custom_call" | custom-call | flops 20000000000 | tf_op jit(solution)/shard_map/prepare/pallas_call | solution.py:253
  13.0 0.0 collective-permute-done.2.refs_3_
  13.0 0.0 collective-permute-done.refs_1_
  13.0 0.0 collective-permute-done.1.refs_2_
  13.0 0.1 collective-permute-start.3
  13.1 1.2 %collective-permute-done.3.refs_4_ = f32[4,32,128]{2,1,0:T(8,128)S(1)} collective-permute-done((f32[4,32,128]{2,1,0:T(8,128)S(1)}, f32[4,32,128]{2,1,0:T(8,128)S(1)}, u32[]{:S(2)}, u32[]{:S(2)}) %collective-permute-start.3) | collective-permute-done | bytes 65568 | tf_op jit(solution)/shard_map/ppermute | solution.py:218
  14.3 0.3 pack.1.after_ref
  14.6 1.9 %collective-permute-start.6 = (f32[2,32,512]{2,1,0:T(8,128)S(1)}, f32[2,32,512]{2,1,0:T(8,128)S(1)}, u32[]{:S(2)}, u32[]{:S(2)}) collective-permute-start(f32[2,32,512]{2,1,0:T(8,128)S(1)} %pack.1.after_ref), channel_id=1, source_target_pairs={{0,2},{1,3},{2,0},{3,1},{4,6},{5,7},{6,4},{7,5},{8,10},{9,11},{10,... | collective-permute-start | bytes 393224 | tf_op jit(solution)/shard_map/ppermute | solution.py:218
  16.5 1.4 %collective-permute-start.5 = (f32[2,32,512]{2,1,0:T(8,128)S(1)}, f32[2,32,512]{2,1,0:T(8,128)S(1)}, u32[]{:S(2)}, u32[]{:S(2)}) collective-permute-start(f32[2,32,512]{2,1,0:T(8,128)S(1)} %pack.1.after_ref), channel_id=1, source_target_pairs={{0,3},{1,2},{2,1},{3,0},{4,7},{5,6},{6,5},{7,4},{8,11},{9,10},{10,... | collective-permute-start | bytes 393224 | tf_op jit(solution)/shard_map/ppermute | solution.py:218
  17.9 0.3 collective-permute-start.4
  18.2 5.2 %prepare.3 = (bf16[2,4,1024,256]{3,2,1,0:T(8,128)(2,1)S(1)}, bf16[2,4,1024,256]{3,2,1,0:T(8,128)(2,1)S(1)}) custom-call(f32[2,32,512]{2,1,0:T(8,128)S(1)} %pack.1.after_ref, f32[2,8,1024,256]{3,2,1,0:T(8,128)} %rep_hbm.3), custom_call_target="tpu_custom_call" | custom-call | flops 20000000000 | tf_op jit(solution)/shard_map/prepare/pallas_call | solution.py:253
  23.4 0.0 collective-permute-done.6
  23.5 2.8 %first.1.proj_ref = f32[8,1024,128]{2,1,0:T(8,128)S(1)} custom-call(f32[4,32,512]{2,1,0:T(8,128)S(1)} %pad_maximum_fusion.1.spec_ref.own_ref, bf16[2,4,1024,256]{3,2,1,0:T(8,128)(2,1)S(1)} %get-tuple-element.18.refs_0_, bf16[2,4,1024,256]{3,2,1,0:T(8,128)(2,1)S(1)} %get-tuple-element.17.after_ref.refs_1_, ...), custom_call_target="tpu_custom_call" | custom-call | flops 20000000000 | tf_op jit(solution)/shard_map/first/pallas_call | solution.py:304
  26.3 0.0 collective-permute-done.5
  26.3 0.0 collective-permute-done.4
  26.3 4.7 %second.1 = (f32[1,256]{1,0:T(1,128)S(1)}, f32[1,256]{1,0:T(1,128)S(1)}, f32[1,256]{1,0:T(1,128)S(1)}, f32[1,256]{1,0:T(1,128)S(1)}) custom-call(f32[4,32,512]{2,1,0:T(8,128)S(1)} %pad_maximum_fusion.spec_ref, f32[4,32,512]{2,1,0:T(8,128)S(1)} %pad_maximum_fusion.1.spec_ref.own_ref, f32[8,1024,128]{2,1,0:T(8,128)S(1)} %first.1.proj_ref, ...), custom_call_target="tpu_custom_call" | custom-call | tf_op jit(solution)/shard_map/second/pallas_call | solution.py:314
  31.0 0.1 collective-permute-start.7
  31.1 1.8 %collective-permute-start.8 = (f32[1,256]{1,0:T(1,128)S(1)}, f32[1,256]{1,0:T(1,128)S(1)}, u32[]{:S(2)}, u32[]{:S(2)}) collective-permute-start(f32[1,256]{1,0:T(1,128)S(1)} %get-tuple-element.23), channel_id=1, source_target_pairs={{0,16},{1,17},{2,18},{3,19},{4,20},{5,21},{6,22},{7,23},{8,24},{9,... | collective-permute-start | bytes 3080 | tf_op jit(solution)/shard_map/ppermute | solution.py:218
  32.9 0.1 collective-permute-start.9
  32.9 0.0 collective-permute-done.7
  32.9 1.8 %collective-permute-done.8 = f32[1,256]{1,0:T(1,128)S(1)} collective-permute-done((f32[1,256]{1,0:T(1,128)S(1)}, f32[1,256]{1,0:T(1,128)S(1)}, u32[]{:S(2)}, u32[]{:S(2)}) %collective-permute-start.8) | collective-permute-done | bytes 1056 | tf_op jit(solution)/shard_map/ppermute | solution.py:218
  34.7 1.2 %collective-permute-done.9 = f32[1,256]{1,0:T(1,128)S(1)} collective-permute-done((f32[1,256]{1,0:T(1,128)S(1)}, f32[1,256]{1,0:T(1,128)S(1)}, u32[]{:S(2)}, u32[]{:S(2)}) %collective-permute-start.9) | collective-permute-done | bytes 1056 | tf_op jit(solution)/shard_map/ppermute | solution.py:218
  35.9 0.6 %add_add_fusion = f32[1,256]{1,0:T(1,128)} fusion(f32[1,256]{1,0:T(1,128)S(1)} %collective-permute-done.9, f32[1,256]{1,0:T(1,128)S(1)} %collective-permute-done.8, f32[1,256]{1,0:T(1,128)S(1)} %get-tuple-element.21, f32[1,256]{1,0:T(1,128)S(1)} %collective-permute-done.7), kind=kLoop, calls=%fused_computation.2 | loop fusion | flops 768 | bytes 5120 | tf_op jit(solution)/shard_map/add | solution.py:325
  (3 shorter events, 0.0 us)
Async XLA Ops:
  2.1 10.9 %collective-permute-start.2 = (f32[2,32,128]{2,1,0:T(8,128)S(1)}, f32[2,32,128]{2,1,0:T(8,128)S(1)}, u32[]{:S(2)}, u32[]{:S(2)}) collective-permute-start(f32[2,32,128]{2,1,0:T(8,128)S(1)} %get-tuple-element.16), channel_id=1, source_target_pairs={{0,20},{1,21},{2,22},{3,23},{4,16},{5,17},{6,18},{7,19},{8,28},{9,... | collective-permute-start | bytes 98312 | tf_op jit(solution)/shard_map/ppermute | solution.py:218
  7.1 5.9 %collective-permute-start = (f32[2,32,128]{2,1,0:T(8,128)S(1)}, f32[2,32,128]{2,1,0:T(8,128)S(1)}, u32[]{:S(2)}, u32[]{:S(2)}) collective-permute-start(f32[2,32,128]{2,1,0:T(8,128)S(1)} %get-tuple-element.16), channel_id=1, source_target_pairs={{0,16},{1,17},{2,18},{3,19},{4,20},{5,21},{6,22},{7,23},{8,24},{9,... | collective-permute-start | bytes 98312 | tf_op jit(solution)/shard_map/ppermute | solution.py:218
  7.6 5.4 %collective-permute-start.1 = (f32[2,32,128]{2,1,0:T(8,128)S(1)}, f32[2,32,128]{2,1,0:T(8,128)S(1)}, u32[]{:S(2)}, u32[]{:S(2)}) collective-permute-start(f32[2,32,128]{2,1,0:T(8,128)S(1)} %get-tuple-element.15.after_ref.refs_0_), channel_id=1, source_target_pairs={{0,4},{1,5},{2,6},{3,7},{4,0},{5,1},{6,2},{7,3},{8,12},{9,13},{10,... | collective-permute-start | bytes 98312 | tf_op jit(solution)/shard_map/ppermute | solution.py:218
  13.0 1.3 %collective-permute-start.3 = (f32[4,32,128]{2,1,0:T(8,128)S(1)}, f32[4,32,128]{2,1,0:T(8,128)S(1)}, u32[]{:S(2)}, u32[]{:S(2)}) collective-permute-start(f32[4,32,128]{2,1,0:T(8,128)S(1)} %collect.1), channel_id=1, source_target_pairs={{0,8},{1,9},{2,10},{3,11},{4,12},{5,13},{6,14},{7,15},{8,0},{9,1},... | collective-permute-start | bytes 196616 | tf_op jit(solution)/shard_map/ppermute | solution.py:218
  14.6 8.8 %collective-permute-start.6 = (f32[2,32,512]{2,1,0:T(8,128)S(1)}, f32[2,32,512]{2,1,0:T(8,128)S(1)}, u32[]{:S(2)}, u32[]{:S(2)}) collective-permute-start(f32[2,32,512]{2,1,0:T(8,128)S(1)} %pack.1.after_ref), channel_id=1, source_target_pairs={{0,2},{1,3},{2,0},{3,1},{4,6},{5,7},{6,4},{7,5},{8,10},{9,11},{10,... | collective-permute-start | bytes 393224 | tf_op jit(solution)/shard_map/ppermute | solution.py:218
  16.5 9.8 %collective-permute-start.5 = (f32[2,32,512]{2,1,0:T(8,128)S(1)}, f32[2,32,512]{2,1,0:T(8,128)S(1)}, u32[]{:S(2)}, u32[]{:S(2)}) collective-permute-start(f32[2,32,512]{2,1,0:T(8,128)S(1)} %pack.1.after_ref), channel_id=1, source_target_pairs={{0,3},{1,2},{2,1},{3,0},{4,7},{5,6},{6,5},{7,4},{8,11},{9,10},{10,... | collective-permute-start | bytes 393224 | tf_op jit(solution)/shard_map/ppermute | solution.py:218
  17.9 8.3 %collective-permute-start.4 = (f32[2,32,512]{2,1,0:T(8,128)S(1)}, f32[2,32,512]{2,1,0:T(8,128)S(1)}, u32[]{:S(2)}, u32[]{:S(2)}) collective-permute-start(f32[2,32,512]{2,1,0:T(8,128)S(1)} %pack.1.after_ref), channel_id=1, source_target_pairs={{0,1},{1,0},{2,3},{3,2},{4,5},{5,4},{6,7},{7,6},{8,9},{9,8},{10,11... | collective-permute-start | bytes 393224 | tf_op jit(solution)/shard_map/ppermute | solution.py:218
  31.0 1.9 %collective-permute-start.7 = (f32[1,256]{1,0:T(1,128)S(1)}, f32[1,256]{1,0:T(1,128)S(1)}, u32[]{:S(2)}, u32[]{:S(2)}) collective-permute-start(f32[1,256]{1,0:T(1,128)S(1)} %get-tuple-element.22), channel_id=1, source_target_pairs={{0,8},{1,9},{2,10},{3,11},{4,12},{5,13},{6,14},{7,15},{8,0},{9,1},... | collective-permute-start | bytes 3080 | tf_op jit(solution)/shard_map/ppermute | solution.py:218
  31.1 3.6 %collective-permute-start.8 = (f32[1,256]{1,0:T(1,128)S(1)}, f32[1,256]{1,0:T(1,128)S(1)}, u32[]{:S(2)}, u32[]{:S(2)}) collective-permute-start(f32[1,256]{1,0:T(1,128)S(1)} %get-tuple-element.23), channel_id=1, source_target_pairs={{0,16},{1,17},{2,18},{3,19},{4,20},{5,21},{6,22},{7,23},{8,24},{9,... | collective-permute-start | bytes 3080 | tf_op jit(solution)/shard_map/ppermute | solution.py:218
  32.9 3.0 %collective-permute-start.9 = (f32[1,256]{1,0:T(1,128)S(1)}, f32[1,256]{1,0:T(1,128)S(1)}, u32[]{:S(2)}, u32[]{:S(2)}) collective-permute-start(f32[1,256]{1,0:T(1,128)S(1)} %get-tuple-element.24), channel_id=1, source_target_pairs={{0,24},{1,25},{2,26},{3,27},{4,28},{5,29},{6,30},{7,31},{8,16},{9,... | collective-permute-start | bytes 3080 | tf_op jit(solution)/shard_map/ppermute | solution.py:218

commit v4 on v3

--- a/solution.py
+++ b/solution.py
@@ -9,7 +9,6 @@
 from jax.sharding import PartitionSpec as P
 
 EPS = 1e-06
-HIGHEST = lax.Precision.HIGHEST
 F32 = jnp.float32
 BF16 = jnp.bfloat16
 MIB = 2**20
@@ -109,36 +108,36 @@
         out_ref[k] = block[1]
 
 
-def prepare_kernel(first, elems, after_ref, rep_hbm, high_ref, low_ref, rep_ref, scale_ref, sems):
+def prepare_kernel(first, elems, after_ref, rep_hbm, high_ref, low_ref, inverse_ref, rep_ref, sems):
     del after_ref
     rows, elem_count = rep_ref.shape[2:]
-    tile = math.gcd(rows, 256)
+    pieces = sems.shape[2]
+    tile = rows // pieces
     step = 128 if 128 % (2 * elems) == 0 and elem_count % 128 == 0 else elem_count
     lane = lax.broadcasted_iota(jnp.int32, (tile, step), 1)
     even = lane // elems % 2 == 0
-    ones = jnp.ones((elem_count, 128), BF16)
-    count = high_ref.shape[1]
-    loads = [
-        [pltpu.make_async_copy(rep_hbm.at[part, first + i], rep_ref.at[part, i], sems.at[part, i]) for part in range(2)]
-        for i in range(count)
-    ]
-    for pair in loads:
-        for load in pair:
-            load.start()
-    for i in range(count):
-        for load in loads[i]:
-            load.wait()
-        re, im = rep_ref[0, i], rep_ref[1, i]
-        high, low = halves(re * re + im * im)
-        norm = dot(high.astype(BF16), ones) + dot(low.astype(BF16), ones) + EPS
-        scale_ref[i] = lax.rsqrt(norm)
-        for k in range(rows // tile):
+    ones = jnp.ones((elem_count, inverse_ref.shape[2]), BF16)
+    bins = range(high_ref.shape[1])
+
+    def load(part, i, k):
+        at = slice(k * tile, (k + 1) * tile)
+        return pltpu.make_async_copy(rep_hbm.at[part, first + i, at], rep_ref.at[part, i, at], sems.at[part, i, k])
+
+    for i in bins:
+        for k in range(pieces):
+            for part in range(2):
+                load(part, i, k).start()
+    for i in bins:
+        for k in range(pieces):
+            for part in range(2):
+                load(part, i, k).wait()
             at = slice(k * tile, (k + 1) * tile)
-            scale = scale_ref[i, at]
+            re, im = rep_ref[0, i, at], rep_ref[1, i, at]
+            high, low = halves(re * re + im * im)
+            inverse_ref[i, at] = 1.0 / (dot(high.astype(BF16), ones) + dot(low.astype(BF16), ones) + EPS)
             for j in range(elem_count // step):
                 cut = slice(j * step, (j + 1) * step)
-                wide = jnp.concatenate([scale] * (step // 128), axis=1)
-                real, imag = rep_ref[0, i, at, cut] * wide, rep_ref[1, i, at, cut] * wide
+                real, imag = rep_ref[0, i, at, cut], rep_ref[1, i, at, cut]
                 pair = (
                     jnp.where(even, real, pltpu.roll(imag, elems, 1)),
                     jnp.where(even, pltpu.roll(real, step - elems, 1), imag),
@@ -149,67 +148,89 @@
                     low_ref[a, i, at, cut] = (pair[a] - high.astype(F32)).astype(BF16)
 
 
-def operand(spec_ref, f, lanes, half, side, me, bits):
+def operands(spec_ref, local_bins, half, side, me, bits):
     count = spec_ref.shape[0]
-    blocks = []
+    lanes = spec_ref.shape[2] // local_bins
+    paired = 2 * lanes == 128 and local_bins % 2 == 0
+    span = 2 * lanes if paired else lanes
+    slots = []
     for p in range(count):
         apart = (2 * p + side) ^ me
-        slot = 0
-        for k in range(1, bits):
-            slot = slot + ((apart >> k) & 1) * (1 << (bits - 1 - k))
-        block = spec_ref[slot, :, f * lanes : (f + 1) * lanes]
-        place = lax.broadcasted_iota(jnp.int32, block.shape, 1) % (2 * half)
-        turned = jnp.where(place < half, pltpu.roll(block, lanes - half, 1), -pltpu.roll(block, half, 1))
-        blocks += [block, turned]
-    high, low = halves(jnp.concatenate(blocks, axis=0))
-    return jnp.concatenate([high, low], axis=1).astype(BF16)
+        slots.append(sum(((apart >> k) & 1) * (1 << (bits - 1 - k)) for k in range(1, bits)))
+    result = []
+    for q in range(spec_ref.shape[2] // span):
+        blocks = []
+        for slot in slots:
+            block = spec_ref[slot, :, q * span : (q + 1) * span]
+            place = lax.broadcasted_iota(jnp.int32, block.shape, 1) % (2 * half)
+            turned = jnp.where(place < half, pltpu.roll(block, span - half, 1), -pltpu.roll(block, half, 1))
+            blocks += [block, turned]
+        high, low = halves(jnp.concatenate(blocks, axis=0))
+        if paired:
+            near = lax.broadcasted_iota(jnp.int32, high.shape, 1) < lanes
+            result.append(jnp.where(near, high, pltpu.roll(low, lanes, 1)).astype(BF16))
+            result.append(jnp.where(near, pltpu.roll(high, lanes, 1), low).astype(BF16))
+        else:
+            result.append(jnp.concatenate([high, low], axis=1).astype(BF16))
+    return result
 
 
 def first_kernel(half, bits, spec_ref, *refs):
     *parts, proj_ref = refs
-    local_bins = proj_ref.shape[0]
     each = parts[0].shape[1]
-    lanes = spec_ref.shape[2] // local_bins
     me = lax.axis_index("rep")
     side = me & 1
-    for f in range(local_bins):
-        right = operand(spec_ref, f, lanes, half, side, me, bits)
+    for f, right in enumerate(operands(spec_ref, proj_ref.shape[0], half, side, me, bits)):
         high_ref, low_ref = parts[f // each * 2 : f // each * 2 + 2]
         proj_ref[f] = dot(high_ref[side, f % each], right) + dot(low_ref[side, f % each], right)
 
 
+def rows_power(own_half, proj_ref, rights, factors, parts, inverses, out_ref, row_ref, sum_ref):
+    count, chunk = row_ref.shape[0], row_ref.shape[2]
+    each = parts[0].shape[1]
+    lanes = proj_ref.shape[2] // 2
+    side = 1 - (lax.axis_index("rep") & 1)
+    owner = lax.axis_index("tm")
+    top = owner // count if own_half else 1 - owner // count
+    at = pl.ds(pl.multiple_of(top * count * chunk, count * chunk), count * chunk)
+    for f in range(proj_ref.shape[0]):
+        high_ref, low_ref = parts[f // each * 2 : f // each * 2 + 2]
+        proj = proj_ref[f, at] + dot(high_ref[side, f % each, at], rights[f])
+        proj += dot(low_ref[side, f % each, at], rights[f])
+        proj += pltpu.roll(proj, lanes, 1)
+        value = proj * proj * (inverses[f // each][f % each, at] * factors[f])
+        sum_ref[...] = value if f == 0 else sum_ref[...] + value
+    for k in range(count):
+        row_ref[k] = jnp.sum(sum_ref[k * chunk : (k + 1) * chunk].T, axis=0, keepdims=True)
+    for d in range(count):
+        out_ref[d : d + 1] = row_ref[(owner ^ d) % count]
+
+
 def second_kernel(elem_count, bins, half, bits, count, spec_ref, own_ref, proj_ref, *refs):
-    *refs, row_ref, sum_ref = refs
-    parts, outs = refs[:count], refs[count:]
+    parts, inverses = refs[: 2 * count], refs[2 * count : 3 * count]
+    out_ref, right_ref, factor_ref, row_ref, sum_ref = refs[3 * count :]
     local_bins = proj_ref.shape[0]
-    each = parts[0].shape[1]
-    lanes = spec_ref.shape[2] // local_bins
+    lanes = proj_ref.shape[2] // 2
     total_snaps = lanes // 2
-    chunk = row_ref.shape[2]
     me = lax.axis_index("rep")
-    side = 1 - (me & 1)
+    rights = operands(spec_ref, local_bins, half, 1 - (me & 1), me ^ 1, bits)
+    squares = 0.0
+    for n in range(own_ref.shape[0]):
+        mine, other = own_ref[n], spec_ref[n]
+        squares = squares + (mine * mine + other * other)
+    squares = jnp.sum(squares, axis=0, keepdims=True)
+    factors = []
     for f in range(local_bins):
-        high_ref, low_ref = parts[f // each * 2 : f // each * 2 + 2]
-        right = operand(spec_ref, f, lanes, half, side, me ^ 1, bits)
-        cut = slice(f * lanes, (f + 1) * lanes)
-        mine, other = own_ref[:, :, cut], spec_ref[:, :, cut]
-        trace = jnp.sum(mine * mine + other * other) / total_snaps + EPS
-        factor = 0.5 * elem_count / (trace * total_snaps * bins)
-        for k in range(row_ref.shape[0]):
-            at = slice(k * chunk, (k + 1) * chunk)
-            proj = proj_ref[f, at] + dot(high_ref[side, f % each, at], right)
-            proj += dot(low_ref[side, f % each, at], right)
-            proj += pltpu.roll(proj, lanes, 1)
-            value = proj * proj * factor
-            sum_ref[at] = value if f == 0 else sum_ref[at] + value
-    ones = jnp.ones((8, 2 * lanes), F32)
-    for k in range(row_ref.shape[0]):
-        block = sum_ref[k * chunk : (k + 1) * chunk]
-        row = lax.dot_general(ones, block, (((1,), (1,)), ((), ())), precision=HIGHEST, preferred_element_type=F32)
-        row_ref[k] = row[0:1]
-    owner = lax.axis_index("tm")
-    for d, out_ref in enumerate(outs):
-        out_ref[...] = row_ref[owner ^ d]
+        trace = jnp.sum(squares[:, f * lanes : (f + 1) * lanes], axis=1, keepdims=True) / total_snaps + EPS
+        factors.append(jnp.broadcast_to(0.5 * elem_count / (trace * total_snaps * bins), factor_ref.shape[1:]))
+        factor_ref[f] = factors[f]
+        right_ref[f] = rights[f]
+    rows_power(False, proj_ref, rights, factors, parts, inverses, out_ref, row_ref, sum_ref)
+
+
+def third_kernel(count, right_ref, factor_ref, proj_ref, *refs):
+    parts, inverses, (out_ref, row_ref, sum_ref) = refs[: 2 * count], refs[2 * count : 3 * count], refs[3 * count :]
+    rows_power(True, proj_ref, right_ref, factor_ref, parts, inverses, out_ref, row_ref, sum_ref)
 
 
 def swap(x, mesh_shape, tm_bit, rep_bit):
@@ -252,22 +273,22 @@
         shape = (2, each, rows, elem_count)
         return pl.pallas_call(
             functools.partial(prepare_kernel, k * each, elems),
-            out_shape=(pltpu.VMEM(shape, BF16), pltpu.VMEM(shape, BF16)),
-            in_specs=[hbm, hbm],
-            out_specs=[vmem] * 2,
+            out_shape=[pltpu.VMEM(shape, BF16), pltpu.VMEM(shape, BF16), pltpu.VMEM((each, rows, 2 * lanes), F32)],
+            in_specs=[pl.BlockSpec(memory_space=pl.ANY), hbm],
+            out_specs=[vmem] * 3,
             scratch_shapes=[
                 pltpu.VMEM(shape, F32),
-                pltpu.VMEM((each, rows, 128), F32),
-                pltpu.SemaphoreType.DMA((2, each)),
+                pltpu.SemaphoreType.DMA((2, each, rows // math.gcd(rows, 512))),
             ],
-            compiler_params=pltpu.CompilerParams(vmem_limit_bytes=36 * MIB),
+            compiler_params=pltpu.CompilerParams(vmem_limit_bytes=34 * MIB),
             cost_estimate=pl.CostEstimate(flops=COST, bytes_accessed=0, transcendentals=0),
             name="prepare",
         )(after, replicas)
 
     send = functools.partial(swap, mesh_shape=(tm, rep))
     held = [(keep, away)]
-    parts = prepare(0, keep)
+    *parts, inverse = prepare(0, keep)
+    inverses = [inverse]
     for bit in bits_of(tm)[:-2]:
         came = [send(b, tm_bit=bit, rep_bit=0) for _, b in held]
         kept = [a for a, _ in held] + came
@@ -295,7 +316,9 @@
         name="pack",
     )(*near, *far, came)
     if each < local_bins:
-        parts += prepare(1, spectra)
+        *more, inverse = prepare(1, spectra)
+        parts += more
+        inverses.append(inverse)
     for bit in middle:
         spectra = jnp.concatenate([spectra, send(spectra, tm_bit=0, rep_bit=bit)])
     own = jnp.concatenate([spectra, send(spectra, tm_bit=0, rep_bit=2)])
@@ -311,19 +334,36 @@
         name="first",
     )(own, *parts)
     chunk = rows // tm
-    shares = pl.pallas_call(
-        functools.partial(second_kernel, elem_count, bins, snaps, bits, len(parts)),
-        out_shape=[pltpu.VMEM((1, chunk), F32)] * tm,
-        in_specs=[vmem] * (3 + len(parts)),
-        out_specs=[vmem] * tm,
-        scratch_shapes=[pltpu.VMEM((tm, 1, chunk), F32), pltpu.VMEM((rows, 2 * lanes), F32)],
+    count = tm // 2
+    share = pltpu.VMEM((count, chunk), F32)
+    sums = [pltpu.VMEM((count, 1, chunk), F32), pltpu.VMEM((rows // 2, 2 * lanes), F32)]
+    there, rights, factors = pl.pallas_call(
+        functools.partial(second_kernel, elem_count, bins, snaps, bits, len(inverses)),
+        out_shape=[
+            share,
+            pltpu.VMEM((local_bins, elem_count, 2 * lanes), BF16),
+            pltpu.VMEM((local_bins, 1, 2 * lanes), F32),
+        ],
+        in_specs=[vmem] * (3 + len(parts) + len(inverses)),
+        out_specs=[vmem] * 3,
+        scratch_shapes=sums,
         compiler_params=pltpu.CompilerParams(vmem_limit_bytes=6 * MIB),
         name="second",
-    )(other, own, proj, *parts)
-    result = shares[0]
-    for step in range(1, tm):
-        result = result + send(shares[step], tm_bit=step, rep_bit=0)
-    return result.reshape(chunk)
+    )(other, own, proj, *parts, *inverses)
+    here = pl.pallas_call(
+        functools.partial(third_kernel, len(inverses)),
+        out_shape=share,
+        in_specs=[vmem] * (3 + len(parts) + len(inverses)),
+        out_specs=vmem,
+        scratch_shapes=sums,
+        compiler_params=pltpu.CompilerParams(vmem_limit_bytes=6 * MIB),
+        cost_estimate=pl.CostEstimate(flops=COST, bytes_accessed=0, transcendentals=0),
+        name="third",
+    )(rights, factors, proj, *parts, *inverses)
+    total = here + send(there, tm_bit=count, rep_bit=0)
+    for bit in bits_of(tm)[1:]:
+        total = total[:bit] + send(total[bit:], tm_bit=bit, rep_bit=0)
+    return total.reshape(chunk)
 
 
 def solution(mesh):

time: 36.6 us -> 32.5 us (0.89)
  Pallas kernels: 20.3 us -> 17.4 us
  waiting for transfers between devices: 4.17 us -> 3.36 us
  starting transfers between devices: 11.2 us -> 10.8 us
    pallas_call x1, Pallas kernels: 4.69 us -> 1.83 us  [shards(): pl.pallas_call(functools.partial(second_kernel, elem_count, bins, snaps,...]
    pallas_call x0 -> x1, Pallas kernels: none -> 1.56 us  [shards(): pl.pallas_call(functools.partial(third_kernel, len(inverses)), out_shape=...]
    pallas_call x2, Pallas kernels: 10.5 us -> 9.21 us  [prepare(): pl.pallas_call(functools.partial(prepare_kernel, k * each, elems), out_sh...]
    ppermute x10 -> x9, waiting for transfers between devices: 4.17 us -> 3.36 us  [swap(): return lax.ppermute(x, ('tm', 'rep'), pairs)]
    ppermute x10 -> x9, starting transfers between devices: 11.2 us -> 10.8 us  [swap(): return lax.ppermute(x, ('tm', 'rep'), pairs)]
  transfers between devices with their start and end apart: 10 -> 9, of which waited for: 3 -> 5; matrix products, arithmetic and copies ran while one was open for 0% -> 0% of each run, Pallas kernels for 36% -> 41%
where the time goes in v4:
time: 32.5 us; the launch traced here: 32.3 us
  Pallas kernels  17.4 us (54%)
  starting transfers between devices  10.8 us (33%)
  waiting for transfers between devices  3.36 us (10%)
  other arithmetic  0.61 us (2%)
    ppermute x9, starting transfers between devices, swap(): return lax.ppermute(x, ('tm', 'rep'), pairs)  10.8 us
    pallas_call x2, Pallas kernels, prepare(): pl.pallas_call(functools.partial(prepare_kernel, k * each, elems), out_sh...  9.21 us
    ppermute x9, waiting for transfers between devices, swap(): return lax.ppermute(x, ('tm', 'rep'), pairs)  3.36 us
    pallas_call x1, Pallas kernels, shards(): pl.pallas_call(functools.partial(first_kernel, snaps, bits), out_shape=pl...  2.49 us
    pallas_call x1, Pallas kernels, shards(): pl.pallas_call(functools.partial(dft_kernel, tm), out_shape=(pltpu.VMEM(s...  2.05 us
    pallas_call x1, Pallas kernels, shards(): pl.pallas_call(functools.partial(second_kernel, elem_count, bins, snaps,...  1.83 us
    pallas_call x1, Pallas kernels, shards(): pl.pallas_call(functools.partial(third_kernel, len(inverses)), out_shape=...  1.56 us
  transfers between devices with their start and end apart: 9, of which 5 were waited for; matrix products, arithmetic and copies ran while one was open for 0% of the time, Pallas kernels for 41%

profile of v4, /device:TPU:0, one launch (start us, length us, event | category | flops | bytes accessed | tf_op | source)
XLA Modules:
  0.0 32.3 jit_solution(16949290971047360801)
XLA Ops:
  0.0 2.0 %dft.1 = (f32[2,32,128]{2,1,0:T(8,128)S(1)}, f32[2,32,128]{2,1,0:T(8,128)S(1)}) custom-call(s32[32]{0:T(128)} %bins_hbm.1, f32[8,32,1024]{2,1,0:T(8,128)} %snap_hbm.1), custom_call_target="tpu_custom_call" | custom-call | tf_op jit(solution)/shard_map/dft/pallas_call | solution.py:256
  2.1 5.0 %collective-permute-start.2 = (f32[2,32,128]{2,1,0:T(8,128)S(1)}, f32[2,32,128]{2,1,0:T(8,128)S(1)}, u32[]{:S(2)}, u32[]{:S(2)}) collective-permute-start(f32[2,32,128]{2,1,0:T(8,128)S(1)} %get-tuple-element.17), channel_id=1, source_target_pairs={{0,20},{1,21},{2,22},{3,23},{4,16},{5,17},{6,18},{7,19},{8,28},{9,... | collective-permute-start | bytes 98312 | tf_op jit(solution)/shard_map/ppermute | solution.py:239
  7.1 0.5 %collective-permute-start = (f32[2,32,128]{2,1,0:T(8,128)S(1)}, f32[2,32,128]{2,1,0:T(8,128)S(1)}, u32[]{:S(2)}, u32[]{:S(2)}) collective-permute-start(f32[2,32,128]{2,1,0:T(8,128)S(1)} %get-tuple-element.17), channel_id=1, source_target_pairs={{0,16},{1,17},{2,18},{3,19},{4,20},{5,21},{6,22},{7,23},{8,24},{9,... | collective-permute-start | bytes 98312 | tf_op jit(solution)/shard_map/ppermute | solution.py:239
  7.6 0.1 collective-permute-start.1
  7.7 4.6 %prepare.2 = (bf16[2,4,1024,256]{3,2,1,0:T(8,128)(2,1)S(1)}, bf16[2,4,1024,256]{3,2,1,0:T(8,128)(2,1)S(1)}, f32[4,1024,128]{2,1,0:T(8,128)S(1)}) custom-call(f32[2,32,128]{2,1,0:T(8,128)S(1)} %get-tuple-element.16.after_ref.refs_0_, f32[2,8,1024,256]{3,2,1,0:T(8,128)} %rep_hbm.3), custom_call_target="tpu_custom_call" | custom-call | flops 20000000000 | tf_op jit(solution)/shard_map/prepare/pallas_call | solution.py:274
  12.3 0.0 collective-permute-done.2.refs_3_
  12.4 0.0 collective-permute-done.refs_1_
  12.4 0.1 collective-permute-done.1.refs_2_
  12.4 0.0 collective-permute-start.3
  12.5 1.2 %collective-permute-done.3.refs_4_ = f32[4,32,128]{2,1,0:T(8,128)S(1)} collective-permute-done((f32[4,32,128]{2,1,0:T(8,128)S(1)}, f32[4,32,128]{2,1,0:T(8,128)S(1)}, u32[]{:S(2)}, u32[]{:S(2)}) %collective-permute-start.3) | collective-permute-done | bytes 65568 | tf_op jit(solution)/shard_map/ppermute | solution.py:239
  13.7 0.3 pack.1.after_ref
  14.0 1.9 %collective-permute-start.6 = (f32[2,32,512]{2,1,0:T(8,128)S(1)}, f32[2,32,512]{2,1,0:T(8,128)S(1)}, u32[]{:S(2)}, u32[]{:S(2)}) collective-permute-start(f32[2,32,512]{2,1,0:T(8,128)S(1)} %pack.1.after_ref), channel_id=1, source_target_pairs={{0,2},{1,3},{2,0},{3,1},{4,6},{5,7},{6,4},{7,5},{8,10},{9,11},{10,... | collective-permute-start | bytes 393224 | tf_op jit(solution)/shard_map/ppermute | solution.py:239
  15.9 1.4 %collective-permute-start.5 = (f32[2,32,512]{2,1,0:T(8,128)S(1)}, f32[2,32,512]{2,1,0:T(8,128)S(1)}, u32[]{:S(2)}, u32[]{:S(2)}) collective-permute-start(f32[2,32,512]{2,1,0:T(8,128)S(1)} %pack.1.after_ref), channel_id=1, source_target_pairs={{0,3},{1,2},{2,1},{3,0},{4,7},{5,6},{6,5},{7,4},{8,11},{9,10},{10,... | collective-permute-start | bytes 393224 | tf_op jit(solution)/shard_map/ppermute | solution.py:239
  17.3 0.3 collective-permute-start.4
  17.6 4.6 %prepare.3 = (bf16[2,4,1024,256]{3,2,1,0:T(8,128)(2,1)S(1)}, bf16[2,4,1024,256]{3,2,1,0:T(8,128)(2,1)S(1)}, f32[4,1024,128]{2,1,0:T(8,128)S(1)}) custom-call(f32[2,32,512]{2,1,0:T(8,128)S(1)} %pack.1.after_ref, f32[2,8,1024,256]{3,2,1,0:T(8,128)} %rep_hbm.3), custom_call_target="tpu_custom_call" | custom-call | flops 20000000000 | tf_op jit(solution)/shard_map/prepare/pallas_call | solution.py:274
  22.2 0.0 collective-permute-done.6
  22.2 2.5 %first.1.proj_ref = f32[8,1024,128]{2,1,0:T(8,128)S(1)} custom-call(f32[4,32,512]{2,1,0:T(8,128)S(1)} %pad_maximum_fusion.1.spec_ref.own_ref, bf16[2,4,1024,256]{3,2,1,0:T(8,128)(2,1)S(1)} %get-tuple-element.19.refs_0_, bf16[2,4,1024,256]{3,2,1,0:T(8,128)(2,1)S(1)} %get-tuple-element.18.after_ref.refs_1_, ...), custom_call_target="tpu_custom_call" | custom-call | flops 20000000000 | tf_op jit(solution)/shard_map/first/pallas_call | solution.py:327
  24.7 0.0 collective-permute-done.5
  24.7 0.4 %collective-permute-done.4 = f32[2,32,512]{2,1,0:T(8,128)S(1)} collective-permute-done((f32[2,32,512]{2,1,0:T(8,128)S(1)}, f32[2,32,512]{2,1,0:T(8,128)S(1)}, u32[]{:S(2)}, u32[]{:S(2)}) %collective-permute-start.4) | collective-permute-done | bytes 131104 | tf_op jit(solution)/shard_map/ppermute | solution.py:239
  25.1 1.8 %second.1 = (f32[2,256]{1,0:T(2,128)S(1)}, bf16[8,256,128]{2,1,0:T(8,128)(2,1)S(1)}, f32[8,1,128]{2,1,0:T(1,128)S(1)}) custom-call(f32[4,32,512]{2,1,0:T(8,128)S(1)} %pad_maximum_fusion.spec_ref, f32[4,32,512]{2,1,0:T(8,128)S(1)} %pad_maximum_fusion.1.spec_ref.own_ref, f32[8,1024,128]{2,1,0:T(8,128)S(1)} %first.1.proj_ref, ...), custom_call_target="tpu_custom_call" | custom-call | tf_op jit(solution)/shard_map/second/pallas_call | solution.py:340
  26.9 1.6 %collective-permute-start.7 = (f32[2,256]{1,0:T(2,128)S(1)}, f32[2,256]{1,0:T(2,128)S(1)}, u32[]{:S(2)}, u32[]{:S(2)}) collective-permute-start(f32[2,256]{1,0:T(2,128)S(1)} %get-tuple-element.26), channel_id=1, source_target_pairs={{0,16},{1,17},{2,18},{3,19},{4,20},{5,21},{6,22},{7,23},{8,24},{9,... | collective-permute-start | bytes 6152 | tf_op jit(solution)/shard_map/ppermute | solution.py:239
  28.5 1.6 %third.1 = f32[2,256]{1,0:T(2,128)S(1)} custom-call(bf16[8,256,128]{2,1,0:T(8,128)(2,1)S(1)} %get-tuple-element.24.right_ref, f32[8,1,128]{2,1,0:T(1,128)S(1)} %get-tuple-element.25.factor_ref, f32[8,1024,128]{2,1,0:T(8,128)S(1)} %first.1.proj_ref, bf16[2,4,1024,256]{3,2,1,0:T(8,128)(2,1)S(1)} %get-tuple-element.19.refs_0_, ...), custom_call_target="tpu_custom_call" | custom-call | flops 20000000000 | tf_op jit(solution)/shard_map/third/pallas_call | solution.py:353
  30.1 0.5 %collective-permute-done.7 = f32[2,256]{1,0:T(2,128)S(1)} collective-permute-done((f32[2,256]{1,0:T(2,128)S(1)}, f32[2,256]{1,0:T(2,128)S(1)}, u32[]{:S(2)}, u32[]{:S(2)}) %collective-permute-start.7) | collective-permute-done | bytes 2080 | tf_op jit(solution)/shard_map/ppermute | solution.py:239
  30.6 0.0 collective-permute-start.8
  30.6 1.1 %collective-permute-done.8 = f32[1,256]{1,0:T(1,128)S(1)} collective-permute-done((f32[1,256]{1,0:T(1,128)S(1)}, f32[1,256]{1,0:T(1,128)S(1)}, u32[]{:S(2)}, u32[]{:S(2)}) %collective-permute-start.8) | collective-permute-done | bytes 1056 | tf_op jit(solution)/shard_map/ppermute | solution.py:239
  31.7 0.6 %slice_add_fusion = f32[1,256]{1,0:T(1,128)} fusion(f32[1,256]{1,0:T(1,128)S(1)} %collective-permute-done.8, f32[2,256]{1,0:T(2,128)S(1)} %add.6), kind=kLoop, calls=%fused_computation.2 | loop fusion | flops 256 | bytes 3072 | tf_op jit(solution)/shard_map/add | solution.py:365
  (5 shorter events, 0.1 us)
Async XLA Ops:
  2.1 10.3 %collective-permute-start.2 = (f32[2,32,128]{2,1,0:T(8,128)S(1)}, f32[2,32,128]{2,1,0:T(8,128)S(1)}, u32[]{:S(2)}, u32[]{:S(2)}) collective-permute-start(f32[2,32,128]{2,1,0:T(8,128)S(1)} %get-tuple-element.17), channel_id=1, source_target_pairs={{0,20},{1,21},{2,22},{3,23},{4,16},{5,17},{6,18},{7,19},{8,28},{9,... | collective-permute-start | bytes 98312 | tf_op jit(solution)/shard_map/ppermute | solution.py:239
  7.1 5.3 %collective-permute-start = (f32[2,32,128]{2,1,0:T(8,128)S(1)}, f32[2,32,128]{2,1,0:T(8,128)S(1)}, u32[]{:S(2)}, u32[]{:S(2)}) collective-permute-start(f32[2,32,128]{2,1,0:T(8,128)S(1)} %get-tuple-element.17), channel_id=1, source_target_pairs={{0,16},{1,17},{2,18},{3,19},{4,20},{5,21},{6,22},{7,23},{8,24},{9,... | collective-permute-start | bytes 98312 | tf_op jit(solution)/shard_map/ppermute | solution.py:239
  7.6 4.8 %collective-permute-start.1 = (f32[2,32,128]{2,1,0:T(8,128)S(1)}, f32[2,32,128]{2,1,0:T(8,128)S(1)}, u32[]{:S(2)}, u32[]{:S(2)}) collective-permute-start(f32[2,32,128]{2,1,0:T(8,128)S(1)} %get-tuple-element.16.after_ref.refs_0_), channel_id=1, source_target_pairs={{0,4},{1,5},{2,6},{3,7},{4,0},{5,1},{6,2},{7,3},{8,12},{9,13},{10,... | collective-permute-start | bytes 98312 | tf_op jit(solution)/shard_map/ppermute | solution.py:239
  12.4 1.3 %collective-permute-start.3 = (f32[4,32,128]{2,1,0:T(8,128)S(1)}, f32[4,32,128]{2,1,0:T(8,128)S(1)}, u32[]{:S(2)}, u32[]{:S(2)}) collective-permute-start(f32[4,32,128]{2,1,0:T(8,128)S(1)} %collect.1), channel_id=1, source_target_pairs={{0,8},{1,9},{2,10},{3,11},{4,12},{5,13},{6,14},{7,15},{8,0},{9,1},... | collective-permute-start | bytes 196616 | tf_op jit(solution)/shard_map/ppermute | solution.py:239
  14.0 8.2 %collective-permute-start.6 = (f32[2,32,512]{2,1,0:T(8,128)S(1)}, f32[2,32,512]{2,1,0:T(8,128)S(1)}, u32[]{:S(2)}, u32[]{:S(2)}) collective-permute-start(f32[2,32,512]{2,1,0:T(8,128)S(1)} %pack.1.after_ref), channel_id=1, source_target_pairs={{0,2},{1,3},{2,0},{3,1},{4,6},{5,7},{6,4},{7,5},{8,10},{9,11},{10,... | collective-permute-start | bytes 393224 | tf_op jit(solution)/shard_map/ppermute | solution.py:239
  15.9 8.8 %collective-permute-start.5 = (f32[2,32,512]{2,1,0:T(8,128)S(1)}, f32[2,32,512]{2,1,0:T(8,128)S(1)}, u32[]{:S(2)}, u32[]{:S(2)}) collective-permute-start(f32[2,32,512]{2,1,0:T(8,128)S(1)} %pack.1.after_ref), channel_id=1, source_target_pairs={{0,3},{1,2},{2,1},{3,0},{4,7},{5,6},{6,5},{7,4},{8,11},{9,10},{10,... | collective-permute-start | bytes 393224 | tf_op jit(solution)/shard_map/ppermute | solution.py:239
  17.3 7.8 %collective-permute-start.4 = (f32[2,32,512]{2,1,0:T(8,128)S(1)}, f32[2,32,512]{2,1,0:T(8,128)S(1)}, u32[]{:S(2)}, u32[]{:S(2)}) collective-permute-start(f32[2,32,512]{2,1,0:T(8,128)S(1)} %pack.1.after_ref), channel_id=1, source_target_pairs={{0,1},{1,0},{2,3},{3,2},{4,5},{5,4},{6,7},{7,6},{8,9},{9,8},{10,11... | collective-permute-start | bytes 393224 | tf_op jit(solution)/shard_map/ppermute | solution.py:239
  26.9 3.6 %collective-permute-start.7 = (f32[2,256]{1,0:T(2,128)S(1)}, f32[2,256]{1,0:T(2,128)S(1)}, u32[]{:S(2)}, u32[]{:S(2)}) collective-permute-start(f32[2,256]{1,0:T(2,128)S(1)} %get-tuple-element.26), channel_id=1, source_target_pairs={{0,16},{1,17},{2,18},{3,19},{4,20},{5,21},{6,22},{7,23},{8,24},{9,... | collective-permute-start | bytes 6152 | tf_op jit(solution)/shard_map/ppermute | solution.py:239
  30.6 1.1 %collective-permute-start.8 = (f32[1,256]{1,0:T(1,128)S(1)}, f32[1,256]{1,0:T(1,128)S(1)}, u32[]{:S(2)}, u32[]{:S(2)}) collective-permute-start(f32[1,256]{1,0:T(1,128)S(1)} %slice.9), channel_id=1, source_target_pairs={{0,8},{1,9},{2,10},{3,11},{4,12},{5,13},{6,14},{7,15},{8,0},{9,1},... | collective-permute-start | bytes 3080 | tf_op jit(solution)/shard_map/ppermute | solution.py:239

commit v5 on v4

--- a/solution.py
+++ b/solution.py
@@ -108,44 +108,58 @@
         out_ref[k] = block[1]
 
 
-def prepare_kernel(first, elems, after_ref, rep_hbm, high_ref, low_ref, inverse_ref, rep_ref, sems):
+def split_rows(elems, rep_ref, i, at, high_ref, low_ref, inverse_ref, out):
+    elem_count = rep_ref.shape[3]
+    step = 128 if 128 % (2 * elems) == 0 and elem_count % 128 == 0 else elem_count
+    ones = jnp.ones((elem_count, inverse_ref.shape[2]), BF16)
+    re, im = rep_ref[0, i, at], rep_ref[1, i, at]
+    high, low = halves(re * re + im * im)
+    inverse_ref[out, at] = 1.0 / (dot(high.astype(BF16), ones) + dot(low.astype(BF16), ones) + EPS)
+    even = lax.broadcasted_iota(jnp.int32, (re.shape[0], step), 1) // elems % 2 == 0
+    for j in range(elem_count // step):
+        cut = slice(j * step, (j + 1) * step)
+        real, imag = rep_ref[0, i, at, cut], rep_ref[1, i, at, cut]
+        pair = (
+            jnp.where(even, real, pltpu.roll(imag, elems, 1)),
+            jnp.where(even, pltpu.roll(real, step - elems, 1), imag),
+        )
+        for a in range(2):
+            high = pair[a].astype(BF16)
+            high_ref[a, out, at, cut] = high
+            low_ref[a, out, at, cut] = (pair[a] - high.astype(F32)).astype(BF16)
+
+
+def prepare_kernel(first, elems, after_ref, rep_hbm, high_ref, low_ref, inverse_ref, *refs):
     del after_ref
-    rows, elem_count = rep_ref.shape[2:]
+    *spare, rep_ref, sems = refs
+    rows = rep_ref.shape[2]
     pieces = sems.shape[2]
     tile = rows // pieces
-    step = 128 if 128 % (2 * elems) == 0 and elem_count % 128 == 0 else elem_count
-    lane = lax.broadcasted_iota(jnp.int32, (tile, step), 1)
-    even = lane // elems % 2 == 0
-    ones = jnp.ones((elem_count, inverse_ref.shape[2]), BF16)
-    bins = range(high_ref.shape[1])
+    count = rep_ref.shape[1]
 
     def load(part, i, k):
         at = slice(k * tile, (k + 1) * tile)
-        return pltpu.make_async_copy(rep_hbm.at[part, first + i, at], rep_ref.at[part, i, at], sems.at[part, i, k])
-
-    for i in bins:
-        for k in range(pieces):
-            for part in range(2):
-                load(part, i, k).start()
-    for i in bins:
-        for k in range(pieces):
-            for part in range(2):
-                load(part, i, k).wait()
-            at = slice(k * tile, (k + 1) * tile)
-            re, im = rep_ref[0, i, at], rep_ref[1, i, at]
-            high, low = halves(re * re + im * im)
-            inverse_ref[i, at] = 1.0 / (dot(high.astype(BF16), ones) + dot(low.astype(BF16), ones) + EPS)
-            for j in range(elem_count // step):
-                cut = slice(j * step, (j + 1) * step)
-                real, imag = rep_ref[0, i, at, cut], rep_ref[1, i, at, cut]
-                pair = (
-                    jnp.where(even, real, pltpu.roll(imag, elems, 1)),
-                    jnp.where(even, pltpu.roll(real, step - elems, 1), imag),
-                )
-                for a in range(2):
-                    high = pair[a].astype(BF16)
-                    high_ref[a, i, at, cut] = high
-                    low_ref[a, i, at, cut] = (pair[a] - high.astype(F32)).astype(BF16)
+        target = rep_ref.at[part, i, at] if i < count else spare[0].at[part, i - count, at]
+        return pltpu.make_async_copy(rep_hbm.at[part, first + i, at], target, sems.at[part, i, k])
+
+    todo = [(i, k) for i in range(sems.shape[1]) for k in range(pieces)]
+    for i, k in todo:
+        for part in range(2):
+            load(part, i, k).start()
+    for i, k in todo:
+        for part in range(2):
+            load(part, i, k).wait()
+        if i < count:
+            split_rows(elems, rep_ref, i, slice(k * tile, (k + 1) * tile), high_ref, low_ref, inverse_ref, i)
+
+
+def finish_kernel(elems, after_ref, rep_ref, high_ref, low_ref, inverse_ref):
+    del after_ref
+    rows = rep_ref.shape[2]
+    tile = math.gcd(rows, 512)
+    for i in range(rep_ref.shape[1]):
+        for k in range(rows // tile):
+            split_rows(elems, rep_ref, i, slice(k * tile, (k + 1) * tile), high_ref, low_ref, inverse_ref, i)
 
 
 def operands(spec_ref, local_bins, half, side, me, bits):
@@ -175,30 +189,35 @@
     return result
 
 
-def first_kernel(half, bits, spec_ref, *refs):
-    *parts, proj_ref = refs
-    each = parts[0].shape[1]
+def prepared(refs, axis):
+    return [(ref, i) for ref in refs for i in range(ref.shape[axis])]
+
+
+def first_kernel(half, bits, count, spec_ref, *refs):
+    highs, lows, (proj_ref,) = prepared(refs[:count], 1), prepared(refs[count : 2 * count], 1), refs[2 * count :]
     me = lax.axis_index("rep")
     side = me & 1
     for f, right in enumerate(operands(spec_ref, proj_ref.shape[0], half, side, me, bits)):
-        high_ref, low_ref = parts[f // each * 2 : f // each * 2 + 2]
-        proj_ref[f] = dot(high_ref[side, f % each], right) + dot(low_ref[side, f % each], right)
-
-
-def rows_power(own_half, proj_ref, rights, factors, parts, inverses, out_ref, row_ref, sum_ref):
+        (high_ref, i), (low_ref, _) = highs[f], lows[f]
+        proj_ref[f] = dot(high_ref[side, i], right) + dot(low_ref[side, i], right)
+
+
+def rows_power(own_half, proj_ref, rights, factors, pieces, out_ref, row_ref, sum_ref):
     count, chunk = row_ref.shape[0], row_ref.shape[2]
-    each = parts[0].shape[1]
+    third = len(pieces) // 3
+    highs, lows = prepared(pieces[:third], 1), prepared(pieces[third : 2 * third], 1)
+    inverses = prepared(pieces[2 * third :], 0)
     lanes = proj_ref.shape[2] // 2
     side = 1 - (lax.axis_index("rep") & 1)
     owner = lax.axis_index("tm")
     top = owner // count if own_half else 1 - owner // count
     at = pl.ds(pl.multiple_of(top * count * chunk, count * chunk), count * chunk)
     for f in range(proj_ref.shape[0]):
-        high_ref, low_ref = parts[f // each * 2 : f // each * 2 + 2]
-        proj = proj_ref[f, at] + dot(high_ref[side, f % each, at], rights[f])
-        proj += dot(low_ref[side, f % each, at], rights[f])
+        (high_ref, i), (low_ref, _), (inverse_ref, _) = highs[f], lows[f], inverses[f]
+        proj = proj_ref[f, at] + dot(high_ref[side, i, at], rights[f])
+        proj += dot(low_ref[side, i, at], rights[f])
         proj += pltpu.roll(proj, lanes, 1)
-        value = proj * proj * (inverses[f // each][f % each, at] * factors[f])
+        value = proj * proj * (inverse_ref[i, at] * factors[f])
         sum_ref[...] = value if f == 0 else sum_ref[...] + value
     for k in range(count):
         row_ref[k] = jnp.sum(sum_ref[k * chunk : (k + 1) * chunk].T, axis=0, keepdims=True)
@@ -207,13 +226,13 @@
 
 
 def second_kernel(elem_count, bins, half, bits, count, spec_ref, own_ref, proj_ref, *refs):
-    parts, inverses = refs[: 2 * count], refs[2 * count : 3 * count]
+    pieces = refs[: 3 * count]
     out_ref, right_ref, factor_ref, row_ref, sum_ref = refs[3 * count :]
     local_bins = proj_ref.shape[0]
     lanes = proj_ref.shape[2] // 2
     total_snaps = lanes // 2
     me = lax.axis_index("rep")
-    rights = operands(spec_ref, local_bins, half, 1 - (me & 1), me ^ 1, bits)
+    rights = operands(spec_ref, local_bins, half, 1 - (me & 1), me ^ 3, bits)
     squares = 0.0
     for n in range(own_ref.shape[0]):
         mine, other = own_ref[n], spec_ref[n]
@@ -225,12 +244,12 @@
         factors.append(jnp.broadcast_to(0.5 * elem_count / (trace * total_snaps * bins), factor_ref.shape[1:]))
         factor_ref[f] = factors[f]
         right_ref[f] = rights[f]
-    rows_power(False, proj_ref, rights, factors, parts, inverses, out_ref, row_ref, sum_ref)
+    rows_power(False, proj_ref, rights, factors, pieces, out_ref, row_ref, sum_ref)
 
 
 def third_kernel(count, right_ref, factor_ref, proj_ref, *refs):
-    parts, inverses, (out_ref, row_ref, sum_ref) = refs[: 2 * count], refs[2 * count : 3 * count], refs[3 * count :]
-    rows_power(True, proj_ref, right_ref, factor_ref, parts, inverses, out_ref, row_ref, sum_ref)
+    pieces, (out_ref, row_ref, sum_ref) = refs[: 3 * count], refs[3 * count :]
+    rows_power(True, proj_ref, right_ref, factor_ref, pieces, out_ref, row_ref, sum_ref)
 
 
 def swap(x, mesh_shape, tm_bit, rep_bit):
@@ -267,28 +286,57 @@
         compiler_params=pltpu.CompilerParams(vmem_limit_bytes=60 * MIB),
         name="dft",
     )(freq_bins, snapshots)
-    each = -(-local_bins // 2)
-
-    def prepare(k, after):
-        shape = (2, each, rows, elem_count)
-        return pl.pallas_call(
-            functools.partial(prepare_kernel, k * each, elems),
-            out_shape=[pltpu.VMEM(shape, BF16), pltpu.VMEM(shape, BF16), pltpu.VMEM((each, rows, 2 * lanes), F32)],
-            in_specs=[pl.BlockSpec(memory_space=pl.ANY), hbm],
-            out_specs=[vmem] * 3,
-            scratch_shapes=[
-                pltpu.VMEM(shape, F32),
-                pltpu.SemaphoreType.DMA((2, each, rows // math.gcd(rows, 512))),
-            ],
-            compiler_params=pltpu.CompilerParams(vmem_limit_bytes=34 * MIB),
-            cost_estimate=pl.CostEstimate(flops=COST, bytes_accessed=0, transcendentals=0),
-            name="prepare",
-        )(after, replicas)
+    highs, lows, inverses = [], [], []
+    anywhere = pl.BlockSpec(memory_space=pl.ANY)
+    cost = pl.CostEstimate(flops=COST, bytes_accessed=0, transcendentals=0)
+    early = -(-local_bins // 2)
+    between = min(local_bins - early, -(-local_bins // 8))
+    late = local_bins - early - between
+
+    def results(count):
+        shape = (2, count, rows, elem_count)
+        return [pltpu.VMEM(shape, BF16), pltpu.VMEM(shape, BF16), pltpu.VMEM((count, rows, 2 * lanes), F32)]
+
+    def add(high, low, inverse, *spare):
+        highs.append(high)
+        lows.append(low)
+        inverses.append(inverse)
+        return spare
+
+    def prepare(count, more, limit, after):
+        first = sum(part.shape[1] for part in highs)
+        return add(
+            *pl.pallas_call(
+                functools.partial(prepare_kernel, first, elems),
+                out_shape=results(count) + [pltpu.VMEM((2, more, rows, elem_count), F32)] * (more > 0),
+                in_specs=[anywhere, hbm],
+                out_specs=[vmem] * (3 + (more > 0)),
+                scratch_shapes=[
+                    pltpu.VMEM((2, count, rows, elem_count), F32),
+                    pltpu.SemaphoreType.DMA((2, count + more, rows // math.gcd(rows, 512))),
+                ],
+                compiler_params=pltpu.CompilerParams(vmem_limit_bytes=limit * MIB),
+                cost_estimate=cost,
+                name="prepare",
+            )(after, replicas)
+        )
+
+    def finish(spare, after):
+        add(
+            *pl.pallas_call(
+                functools.partial(finish_kernel, elems),
+                out_shape=results(spare.shape[1]),
+                in_specs=[anywhere, vmem],
+                out_specs=[vmem] * 3,
+                compiler_params=pltpu.CompilerParams(vmem_limit_bytes=4 * MIB),
+                cost_estimate=cost,
+                name="finish",
+            )(after, spare)
+        )
 
     send = functools.partial(swap, mesh_shape=(tm, rep))
     held = [(keep, away)]
-    *parts, inverse = prepare(0, keep)
-    inverses = [inverse]
+    spare = prepare(early, between, 38, keep)
     for bit in bits_of(tm)[:-2]:
         came = [send(b, tm_bit=bit, rep_bit=0) for _, b in held]
         kept = [a for a, _ in held] + came
@@ -304,7 +352,9 @@
         out_specs=vmem,
         compiler_params=pltpu.CompilerParams(vmem_limit_bytes=4 * MIB),
         name="collect",
-    )(parts[1], *near, *far)
+    )(lows[0], *near, *far)
+    if spare:
+        finish(spare[0], crossing)
     came = send(crossing, tm_bit=1, rep_bit=0)
     slots = [[(n * count + k, 0) for k in range(count)] + [(2 * count, n * count + k) for k in range(count)] for n in range(2)]
     spectra = pl.pallas_call(
@@ -315,24 +365,22 @@
         compiler_params=pltpu.CompilerParams(vmem_limit_bytes=4 * MIB),
         name="pack",
     )(*near, *far, came)
-    if each < local_bins:
-        *more, inverse = prepare(1, spectra)
-        parts += more
-        inverses.append(inverse)
+    if late:
+        prepare(late, 0, 34, spectra)
     for bit in middle:
         spectra = jnp.concatenate([spectra, send(spectra, tm_bit=0, rep_bit=bit)])
     own = jnp.concatenate([spectra, send(spectra, tm_bit=0, rep_bit=2)])
-    other = jnp.concatenate([send(spectra, tm_bit=0, rep_bit=1), send(spectra, tm_bit=0, rep_bit=3)])
+    other = jnp.concatenate([send(spectra, tm_bit=0, rep_bit=3), send(spectra, tm_bit=0, rep_bit=1)])
     bits = rep.bit_length() - 1
     proj = pl.pallas_call(
-        functools.partial(first_kernel, snaps, bits),
+        functools.partial(first_kernel, snaps, bits, len(highs)),
         out_shape=pltpu.VMEM((local_bins, rows, 2 * lanes), F32),
-        in_specs=[vmem] * (1 + len(parts)),
+        in_specs=[vmem] * (1 + 2 * len(highs)),
         out_specs=vmem,
         compiler_params=pltpu.CompilerParams(vmem_limit_bytes=6 * MIB),
         cost_estimate=pl.CostEstimate(flops=COST, bytes_accessed=0, transcendentals=0),
         name="first",
-    )(own, *parts)
+    )(own, *highs, *lows)
     chunk = rows // tm
     count = tm // 2
     share = pltpu.VMEM((count, chunk), F32)
@@ -344,22 +392,22 @@
             pltpu.VMEM((local_bins, elem_count, 2 * lanes), BF16),
             pltpu.VMEM((local_bins, 1, 2 * lanes), F32),
         ],
-        in_specs=[vmem] * (3 + len(parts) + len(inverses)),
+        in_specs=[vmem] * (3 + 3 * len(highs)),
         out_specs=[vmem] * 3,
         scratch_shapes=sums,
         compiler_params=pltpu.CompilerParams(vmem_limit_bytes=6 * MIB),
         name="second",
-    )(other, own, proj, *parts, *inverses)
+    )(other, own, proj, *highs, *lows, *inverses)
     here = pl.pallas_call(
         functools.partial(third_kernel, len(inverses)),
         out_shape=share,
-        in_specs=[vmem] * (3 + len(parts) + len(inverses)),
+        in_specs=[vmem] * (3 + 3 * len(highs)),
         out_specs=vmem,
         scratch_shapes=sums,
         compiler_params=pltpu.CompilerParams(vmem_limit_bytes=6 * MIB),
         cost_estimate=pl.CostEstimate(flops=COST, bytes_accessed=0, transcendentals=0),
         name="third",
-    )(rights, factors, proj, *parts, *inverses)
+    )(rights, factors, proj, *highs, *lows, *inverses)
     total = here + send(there, tm_bit=count, rep_bit=0)
     for bit in bits_of(tm)[1:]:
         total = total[:bit] + send(total[bit:], tm_bit=bit, rep_bit=0)

time: 32.5 us -> 31.4 us (0.966)
  waiting for transfers between devices: 3.36 us -> 2.16 us
    ppermute x9, waiting for transfers between devices: 3.36 us -> 2.16 us  [swap(): return lax.ppermute(x, ('tm', 'rep'), pairs)]
    pallas_call x3 -> x4, Pallas kernels: 11.7 us -> 11.7 us  [the longest x2 8.4 us: prepare(): pl.pallas_call(functools.partial(prepare_kernel, first, elems), out_shape...]
  transfers between devices with their start and end apart: 9 -> 9, of which waited for: 5 -> 4; matrix products, arithmetic and copies ran while one was open for 0% -> 0% of each run, Pallas kernels for 41% -> 42%
where the time goes in v5:
time: 31.4 us; the launch traced here: 31.2 us
  Pallas kernels  17.4 us (55%)
  starting transfers between devices  11 us (35%)
  waiting for transfers between devices  2.16 us (7%)
  other arithmetic  0.61 us (2%)
    ppermute x9, starting transfers between devices, swap(): return lax.ppermute(x, ('tm', 'rep'), pairs)  11 us
    pallas_call x2, Pallas kernels, prepare(): pl.pallas_call(functools.partial(prepare_kernel, first, elems), out_shape...  8.4 us
    pallas_call x1, Pallas kernels, shards(): pl.pallas_call(functools.partial(first_kernel, snaps, bits, len(highs)),...  2.49 us
    ppermute x9, waiting for transfers between devices, swap(): return lax.ppermute(x, ('tm', 'rep'), pairs)  2.16 us
    pallas_call x1, Pallas kernels, shards(): pl.pallas_call(functools.partial(dft_kernel, tm), out_shape=(pltpu.VMEM(s...  2.05 us
    pallas_call x1, Pallas kernels, shards(): pl.pallas_call(functools.partial(second_kernel, elem_count, bins, snaps,...  1.81 us
    pallas_call x1, Pallas kernels, shards(): pl.pallas_call(functools.partial(third_kernel, len(inverses)), out_shape=...  1.55 us
    pallas_call x1, Pallas kernels, finish(): pl.pallas_call(functools.partial(finish_kernel, elems), out_shape=results...  0.77 us
  transfers between devices with their start and end apart: 9, of which 4 were waited for; matrix products, arithmetic and copies ran while one was open for 0% of the time, Pallas kernels for 42%

profile of v5, /device:TPU:0, one launch (start us, length us, event | category | flops | bytes accessed | tf_op | source)
XLA Modules:
  0.0 31.2 jit_solution(1504229906427305139)
XLA Ops:
  0.0 2.0 %dft.1 = (f32[2,32,128]{2,1,0:T(8,128)S(1)}, f32[2,32,128]{2,1,0:T(8,128)S(1)}) custom-call(s32[32]{0:T(128)} %bins_hbm.1, f32[8,32,1024]{2,1,0:T(8,128)} %snap_hbm.1), custom_call_target="tpu_custom_call" | custom-call | tf_op jit(solution)/shard_map/dft/pallas_call | solution.py:275
  2.1 5.0 %collective-permute-start.2 = (f32[2,32,128]{2,1,0:T(8,128)S(1)}, f32[2,32,128]{2,1,0:T(8,128)S(1)}, u32[]{:S(2)}, u32[]{:S(2)}) collective-permute-start(f32[2,32,128]{2,1,0:T(8,128)S(1)} %get-tuple-element.21), channel_id=1, source_target_pairs={{0,20},{1,21},{2,22},{3,23},{4,16},{5,17},{6,18},{7,19},{8,28},{9,... | collective-permute-start | bytes 98312 | tf_op jit(solution)/shard_map/ppermute | solution.py:258
  7.1 0.5 %collective-permute-start = (f32[2,32,128]{2,1,0:T(8,128)S(1)}, f32[2,32,128]{2,1,0:T(8,128)S(1)}, u32[]{:S(2)}, u32[]{:S(2)}) collective-permute-start(f32[2,32,128]{2,1,0:T(8,128)S(1)} %get-tuple-element.21), channel_id=1, source_target_pairs={{0,16},{1,17},{2,18},{3,19},{4,20},{5,21},{6,22},{7,23},{8,24},{9,... | collective-permute-start | bytes 98312 | tf_op jit(solution)/shard_map/ppermute | solution.py:258
  7.6 0.1 collective-permute-start.1
  7.7 4.6 %prepare.2 = (bf16[2,4,1024,256]{3,2,1,0:T(8,128)(2,1)S(1)}, bf16[2,4,1024,256]{3,2,1,0:T(8,128)(2,1)S(1)}, f32[4,1024,128]{2,1,0:T(8,128)S(1)}, f32[2,1,1024,256]{3,2,1,0:T(8,128)S(1)}) custom-call(f32[2,32,128]{2,1,0:T(8,128)S(1)} %get-tuple-element.20.after_ref.refs_0_, f32[2,8,1024,256]{3,2,1,0:T(8,128)} %rep_hbm.3), custom_call_target="tpu_custom_call" | custom-call | flops 20000000000 | tf_op jit(solution)/shard_map/prepare/pallas_call | solution.py:309
  12.4 0.0 collective-permute-done.2.refs_3_
  12.4 0.0 collective-permute-done.refs_1_
  12.4 0.0 collective-permute-done.1.refs_2_
  12.4 0.1 collective-permute-start.3
  12.5 0.8 %finish.1 = (bf16[2,1,1024,256]{3,2,1,0:T(8,128)(2,1)S(1)}, bf16[2,1,1024,256]{3,2,1,0:T(8,128)(2,1)S(1)}, f32[1,1024,128]{2,1,0:T(8,128)S(1)}) custom-call(f32[4,32,128]{2,1,0:T(8,128)S(1)} %collect.1.after_ref, f32[2,1,1024,256]{3,2,1,0:T(8,128)S(1)} %get-tuple-element.24.rep_ref), custom_call_target="tpu_custom_call" | custom-call | flops 20000000000 | tf_op jit(solution)/shard_map/finish/pallas_call | solution.py:326
  13.3 0.5 %collective-permute-done.3.refs_4_ = f32[4,32,128]{2,1,0:T(8,128)S(1)} collective-permute-done((f32[4,32,128]{2,1,0:T(8,128)S(1)}, f32[4,32,128]{2,1,0:T(8,128)S(1)}, u32[]{:S(2)}, u32[]{:S(2)}) %collective-permute-start.3) | collective-permute-done | bytes 65568 | tf_op jit(solution)/shard_map/ppermute | solution.py:258
  13.8 0.3 pack.1.after_ref
  14.1 1.9 %collective-permute-start.6 = (f32[2,32,512]{2,1,0:T(8,128)S(1)}, f32[2,32,512]{2,1,0:T(8,128)S(1)}, u32[]{:S(2)}, u32[]{:S(2)}) collective-permute-start(f32[2,32,512]{2,1,0:T(8,128)S(1)} %pack.1.after_ref), channel_id=1, source_target_pairs={{0,2},{1,3},{2,0},{3,1},{4,6},{5,7},{6,4},{7,5},{8,10},{9,11},{10,... | collective-permute-start | bytes 393224 | tf_op jit(solution)/shard_map/ppermute | solution.py:258
  15.9 1.5 %collective-permute-start.5 = (f32[2,32,512]{2,1,0:T(8,128)S(1)}, f32[2,32,512]{2,1,0:T(8,128)S(1)}, u32[]{:S(2)}, u32[]{:S(2)}) collective-permute-start(f32[2,32,512]{2,1,0:T(8,128)S(1)} %pack.1.after_ref), channel_id=1, source_target_pairs={{0,1},{1,0},{2,3},{3,2},{4,5},{5,4},{6,7},{7,6},{8,9},{9,8},{10,11... | collective-permute-start | bytes 393224 | tf_op jit(solution)/shard_map/ppermute | solution.py:258
  17.4 0.2 collective-permute-start.4
  17.6 3.8 %prepare.3 = (bf16[2,3,1024,256]{3,2,1,0:T(8,128)(2,1)S(1)}, bf16[2,3,1024,256]{3,2,1,0:T(8,128)(2,1)S(1)}, f32[3,1024,128]{2,1,0:T(8,128)S(1)}) custom-call(f32[2,32,512]{2,1,0:T(8,128)S(1)} %pack.1.after_ref, f32[2,8,1024,256]{3,2,1,0:T(8,128)} %rep_hbm.3), custom_call_target="tpu_custom_call" | custom-call | flops 20000000000 | tf_op jit(solution)/shard_map/prepare/pallas_call | solution.py:309
  21.4 0.0 collective-permute-done.6
  21.4 2.5 %first.1.proj_ref = f32[8,1024,128]{2,1,0:T(8,128)S(1)} custom-call(f32[4,32,512]{2,1,0:T(8,128)S(1)} %pad_maximum_fusion.1.spec_ref.own_ref, bf16[2,4,1024,256]{3,2,1,0:T(8,128)(2,1)S(1)} %get-tuple-element.23.refs_0_, bf16[2,1,1024,256]{3,2,1,0:T(8,128)(2,1)S(1)} %get-tuple-element.25.refs_1_, bf16[2,3,1024,256]{3,2,1,0:T(8,128)(2,1)S(1)} %get-tuple-element.26.refs_2_, ...), custom_call_target="tpu_custom_call" | custom-call | flops 20000000000 | tf_op jit(solution)/shard_map/first/pallas_call | solution.py:375
  23.9 0.1 collective-permute-done.5
  24.0 0.0 collective-permute-done.4
  24.0 1.8 %second.1 = (f32[2,256]{1,0:T(2,128)S(1)}, bf16[8,256,128]{2,1,0:T(8,128)(2,1)S(1)}, f32[8,1,128]{2,1,0:T(1,128)S(1)}) custom-call(f32[4,32,512]{2,1,0:T(8,128)S(1)} %pad_maximum_fusion.spec_ref, f32[4,32,512]{2,1,0:T(8,128)S(1)} %pad_maximum_fusion.1.spec_ref.own_ref, f32[8,1024,128]{2,1,0:T(8,128)S(1)} %first.1.proj_ref, ...), custom_call_target="tpu_custom_call" | custom-call | tf_op jit(solution)/shard_map/second/pallas_call | solution.py:388
  25.9 1.7 %collective-permute-start.7 = (f32[2,256]{1,0:T(2,128)S(1)}, f32[2,256]{1,0:T(2,128)S(1)}, u32[]{:S(2)}, u32[]{:S(2)}) collective-permute-start(f32[2,256]{1,0:T(2,128)S(1)} %get-tuple-element.34), channel_id=1, source_target_pairs={{0,16},{1,17},{2,18},{3,19},{4,20},{5,21},{6,22},{7,23},{8,24},{9,... | collective-permute-start | bytes 6152 | tf_op jit(solution)/shard_map/ppermute | solution.py:258
  27.6 1.5 %third.1 = f32[2,256]{1,0:T(2,128)S(1)} custom-call(bf16[8,256,128]{2,1,0:T(8,128)(2,1)S(1)} %get-tuple-element.32.right_ref, f32[8,1,128]{2,1,0:T(1,128)S(1)} %get-tuple-element.33.factor_ref, f32[8,1024,128]{2,1,0:T(8,128)S(1)} %first.1.proj_ref, bf16[2,4,1024,256]{3,2,1,0:T(8,128)(2,1)S(1)} %get-tuple-element.23.refs_0_, ...), custom_call_target="tpu_custom_call" | custom-call | flops 20000000000 | tf_op jit(solution)/shard_map/third/pallas_call | solution.py:401
  29.1 0.4 %collective-permute-done.7 = f32[2,256]{1,0:T(2,128)S(1)} collective-permute-done((f32[2,256]{1,0:T(2,128)S(1)}, f32[2,256]{1,0:T(2,128)S(1)}, u32[]{:S(2)}, u32[]{:S(2)}) %collective-permute-start.7) | collective-permute-done | bytes 2080 | tf_op jit(solution)/shard_map/ppermute | solution.py:258
  29.5 0.0 collective-permute-start.8
  29.5 1.1 %collective-permute-done.8 = f32[1,256]{1,0:T(1,128)S(1)} collective-permute-done((f32[1,256]{1,0:T(1,128)S(1)}, f32[1,256]{1,0:T(1,128)S(1)}, u32[]{:S(2)}, u32[]{:S(2)}) %collective-permute-start.8) | collective-permute-done | bytes 1056 | tf_op jit(solution)/shard_map/ppermute | solution.py:258
  30.7 0.6 %slice_add_fusion = f32[1,256]{1,0:T(1,128)} fusion(f32[1,256]{1,0:T(1,128)S(1)} %collective-permute-done.8, f32[2,256]{1,0:T(2,128)S(1)} %add.6), kind=kLoop, calls=%fused_computation.2 | loop fusion | flops 256 | bytes 3072 | tf_op jit(solution)/shard_map/add | solution.py:413
  (5 shorter events, 0.1 us)
Async XLA Ops:
  2.1 10.3 %collective-permute-start.2 = (f32[2,32,128]{2,1,0:T(8,128)S(1)}, f32[2,32,128]{2,1,0:T(8,128)S(1)}, u32[]{:S(2)}, u32[]{:S(2)}) collective-permute-start(f32[2,32,128]{2,1,0:T(8,128)S(1)} %get-tuple-element.21), channel_id=1, source_target_pairs={{0,20},{1,21},{2,22},{3,23},{4,16},{5,17},{6,18},{7,19},{8,28},{9,... | collective-permute-start | bytes 98312 | tf_op jit(solution)/shard_map/ppermute | solution.py:258
  7.1 5.3 %collective-permute-start = (f32[2,32,128]{2,1,0:T(8,128)S(1)}, f32[2,32,128]{2,1,0:T(8,128)S(1)}, u32[]{:S(2)}, u32[]{:S(2)}) collective-permute-start(f32[2,32,128]{2,1,0:T(8,128)S(1)} %get-tuple-element.21), channel_id=1, source_target_pairs={{0,16},{1,17},{2,18},{3,19},{4,20},{5,21},{6,22},{7,23},{8,24},{9,... | collective-permute-start | bytes 98312 | tf_op jit(solution)/shard_map/ppermute | solution.py:258
  7.6 4.8 %collective-permute-start.1 = (f32[2,32,128]{2,1,0:T(8,128)S(1)}, f32[2,32,128]{2,1,0:T(8,128)S(1)}, u32[]{:S(2)}, u32[]{:S(2)}) collective-permute-start(f32[2,32,128]{2,1,0:T(8,128)S(1)} %get-tuple-element.20.after_ref.refs_0_), channel_id=1, source_target_pairs={{0,4},{1,5},{2,6},{3,7},{4,0},{5,1},{6,2},{7,3},{8,12},{9,13},{10,... | collective-permute-start | bytes 98312 | tf_op jit(solution)/shard_map/ppermute | solution.py:258
  12.4 1.3 %collective-permute-start.3 = (f32[4,32,128]{2,1,0:T(8,128)S(1)}, f32[4,32,128]{2,1,0:T(8,128)S(1)}, u32[]{:S(2)}, u32[]{:S(2)}) collective-permute-start(f32[4,32,128]{2,1,0:T(8,128)S(1)} %collect.1.after_ref), channel_id=1, source_target_pairs={{0,8},{1,9},{2,10},{3,11},{4,12},{5,13},{6,14},{7,15},{8,0},{9,1},... | collective-permute-start | bytes 196616 | tf_op jit(solution)/shard_map/ppermute | solution.py:258
  14.1 7.3 %collective-permute-start.6 = (f32[2,32,512]{2,1,0:T(8,128)S(1)}, f32[2,32,512]{2,1,0:T(8,128)S(1)}, u32[]{:S(2)}, u32[]{:S(2)}) collective-permute-start(f32[2,32,512]{2,1,0:T(8,128)S(1)} %pack.1.after_ref), channel_id=1, source_target_pairs={{0,2},{1,3},{2,0},{3,1},{4,6},{5,7},{6,4},{7,5},{8,10},{9,11},{10,... | collective-permute-start | bytes 393224 | tf_op jit(solution)/shard_map/ppermute | solution.py:258
  15.9 8.1 %collective-permute-start.5 = (f32[2,32,512]{2,1,0:T(8,128)S(1)}, f32[2,32,512]{2,1,0:T(8,128)S(1)}, u32[]{:S(2)}, u32[]{:S(2)}) collective-permute-start(f32[2,32,512]{2,1,0:T(8,128)S(1)} %pack.1.after_ref), channel_id=1, source_target_pairs={{0,1},{1,0},{2,3},{3,2},{4,5},{5,4},{6,7},{7,6},{8,9},{9,8},{10,11... | collective-permute-start | bytes 393224 | tf_op jit(solution)/shard_map/ppermute | solution.py:258
  17.4 6.6 %collective-permute-start.4 = (f32[2,32,512]{2,1,0:T(8,128)S(1)}, f32[2,32,512]{2,1,0:T(8,128)S(1)}, u32[]{:S(2)}, u32[]{:S(2)}) collective-permute-start(f32[2,32,512]{2,1,0:T(8,128)S(1)} %pack.1.after_ref), channel_id=1, source_target_pairs={{0,3},{1,2},{2,1},{3,0},{4,7},{5,6},{6,5},{7,4},{8,11},{9,10},{10,... | collective-permute-start | bytes 393224 | tf_op jit(solution)/shard_map/ppermute | solution.py:258
  25.9 3.7 %collective-permute-start.7 = (f32[2,256]{1,0:T(2,128)S(1)}, f32[2,256]{1,0:T(2,128)S(1)}, u32[]{:S(2)}, u32[]{:S(2)}) collective-permute-start(f32[2,256]{1,0:T(2,128)S(1)} %get-tuple-element.34), channel_id=1, source_target_pairs={{0,16},{1,17},{2,18},{3,19},{4,20},{5,21},{6,22},{7,23},{8,24},{9,... | collective-permute-start | bytes 6152 | tf_op jit(solution)/shard_map/ppermute | solution.py:258
  29.5 1.1 %collective-permute-start.8 = (f32[1,256]{1,0:T(1,128)S(1)}, f32[1,256]{1,0:T(1,128)S(1)}, u32[]{:S(2)}, u32[]{:S(2)}) collective-permute-start(f32[1,256]{1,0:T(1,128)S(1)} %slice.9), channel_id=1, source_target_pairs={{0,8},{1,9},{2,10},{3,11},{4,12},{5,13},{6,14},{7,15},{8,0},{9,1},... | collective-permute-start | bytes 3080 | tf_op jit(solution)/shard_map/ppermute | solution.py:258

commit v6 on v5

--- a/solution.py
+++ b/solution.py
@@ -91,14 +91,40 @@
     away_ref[...] = moved[keep_ref.shape[0] :]
 
 
+def interleave(parts, local_bins):
+    width = parts[0].shape[1]
+    group = width // local_bins
+    fits = width == 128 and len(parts) * 2 * group == width and local_bins % 2 == 0
+    if not fits or len(parts) & (len(parts) - 1):
+        return jnp.concatenate(
+            [part[:, f * group : (f + 1) * group] for f in range(local_bins) for part in parts], axis=1
+        )
+    lane = lax.broadcasted_iota(jnp.int32, parts[0].shape, 1)
+    merged, size = [{None: (part, list(range(local_bins)))} for part in parts], group
+    while len(merged) > 1:
+        even = lane // size % 2 == 0
+        following = []
+        for a, b in zip(merged[::2], merged[1::2]):
+            both = {}
+            for key in a:
+                (x, bins), (y, _) = a[key], b[key]
+                both[key, 0] = jnp.where(even, x, pltpu.roll(y, size, 1)), bins[::2]
+                both[key, 1] = jnp.where(even, pltpu.roll(x, width - size, 1), y), bins[1::2]
+            following.append(both)
+        merged, size = following, 2 * size
+    place = {f: (x, k) for x, bins in merged[0].values() for k, f in enumerate(bins)}
+    near = lane < size
+    pairs = []
+    for f in range(0, local_bins, 2):
+        (x, i), (y, j) = place[f], place[f + 1]
+        pairs.append(jnp.where(near, pltpu.roll(x, size, 1) if i else x, y if j else pltpu.roll(y, size, 1)))
+    return jnp.concatenate(pairs, axis=1)
+
+
 def pack_kernel(local_bins, slots, *refs):
     *blocks, out_ref = refs
     for n in range(out_ref.shape[0]):
-        parts = [blocks[k][b] for k, b in slots[n]]
-        group = parts[0].shape[1] // local_bins
-        out_ref[n] = jnp.concatenate(
-            [part[:, f * group : (f + 1) * group] for f in range(local_bins) for part in parts], axis=1
-        )
+        out_ref[n] = interleave([blocks[k][b] for k, b in slots[n]], local_bins)
 
 
 def collect_kernel(after_ref, *refs):

time: 31.4 us -> 31.3 us (level)
  no operation moved by 1% of the time
where the time goes in v6:
time: 31.3 us; the launch traced here: 31.2 us
  Pallas kernels  17.3 us (55%)
  starting transfers between devices  11 us (35%)
  waiting for transfers between devices  2.16 us (7%)
  other arithmetic  0.61 us (2%)
    ppermute x9, starting transfers between devices, swap(): return lax.ppermute(x, ('tm', 'rep'), pairs)  11 us
    pallas_call x2, Pallas kernels, prepare(): pl.pallas_call(functools.partial(prepare_kernel, first, elems), out_shape...  8.4 us
    pallas_call x1, Pallas kernels, shards(): pl.pallas_call(functools.partial(first_kernel, snaps, bits, len(highs)),...  2.49 us
    ppermute x9, waiting for transfers between devices, swap(): return lax.ppermute(x, ('tm', 'rep'), pairs)  2.16 us
    pallas_call x1, Pallas kernels, shards(): pl.pallas_call(functools.partial(dft_kernel, tm), out_shape=(pltpu.VMEM(s...  2.05 us
    pallas_call x1, Pallas kernels, shards(): pl.pallas_call(functools.partial(second_kernel, elem_count, bins, snaps,...  1.81 us
    pallas_call x1, Pallas kernels, shards(): pl.pallas_call(functools.partial(third_kernel, len(inverses)), out_shape=...  1.55 us
    pallas_call x1, Pallas kernels, finish(): pl.pallas_call(functools.partial(finish_kernel, elems), out_shape=results...  0.77 us
  transfers between devices with their start and end apart: 9, of which 4 were waited for; matrix products, arithmetic and copies ran while one was open for 0% of the time, Pallas kernels for 42%

profile of v6, /device:TPU:0, one launch (start us, length us, event | category | flops | bytes accessed | tf_op | source)
XLA Modules:
  0.0 31.2 jit_solution(8339659500541491618)
XLA Ops:
  0.0 2.0 %dft.1 = (f32[2,32,128]{2,1,0:T(8,128)S(1)}, f32[2,32,128]{2,1,0:T(8,128)S(1)}) custom-call(s32[32]{0:T(128)} %bins_hbm.1, f32[8,32,1024]{2,1,0:T(8,128)} %snap_hbm.1), custom_call_target="tpu_custom_call" | custom-call | tf_op jit(solution)/shard_map/dft/pallas_call | solution.py:301
  2.1 5.0 %collective-permute-start.2 = (f32[2,32,128]{2,1,0:T(8,128)S(1)}, f32[2,32,128]{2,1,0:T(8,128)S(1)}, u32[]{:S(2)}, u32[]{:S(2)}) collective-permute-start(f32[2,32,128]{2,1,0:T(8,128)S(1)} %get-tuple-element.21), channel_id=1, source_target_pairs={{0,20},{1,21},{2,22},{3,23},{4,16},{5,17},{6,18},{7,19},{8,28},{9,... | collective-permute-start | bytes 98312 | tf_op jit(solution)/shard_map/ppermute | solution.py:284
  7.1 0.5 %collective-permute-start = (f32[2,32,128]{2,1,0:T(8,128)S(1)}, f32[2,32,128]{2,1,0:T(8,128)S(1)}, u32[]{:S(2)}, u32[]{:S(2)}) collective-permute-start(f32[2,32,128]{2,1,0:T(8,128)S(1)} %get-tuple-element.21), channel_id=1, source_target_pairs={{0,16},{1,17},{2,18},{3,19},{4,20},{5,21},{6,22},{7,23},{8,24},{9,... | collective-permute-start | bytes 98312 | tf_op jit(solution)/shard_map/ppermute | solution.py:284
  7.6 0.1 collective-permute-start.1
  7.7 4.6 %prepare.2 = (bf16[2,4,1024,256]{3,2,1,0:T(8,128)(2,1)S(1)}, bf16[2,4,1024,256]{3,2,1,0:T(8,128)(2,1)S(1)}, f32[4,1024,128]{2,1,0:T(8,128)S(1)}, f32[2,1,1024,256]{3,2,1,0:T(8,128)S(1)}) custom-call(f32[2,32,128]{2,1,0:T(8,128)S(1)} %get-tuple-element.20.after_ref.refs_0_, f32[2,8,1024,256]{3,2,1,0:T(8,128)} %rep_hbm.3), custom_call_target="tpu_custom_call" | custom-call | flops 20000000000 | tf_op jit(solution)/shard_map/prepare/pallas_call | solution.py:335
  12.4 0.0 collective-permute-done.2.refs_3_
  12.4 0.0 collective-permute-done.refs_1_
  12.4 0.0 collective-permute-done.1.refs_2_
  12.4 0.1 collective-permute-start.3
  12.5 0.8 %finish.1 = (bf16[2,1,1024,256]{3,2,1,0:T(8,128)(2,1)S(1)}, bf16[2,1,1024,256]{3,2,1,0:T(8,128)(2,1)S(1)}, f32[1,1024,128]{2,1,0:T(8,128)S(1)}) custom-call(f32[4,32,128]{2,1,0:T(8,128)S(1)} %collect.1.after_ref, f32[2,1,1024,256]{3,2,1,0:T(8,128)S(1)} %get-tuple-element.24.rep_ref), custom_call_target="tpu_custom_call" | custom-call | flops 20000000000 | tf_op jit(solution)/shard_map/finish/pallas_call | solution.py:352
  13.3 0.5 %collective-permute-done.3.refs_4_ = f32[4,32,128]{2,1,0:T(8,128)S(1)} collective-permute-done((f32[4,32,128]{2,1,0:T(8,128)S(1)}, f32[4,32,128]{2,1,0:T(8,128)S(1)}, u32[]{:S(2)}, u32[]{:S(2)}) %collective-permute-start.3) | collective-permute-done | bytes 65568 | tf_op jit(solution)/shard_map/ppermute | solution.py:284
  13.8 0.2 pack.1.after_ref
  14.0 1.9 %collective-permute-start.6 = (f32[2,32,512]{2,1,0:T(8,128)S(1)}, f32[2,32,512]{2,1,0:T(8,128)S(1)}, u32[]{:S(2)}, u32[]{:S(2)}) collective-permute-start(f32[2,32,512]{2,1,0:T(8,128)S(1)} %pack.1.after_ref), channel_id=1, source_target_pairs={{0,2},{1,3},{2,0},{3,1},{4,6},{5,7},{6,4},{7,5},{8,10},{9,11},{10,... | collective-permute-start | bytes 393224 | tf_op jit(solution)/shard_map/ppermute | solution.py:284
  15.9 1.5 %collective-permute-start.5 = (f32[2,32,512]{2,1,0:T(8,128)S(1)}, f32[2,32,512]{2,1,0:T(8,128)S(1)}, u32[]{:S(2)}, u32[]{:S(2)}) collective-permute-start(f32[2,32,512]{2,1,0:T(8,128)S(1)} %pack.1.after_ref), channel_id=1, source_target_pairs={{0,1},{1,0},{2,3},{3,2},{4,5},{5,4},{6,7},{7,6},{8,9},{9,8},{10,11... | collective-permute-start | bytes 393224 | tf_op jit(solution)/shard_map/ppermute | solution.py:284
  17.4 0.2 collective-permute-start.4
  17.6 3.8 %prepare.3 = (bf16[2,3,1024,256]{3,2,1,0:T(8,128)(2,1)S(1)}, bf16[2,3,1024,256]{3,2,1,0:T(8,128)(2,1)S(1)}, f32[3,1024,128]{2,1,0:T(8,128)S(1)}) custom-call(f32[2,32,512]{2,1,0:T(8,128)S(1)} %pack.1.after_ref, f32[2,8,1024,256]{3,2,1,0:T(8,128)} %rep_hbm.3), custom_call_target="tpu_custom_call" | custom-call | flops 20000000000 | tf_op jit(solution)/shard_map/prepare/pallas_call | solution.py:335
  21.3 0.0 collective-permute-done.6
  21.4 2.5 %first.1.proj_ref = f32[8,1024,128]{2,1,0:T(8,128)S(1)} custom-call(f32[4,32,512]{2,1,0:T(8,128)S(1)} %pad_maximum_fusion.1.spec_ref.own_ref, bf16[2,4,1024,256]{3,2,1,0:T(8,128)(2,1)S(1)} %get-tuple-element.23.refs_0_, bf16[2,1,1024,256]{3,2,1,0:T(8,128)(2,1)S(1)} %get-tuple-element.25.refs_1_, bf16[2,3,1024,256]{3,2,1,0:T(8,128)(2,1)S(1)} %get-tuple-element.26.refs_2_, ...), custom_call_target="tpu_custom_call" | custom-call | flops 20000000000 | tf_op jit(solution)/shard_map/first/pallas_call | solution.py:401
  23.9 0.1 collective-permute-done.5
  24.0 0.0 collective-permute-done.4
  24.0 1.8 %second.1 = (f32[2,256]{1,0:T(2,128)S(1)}, bf16[8,256,128]{2,1,0:T(8,128)(2,1)S(1)}, f32[8,1,128]{2,1,0:T(1,128)S(1)}) custom-call(f32[4,32,512]{2,1,0:T(8,128)S(1)} %pad_maximum_fusion.spec_ref, f32[4,32,512]{2,1,0:T(8,128)S(1)} %pad_maximum_fusion.1.spec_ref.own_ref, f32[8,1024,128]{2,1,0:T(8,128)S(1)} %first.1.proj_ref, ...), custom_call_target="tpu_custom_call" | custom-call | tf_op jit(solution)/shard_map/second/pallas_call | solution.py:414
  25.8 1.7 %collective-permute-start.7 = (f32[2,256]{1,0:T(2,128)S(1)}, f32[2,256]{1,0:T(2,128)S(1)}, u32[]{:S(2)}, u32[]{:S(2)}) collective-permute-start(f32[2,256]{1,0:T(2,128)S(1)} %get-tuple-element.34), channel_id=1, source_target_pairs={{0,16},{1,17},{2,18},{3,19},{4,20},{5,21},{6,22},{7,23},{8,24},{9,... | collective-permute-start | bytes 6152 | tf_op jit(solution)/shard_map/ppermute | solution.py:284
  27.5 1.6 %third.1 = f32[2,256]{1,0:T(2,128)S(1)} custom-call(bf16[8,256,128]{2,1,0:T(8,128)(2,1)S(1)} %get-tuple-element.32.right_ref, f32[8,1,128]{2,1,0:T(1,128)S(1)} %get-tuple-element.33.factor_ref, f32[8,1024,128]{2,1,0:T(8,128)S(1)} %first.1.proj_ref, bf16[2,4,1024,256]{3,2,1,0:T(8,128)(2,1)S(1)} %get-tuple-element.23.refs_0_, ...), custom_call_target="tpu_custom_call" | custom-call | flops 20000000000 | tf_op jit(solution)/shard_map/third/pallas_call | solution.py:427
  29.1 0.4 %collective-permute-done.7 = f32[2,256]{1,0:T(2,128)S(1)} collective-permute-done((f32[2,256]{1,0:T(2,128)S(1)}, f32[2,256]{1,0:T(2,128)S(1)}, u32[]{:S(2)}, u32[]{:S(2)}) %collective-permute-start.7) | collective-permute-done | bytes 2080 | tf_op jit(solution)/shard_map/ppermute | solution.py:284
  29.5 0.0 collective-permute-start.8
  29.5 1.1 %collective-permute-done.8 = f32[1,256]{1,0:T(1,128)S(1)} collective-permute-done((f32[1,256]{1,0:T(1,128)S(1)}, f32[1,256]{1,0:T(1,128)S(1)}, u32[]{:S(2)}, u32[]{:S(2)}) %collective-permute-start.8) | collective-permute-done | bytes 1056 | tf_op jit(solution)/shard_map/ppermute | solution.py:284
  30.6 0.6 %slice_add_fusion = f32[1,256]{1,0:T(1,128)} fusion(f32[1,256]{1,0:T(1,128)S(1)} %collective-permute-done.8, f32[2,256]{1,0:T(2,128)S(1)} %add.6), kind=kLoop, calls=%fused_computation.2 | loop fusion | flops 256 | bytes 3072 | tf_op jit(solution)/shard_map/add | solution.py:439
  (5 shorter events, 0.1 us)
Async XLA Ops:
  2.1 10.3 %collective-permute-start.2 = (f32[2,32,128]{2,1,0:T(8,128)S(1)}, f32[2,32,128]{2,1,0:T(8,128)S(1)}, u32[]{:S(2)}, u32[]{:S(2)}) collective-permute-start(f32[2,32,128]{2,1,0:T(8,128)S(1)} %get-tuple-element.21), channel_id=1, source_target_pairs={{0,20},{1,21},{2,22},{3,23},{4,16},{5,17},{6,18},{7,19},{8,28},{9,... | collective-permute-start | bytes 98312 | tf_op jit(solution)/shard_map/ppermute | solution.py:284
  7.1 5.3 %collective-permute-start = (f32[2,32,128]{2,1,0:T(8,128)S(1)}, f32[2,32,128]{2,1,0:T(8,128)S(1)}, u32[]{:S(2)}, u32[]{:S(2)}) collective-permute-start(f32[2,32,128]{2,1,0:T(8,128)S(1)} %get-tuple-element.21), channel_id=1, source_target_pairs={{0,16},{1,17},{2,18},{3,19},{4,20},{5,21},{6,22},{7,23},{8,24},{9,... | collective-permute-start | bytes 98312 | tf_op jit(solution)/shard_map/ppermute | solution.py:284
  7.6 4.8 %collective-permute-start.1 = (f32[2,32,128]{2,1,0:T(8,128)S(1)}, f32[2,32,128]{2,1,0:T(8,128)S(1)}, u32[]{:S(2)}, u32[]{:S(2)}) collective-permute-start(f32[2,32,128]{2,1,0:T(8,128)S(1)} %get-tuple-element.20.after_ref.refs_0_), channel_id=1, source_target_pairs={{0,4},{1,5},{2,6},{3,7},{4,0},{5,1},{6,2},{7,3},{8,12},{9,13},{10,... | collective-permute-start | bytes 98312 | tf_op jit(solution)/shard_map/ppermute | solution.py:284
  12.4 1.3 %collective-permute-start.3 = (f32[4,32,128]{2,1,0:T(8,128)S(1)}, f32[4,32,128]{2,1,0:T(8,128)S(1)}, u32[]{:S(2)}, u32[]{:S(2)}) collective-permute-start(f32[4,32,128]{2,1,0:T(8,128)S(1)} %collect.1.after_ref), channel_id=1, source_target_pairs={{0,8},{1,9},{2,10},{3,11},{4,12},{5,13},{6,14},{7,15},{8,0},{9,1},... | collective-permute-start | bytes 196616 | tf_op jit(solution)/shard_map/ppermute | solution.py:284
  14.0 7.3 %collective-permute-start.6 = (f32[2,32,512]{2,1,0:T(8,128)S(1)}, f32[2,32,512]{2,1,0:T(8,128)S(1)}, u32[]{:S(2)}, u32[]{:S(2)}) collective-permute-start(f32[2,32,512]{2,1,0:T(8,128)S(1)} %pack.1.after_ref), channel_id=1, source_target_pairs={{0,2},{1,3},{2,0},{3,1},{4,6},{5,7},{6,4},{7,5},{8,10},{9,11},{10,... | collective-permute-start | bytes 393224 | tf_op jit(solution)/shard_map/ppermute | solution.py:284
  15.9 8.1 %collective-permute-start.5 = (f32[2,32,512]{2,1,0:T(8,128)S(1)}, f32[2,32,512]{2,1,0:T(8,128)S(1)}, u32[]{:S(2)}, u32[]{:S(2)}) collective-permute-start(f32[2,32,512]{2,1,0:T(8,128)S(1)} %pack.1.after_ref), channel_id=1, source_target_pairs={{0,1},{1,0},{2,3},{3,2},{4,5},{5,4},{6,7},{7,6},{8,9},{9,8},{10,11... | collective-permute-start | bytes 393224 | tf_op jit(solution)/shard_map/ppermute | solution.py:284
  17.4 6.6 %collective-permute-start.4 = (f32[2,32,512]{2,1,0:T(8,128)S(1)}, f32[2,32,512]{2,1,0:T(8,128)S(1)}, u32[]{:S(2)}, u32[]{:S(2)}) collective-permute-start(f32[2,32,512]{2,1,0:T(8,128)S(1)} %pack.1.after_ref), channel_id=1, source_target_pairs={{0,3},{1,2},{2,1},{3,0},{4,7},{5,6},{6,5},{7,4},{8,11},{9,10},{10,... | collective-permute-start | bytes 393224 | tf_op jit(solution)/shard_map/ppermute | solution.py:284
  25.8 3.7 %collective-permute-start.7 = (f32[2,256]{1,0:T(2,128)S(1)}, f32[2,256]{1,0:T(2,128)S(1)}, u32[]{:S(2)}, u32[]{:S(2)}) collective-permute-start(f32[2,256]{1,0:T(2,128)S(1)} %get-tuple-element.34), channel_id=1, source_target_pairs={{0,16},{1,17},{2,18},{3,19},{4,20},{5,21},{6,22},{7,23},{8,24},{9,... | collective-permute-start | bytes 6152 | tf_op jit(solution)/shard_map/ppermute | solution.py:284
  29.5 1.1 %collective-permute-start.8 = (f32[1,256]{1,0:T(1,128)S(1)}, f32[1,256]{1,0:T(1,128)S(1)}, u32[]{:S(2)}, u32[]{:S(2)}) collective-permute-start(f32[1,256]{1,0:T(1,128)S(1)} %slice.9), channel_id=1, source_target_pairs={{0,8},{1,9},{2,10},{3,11},{4,12},{5,13},{6,14},{7,15},{8,0},{9,1},... | collective-permute-start | bytes 3080 | tf_op jit(solution)/shard_map/ppermute | solution.py:284

commit v7 on v6

--- a/solution.py
+++ b/solution.py
@@ -29,8 +29,8 @@
     bins = bins_ref.shape[0]
     load_bins = pltpu.make_async_copy(bins_hbm, bins_ref, sems.at[0])
     load_snaps = pltpu.make_async_copy(snap_hbm, snap_ref, sems.at[1])
+    load_snaps.start()
     load_bins.start()
-    load_snaps.start()
     me = lax.axis_index("tm")
     cols = 2 * bins
     group = cols // owners

time: 31.3 us -> 31.4 us (level)
  no operation moved by 1% of the time
where the time goes in v7:
time: 31.4 us; the launch traced here: 31.2 us
  Pallas kernels  17.4 us (55%)
  starting transfers between devices  11 us (35%)
  waiting for transfers between devices  2.15 us (7%)
  other arithmetic  0.61 us (2%)
    ppermute x9, starting transfers between devices, swap(): return lax.ppermute(x, ('tm', 'rep'), pairs)  11 us
    pallas_call x2, Pallas kernels, prepare(): pl.pallas_call(functools.partial(prepare_kernel, first, elems), out_shape...  8.4 us
    pallas_call x1, Pallas kernels, shards(): pl.pallas_call(functools.partial(first_kernel, snaps, bits, len(highs)),...  2.49 us
    ppermute x9, waiting for transfers between devices, swap(): return lax.ppermute(x, ('tm', 'rep'), pairs)  2.15 us
    pallas_call x1, Pallas kernels, shards(): pl.pallas_call(functools.partial(dft_kernel, tm), out_shape=(pltpu.VMEM(s...  2.1 us
    pallas_call x1, Pallas kernels, shards(): pl.pallas_call(functools.partial(second_kernel, elem_count, bins, snaps,...  1.81 us
    pallas_call x1, Pallas kernels, shards(): pl.pallas_call(functools.partial(third_kernel, len(inverses)), out_shape=...  1.55 us
    pallas_call x1, Pallas kernels, finish(): pl.pallas_call(functools.partial(finish_kernel, elems), out_shape=results...  0.77 us
  transfers between devices with their start and end apart: 9, of which 4 were waited for; matrix products, arithmetic and copies ran while one was open for 0% of the time, Pallas kernels for 42%

profile of v7, /device:TPU:0, one launch (start us, length us, event | category | flops | bytes accessed | tf_op | source)
XLA Modules:
  0.0 31.2 jit_solution(2971241334633645781)
XLA Ops:
  0.0 2.1 %dft.1 = (f32[2,32,128]{2,1,0:T(8,128)S(1)}, f32[2,32,128]{2,1,0:T(8,128)S(1)}) custom-call(s32[32]{0:T(128)} %bins_hbm.1, f32[8,32,1024]{2,1,0:T(8,128)} %snap_hbm.1), custom_call_target="tpu_custom_call" | custom-call | tf_op jit(solution)/shard_map/dft/pallas_call | solution.py:301
  2.1 5.0 %collective-permute-start.2 = (f32[2,32,128]{2,1,0:T(8,128)S(1)}, f32[2,32,128]{2,1,0:T(8,128)S(1)}, u32[]{:S(2)}, u32[]{:S(2)}) collective-permute-start(f32[2,32,128]{2,1,0:T(8,128)S(1)} %get-tuple-element.21), channel_id=1, source_target_pairs={{0,20},{1,21},{2,22},{3,23},{4,16},{5,17},{6,18},{7,19},{8,28},{9,... | collective-permute-start | bytes 98312 | tf_op jit(solution)/shard_map/ppermute | solution.py:284
  7.1 0.5 %collective-permute-start = (f32[2,32,128]{2,1,0:T(8,128)S(1)}, f32[2,32,128]{2,1,0:T(8,128)S(1)}, u32[]{:S(2)}, u32[]{:S(2)}) collective-permute-start(f32[2,32,128]{2,1,0:T(8,128)S(1)} %get-tuple-element.21), channel_id=1, source_target_pairs={{0,16},{1,17},{2,18},{3,19},{4,20},{5,21},{6,22},{7,23},{8,24},{9,... | collective-permute-start | bytes 98312 | tf_op jit(solution)/shard_map/ppermute | solution.py:284
  7.7 0.1 collective-permute-start.1
  7.8 4.6 %prepare.2 = (bf16[2,4,1024,256]{3,2,1,0:T(8,128)(2,1)S(1)}, bf16[2,4,1024,256]{3,2,1,0:T(8,128)(2,1)S(1)}, f32[4,1024,128]{2,1,0:T(8,128)S(1)}, f32[2,1,1024,256]{3,2,1,0:T(8,128)S(1)}) custom-call(f32[2,32,128]{2,1,0:T(8,128)S(1)} %get-tuple-element.20.after_ref.refs_0_, f32[2,8,1024,256]{3,2,1,0:T(8,128)} %rep_hbm.3), custom_call_target="tpu_custom_call" | custom-call | flops 20000000000 | tf_op jit(solution)/shard_map/prepare/pallas_call | solution.py:335
  12.4 0.0 collective-permute-done.2.refs_3_
  12.4 0.0 collective-permute-done.refs_1_
  12.4 0.0 collective-permute-done.1.refs_2_
  12.5 0.1 collective-permute-start.3
  12.6 0.8 %finish.1 = (bf16[2,1,1024,256]{3,2,1,0:T(8,128)(2,1)S(1)}, bf16[2,1,1024,256]{3,2,1,0:T(8,128)(2,1)S(1)}, f32[1,1024,128]{2,1,0:T(8,128)S(1)}) custom-call(f32[4,32,128]{2,1,0:T(8,128)S(1)} %collect.1.after_ref, f32[2,1,1024,256]{3,2,1,0:T(8,128)S(1)} %get-tuple-element.24.rep_ref), custom_call_target="tpu_custom_call" | custom-call | flops 20000000000 | tf_op jit(solution)/shard_map/finish/pallas_call | solution.py:352
  13.3 0.5 %collective-permute-done.3.refs_4_ = f32[4,32,128]{2,1,0:T(8,128)S(1)} collective-permute-done((f32[4,32,128]{2,1,0:T(8,128)S(1)}, f32[4,32,128]{2,1,0:T(8,128)S(1)}, u32[]{:S(2)}, u32[]{:S(2)}) %collective-permute-start.3) | collective-permute-done | bytes 65568 | tf_op jit(solution)/shard_map/ppermute | solution.py:284
  13.8 0.2 pack.1.after_ref
  14.1 1.9 %collective-permute-start.6 = (f32[2,32,512]{2,1,0:T(8,128)S(1)}, f32[2,32,512]{2,1,0:T(8,128)S(1)}, u32[]{:S(2)}, u32[]{:S(2)}) collective-permute-start(f32[2,32,512]{2,1,0:T(8,128)S(1)} %pack.1.after_ref), channel_id=1, source_target_pairs={{0,2},{1,3},{2,0},{3,1},{4,6},{5,7},{6,4},{7,5},{8,10},{9,11},{10,... | collective-permute-start | bytes 393224 | tf_op jit(solution)/shard_map/ppermute | solution.py:284
  15.9 1.5 %collective-permute-start.5 = (f32[2,32,512]{2,1,0:T(8,128)S(1)}, f32[2,32,512]{2,1,0:T(8,128)S(1)}, u32[]{:S(2)}, u32[]{:S(2)}) collective-permute-start(f32[2,32,512]{2,1,0:T(8,128)S(1)} %pack.1.after_ref), channel_id=1, source_target_pairs={{0,1},{1,0},{2,3},{3,2},{4,5},{5,4},{6,7},{7,6},{8,9},{9,8},{10,11... | collective-permute-start | bytes 393224 | tf_op jit(solution)/shard_map/ppermute | solution.py:284
  17.4 0.2 collective-permute-start.4
  17.6 3.8 %prepare.3 = (bf16[2,3,1024,256]{3,2,1,0:T(8,128)(2,1)S(1)}, bf16[2,3,1024,256]{3,2,1,0:T(8,128)(2,1)S(1)}, f32[3,1024,128]{2,1,0:T(8,128)S(1)}) custom-call(f32[2,32,512]{2,1,0:T(8,128)S(1)} %pack.1.after_ref, f32[2,8,1024,256]{3,2,1,0:T(8,128)} %rep_hbm.3), custom_call_target="tpu_custom_call" | custom-call | flops 20000000000 | tf_op jit(solution)/shard_map/prepare/pallas_call | solution.py:335
  21.4 0.0 collective-permute-done.6
  21.4 2.5 %first.1.proj_ref = f32[8,1024,128]{2,1,0:T(8,128)S(1)} custom-call(f32[4,32,512]{2,1,0:T(8,128)S(1)} %pad_maximum_fusion.1.spec_ref.own_ref, bf16[2,4,1024,256]{3,2,1,0:T(8,128)(2,1)S(1)} %get-tuple-element.23.refs_0_, bf16[2,1,1024,256]{3,2,1,0:T(8,128)(2,1)S(1)} %get-tuple-element.25.refs_1_, bf16[2,3,1024,256]{3,2,1,0:T(8,128)(2,1)S(1)} %get-tuple-element.26.refs_2_, ...), custom_call_target="tpu_custom_call" | custom-call | flops 20000000000 | tf_op jit(solution)/shard_map/first/pallas_call | solution.py:401
  23.9 0.1 collective-permute-done.5
  24.0 0.0 collective-permute-done.4
  24.0 1.8 %second.1 = (f32[2,256]{1,0:T(2,128)S(1)}, bf16[8,256,128]{2,1,0:T(8,128)(2,1)S(1)}, f32[8,1,128]{2,1,0:T(1,128)S(1)}) custom-call(f32[4,32,512]{2,1,0:T(8,128)S(1)} %pad_maximum_fusion.spec_ref, f32[4,32,512]{2,1,0:T(8,128)S(1)} %pad_maximum_fusion.1.spec_ref.own_ref, f32[8,1024,128]{2,1,0:T(8,128)S(1)} %first.1.proj_ref, ...), custom_call_target="tpu_custom_call" | custom-call | tf_op jit(solution)/shard_map/second/pallas_call | solution.py:414
  25.8 1.7 %collective-permute-start.7 = (f32[2,256]{1,0:T(2,128)S(1)}, f32[2,256]{1,0:T(2,128)S(1)}, u32[]{:S(2)}, u32[]{:S(2)}) collective-permute-start(f32[2,256]{1,0:T(2,128)S(1)} %get-tuple-element.34), channel_id=1, source_target_pairs={{0,16},{1,17},{2,18},{3,19},{4,20},{5,21},{6,22},{7,23},{8,24},{9,... | collective-permute-start | bytes 6152 | tf_op jit(solution)/shard_map/ppermute | solution.py:284
  27.5 1.6 %third.1 = f32[2,256]{1,0:T(2,128)S(1)} custom-call(bf16[8,256,128]{2,1,0:T(8,128)(2,1)S(1)} %get-tuple-element.32.right_ref, f32[8,1,128]{2,1,0:T(1,128)S(1)} %get-tuple-element.33.factor_ref, f32[8,1024,128]{2,1,0:T(8,128)S(1)} %first.1.proj_ref, bf16[2,4,1024,256]{3,2,1,0:T(8,128)(2,1)S(1)} %get-tuple-element.23.refs_0_, ...), custom_call_target="tpu_custom_call" | custom-call | flops 20000000000 | tf_op jit(solution)/shard_map/third/pallas_call | solution.py:427
  29.1 0.4 %collective-permute-done.7 = f32[2,256]{1,0:T(2,128)S(1)} collective-permute-done((f32[2,256]{1,0:T(2,128)S(1)}, f32[2,256]{1,0:T(2,128)S(1)}, u32[]{:S(2)}, u32[]{:S(2)}) %collective-permute-start.7) | collective-permute-done | bytes 2080 | tf_op jit(solution)/shard_map/ppermute | solution.py:284
  29.5 0.0 collective-permute-start.8
  29.5 1.1 %collective-permute-done.8 = f32[1,256]{1,0:T(1,128)S(1)} collective-permute-done((f32[1,256]{1,0:T(1,128)S(1)}, f32[1,256]{1,0:T(1,128)S(1)}, u32[]{:S(2)}, u32[]{:S(2)}) %collective-permute-start.8) | collective-permute-done | bytes 1056 | tf_op jit(solution)/shard_map/ppermute | solution.py:284
  30.6 0.6 %slice_add_fusion = f32[1,256]{1,0:T(1,128)} fusion(f32[1,256]{1,0:T(1,128)S(1)} %collective-permute-done.8, f32[2,256]{1,0:T(2,128)S(1)} %add.6), kind=kLoop, calls=%fused_computation.2 | loop fusion | flops 256 | bytes 3072 | tf_op jit(solution)/shard_map/add | solution.py:439
  (5 shorter events, 0.1 us)
Async XLA Ops:
  2.1 10.3 %collective-permute-start.2 = (f32[2,32,128]{2,1,0:T(8,128)S(1)}, f32[2,32,128]{2,1,0:T(8,128)S(1)}, u32[]{:S(2)}, u32[]{:S(2)}) collective-permute-start(f32[2,32,128]{2,1,0:T(8,128)S(1)} %get-tuple-element.21), channel_id=1, source_target_pairs={{0,20},{1,21},{2,22},{3,23},{4,16},{5,17},{6,18},{7,19},{8,28},{9,... | collective-permute-start | bytes 98312 | tf_op jit(solution)/shard_map/ppermute | solution.py:284
  7.1 5.3 %collective-permute-start = (f32[2,32,128]{2,1,0:T(8,128)S(1)}, f32[2,32,128]{2,1,0:T(8,128)S(1)}, u32[]{:S(2)}, u32[]{:S(2)}) collective-permute-start(f32[2,32,128]{2,1,0:T(8,128)S(1)} %get-tuple-element.21), channel_id=1, source_target_pairs={{0,16},{1,17},{2,18},{3,19},{4,20},{5,21},{6,22},{7,23},{8,24},{9,... | collective-permute-start | bytes 98312 | tf_op jit(solution)/shard_map/ppermute | solution.py:284
  7.7 4.8 %collective-permute-start.1 = (f32[2,32,128]{2,1,0:T(8,128)S(1)}, f32[2,32,128]{2,1,0:T(8,128)S(1)}, u32[]{:S(2)}, u32[]{:S(2)}) collective-permute-start(f32[2,32,128]{2,1,0:T(8,128)S(1)} %get-tuple-element.20.after_ref.refs_0_), channel_id=1, source_target_pairs={{0,4},{1,5},{2,6},{3,7},{4,0},{5,1},{6,2},{7,3},{8,12},{9,13},{10,... | collective-permute-start | bytes 98312 | tf_op jit(solution)/shard_map/ppermute | solution.py:284
  12.5 1.3 %collective-permute-start.3 = (f32[4,32,128]{2,1,0:T(8,128)S(1)}, f32[4,32,128]{2,1,0:T(8,128)S(1)}, u32[]{:S(2)}, u32[]{:S(2)}) collective-permute-start(f32[4,32,128]{2,1,0:T(8,128)S(1)} %collect.1.after_ref), channel_id=1, source_target_pairs={{0,8},{1,9},{2,10},{3,11},{4,12},{5,13},{6,14},{7,15},{8,0},{9,1},... | collective-permute-start | bytes 196616 | tf_op jit(solution)/shard_map/ppermute | solution.py:284
  14.1 7.3 %collective-permute-start.6 = (f32[2,32,512]{2,1,0:T(8,128)S(1)}, f32[2,32,512]{2,1,0:T(8,128)S(1)}, u32[]{:S(2)}, u32[]{:S(2)}) collective-permute-start(f32[2,32,512]{2,1,0:T(8,128)S(1)} %pack.1.after_ref), channel_id=1, source_target_pairs={{0,2},{1,3},{2,0},{3,1},{4,6},{5,7},{6,4},{7,5},{8,10},{9,11},{10,... | collective-permute-start | bytes 393224 | tf_op jit(solution)/shard_map/ppermute | solution.py:284
  15.9 8.1 %collective-permute-start.5 = (f32[2,32,512]{2,1,0:T(8,128)S(1)}, f32[2,32,512]{2,1,0:T(8,128)S(1)}, u32[]{:S(2)}, u32[]{:S(2)}) collective-permute-start(f32[2,32,512]{2,1,0:T(8,128)S(1)} %pack.1.after_ref), channel_id=1, source_target_pairs={{0,1},{1,0},{2,3},{3,2},{4,5},{5,4},{6,7},{7,6},{8,9},{9,8},{10,11... | collective-permute-start | bytes 393224 | tf_op jit(solution)/shard_map/ppermute | solution.py:284
  17.4 6.6 %collective-permute-start.4 = (f32[2,32,512]{2,1,0:T(8,128)S(1)}, f32[2,32,512]{2,1,0:T(8,128)S(1)}, u32[]{:S(2)}, u32[]{:S(2)}) collective-permute-start(f32[2,32,512]{2,1,0:T(8,128)S(1)} %pack.1.after_ref), channel_id=1, source_target_pairs={{0,3},{1,2},{2,1},{3,0},{4,7},{5,6},{6,5},{7,4},{8,11},{9,10},{10,... | collective-permute-start | bytes 393224 | tf_op jit(solution)/shard_map/ppermute | solution.py:284
  25.8 3.7 %collective-permute-start.7 = (f32[2,256]{1,0:T(2,128)S(1)}, f32[2,256]{1,0:T(2,128)S(1)}, u32[]{:S(2)}, u32[]{:S(2)}) collective-permute-start(f32[2,256]{1,0:T(2,128)S(1)} %get-tuple-element.34), channel_id=1, source_target_pairs={{0,16},{1,17},{2,18},{3,19},{4,20},{5,21},{6,22},{7,23},{8,24},{9,... | collective-permute-start | bytes 6152 | tf_op jit(solution)/shard_map/ppermute | solution.py:284
  29.5 1.1 %collective-permute-start.8 = (f32[1,256]{1,0:T(1,128)S(1)}, f32[1,256]{1,0:T(1,128)S(1)}, u32[]{:S(2)}, u32[]{:S(2)}) collective-permute-start(f32[1,256]{1,0:T(1,128)S(1)} %slice.9), channel_id=1, source_target_pairs={{0,8},{1,9},{2,10},{3,11},{4,12},{5,13},{6,14},{7,15},{8,0},{9,1},... | collective-permute-start | bytes 3080 | tf_op jit(solution)/shard_map/ppermute | solution.py:284
